TPU v7x, 32 devices: a whole 2x2x4 slice. The times are simulated.
32 devices in a mesh: tile: 8 (over z, y), chan: 4 (over x, core).
Axes of the slice: x: 2, y: 2, z: 4, core: 2. Of those that a mesh axis runs over, the one named last changes fastest.
Arguments:
- features: bfloat16 [128, 32768], P('chan', 'tile'), may hold values from -6 to 6
- conv1_weight: bfloat16 [9, 128, 128], P(None, 'chan'), may hold values from -0.1875 to 0.1875
- down_weight: bfloat16 [4, 128, 128], P(None, 'chan'), may hold values from -0.25 to 0.25
- conv2_weight: bfloat16 [9, 128, 128], P(None, 'chan'), may hold values from -0.1875 to 0.1875
- up_weight: bfloat16 [128, 128], P('chan'), may hold values from -0.5 to 0.5
- out_grad: bfloat16 [128, 32768], P('chan', 'tile'), may hold values from -6 to 6
- adjacency: int32 [8, 8, 2], replicated, may hold values from -1 to 7, as said below
Outputs:
- output: bfloat16 [128, 32768], P('chan', 'tile')
- grad_conv1: float32 [9, 128, 128], P(None, 'chan')
- grad_down: float32 [4, 128, 128], P(None, 'chan')
- grad_conv2: float32 [9, 128, 128], P(None, 'chan')
- grad_up: float32 [128, 128], P('chan')
Inputs may be any that keep to these rules, and one draw needn't show every extreme that they name: adjacency[t, k, 0] is the tile beside side k of tile t (sides north, east, south, west, then corners north-east, south-east, south-west, north-west); it is -1 only at corners, where no single tile meets; adjacency[t, k, 1] is the number of counterclockwise quarter turns, 0 to 3, of that neighbour as seen from tile t.
All inputs are finite; a program needn't handle non-finite values.
Results may differ from a plain program's by a relative error of at most 0.0073.
Values may be sent and summed in bfloat16 or wider, within the bound.
No kernel may reach another device: no remote copies, remote signals or barrier semaphores. Data moves between devices by JAX's collectives and lax.ppermute only.
A program may use at most 128 MiB of HBM per device.

v0:
```python
from functools import partial

import jax
import jax.numpy as jnp
import numpy as np
from jax import lax
from jax.experimental import pallas as pl
from jax.experimental.pallas import tpu as pltpu
from jax.sharding import PartitionSpec as P

SIDE = 64
HALF = 32
CELLS = HALF * HALF
PADDED = 36 * HALF
BLOCK = 8 * SIDE
BF16 = jnp.bfloat16
F32 = jnp.float32
NT = (((1,), (1,)), ((), ()))
ROOT = float(np.sqrt(2.0 / np.pi))
CUBE = 0.044715
side_turns = (0, 1, 2, 3, 0, 2, 2, 0)


def mm(left, right):
    return jnp.dot(left, right, preferred_element_type=F32)


def mm_nt(left, right):
    return lax.dot_general(left, right, NT, preferred_element_type=F32)


def gelu(v):
    return 0.5 * v * (1.0 + jnp.tanh(ROOT * (v + CUBE * (v * v * v))))


def gelu_slope(v):
    square = v * v
    t = jnp.tanh(ROOT * (v + CUBE * (square * v)))
    return 0.5 * (1.0 + t) + (0.5 * ROOT) * v * (1.0 - t * t) * (1.0 + 3.0 * CUBE * square)


def gelu_and_slope(v):
    square = v * v
    t = jnp.tanh(ROOT * (v + CUBE * (square * v)))
    both = 0.5 * (1.0 + t)
    return v * both, both + (0.5 * ROOT) * v * (1.0 - t * t) * (1.0 + 3.0 * CUBE * square)


def iota(shape, dim):
    return lax.broadcasted_iota(jnp.int32, shape, dim)


def one_hot(mask):
    return jnp.where(mask, 1.0, 0.0).astype(BF16)


def flip32(rows):
    anti = one_hot(iota((HALF, HALF), 0) + iota((HALF, HALF), 1) == HALF - 1)
    return mm(anti, rows)


def own_rows(me, own, chans):
    return one_hot(iota((own, chans), 0) + me * own == iota((own, chans), 1))


def side_of(codes_ref, tile, side):
    code = codes_ref[tile, side]
    return jnp.maximum(code, 0) // 4, code & 3, code >= 0


def is_beside(codes_ref, tile, side, partner):
    code = codes_ref[tile, side]
    return (code >= partner * 4) & (code < partner * 4 + 4)


def rows_of(slot, base, own):
    return pl.multiple_of((slot ^ base) * own, own)


def place_conv(packs, base, start, dst_ref):
    own = packs[0].shape[1]
    for slot, pack in enumerate(packs):
        row = rows_of(slot, base, own)
        for a in range(3):
            for b in range(3):
                dst_ref[pl.ds(a * 128 + row, own), b * 128 : (b + 1) * 128] = pack[start + 3 * a + b]


def spread_columns(dst, left, right, center, north, south, west, east, corners):
    rows = 34 * HALF
    middle = jnp.concatenate([north, center, south], axis=0)
    north_east, south_east, south_west, north_west = corners
    left[...] = pltpu.roll(middle, 1, 0)
    right[...] = pltpu.roll(middle, rows - 1, 0)
    left[pl.ds(HALF, HALF, stride=HALF), :] = west
    left[0:1, :] = north_west
    left[33 * HALF : 33 * HALF + 1, :] = south_west
    right[pl.ds(2 * HALF - 1, HALF, stride=HALF), :] = east
    right[HALF - 1 : HALF, :] = north_east
    right[rows - 1 : rows, :] = south_east
    dst[0:rows, 0:128] = left[...].astype(BF16)
    dst[0:rows, 128:256] = middle.astype(BF16)
    dst[0:rows, 256:384] = right[...].astype(BF16)
    dst[rows:PADDED, :] = jnp.zeros((PADDED - rows, 384), BF16)


def fetch(pairs, sems):
    started = [
        pltpu.make_async_copy(source, target, sems.at[index])
        for index, (source, target) in enumerate(pairs)
    ]
    for copy in started:
        copy.start()
    return started


def stacked(ref):
    return jnp.concatenate([ref[:, jb * BLOCK : (jb + 1) * BLOCK] for jb in range(8)], axis=0)


def sort_kernel(
    f_hbm, g_hbm, w1_hbm, wd_hbm, w2_hbm, up_hbm, m_hbm, pack_ref, rims_ref, sorted_ref, pack2_ref, f_ref, g_ref, m_ref, sems
):
    count = f_ref.shape[0]
    started = fetch(
        [
            (f_hbm, f_ref),
            (m_hbm, m_ref),
            (g_hbm, g_ref),
            (w1_hbm, pack_ref.at[32:41]),
            (wd_hbm, pack_ref.at[41:45]),
            (w2_hbm, pack2_ref.at[8:17]),
            (up_hbm, pack2_ref.at[17]),
        ],
        sems,
    )
    lane = iota((count, BLOCK), 1)
    turn, slot = lane // 128, lane % HALF
    wanted = jnp.where(
        turn == 0, 7, jnp.where(turn == 1, slot // 4, jnp.where(turn == 2, 0, (HALF - 1 - slot) // 4))
    )
    spot, cell = iota((BLOCK, 128), 0), iota((BLOCK, 128), 1)
    pooling = one_hot((spot // 128 == cell // HALF) & (spot % HALF == cell % HALF))

    def moved(ref):
        stack = jnp.concatenate([ref[:, jb * BLOCK : (jb + 1) * BLOCK] for jb in range(8)], axis=0)
        both = mm(stack, m_ref[...])
        parts = [both[jb * count : (jb + 1) * count] for jb in range(8)]
        rims = jnp.zeros((count, BLOCK), F32)
        for jb in range(8):
            rims = rims + jnp.where(wanted == jb, parts[jb][:, BLOCK:], 0.0)
        return [[part[:, ph * 128 : (ph + 1) * 128] for ph in range(4)] for part in parts], rims.astype(BF16)

    started[0].wait()
    started[1].wait()
    pieces, rims = moved(f_ref)
    for turn_index in range(4):
        rims_ref[0, turn_index] = rims[:, turn_index * 128 : (turn_index + 1) * 128]
    for jb in range(8):
        for ph in range(4):
            pack_ref[ph * 8 + jb] = pieces[jb][ph].astype(BF16)
    started[2].wait()
    pieces, rims = moved(g_ref)
    rims_ref[0, 4] = mm(rims, pooling).astype(BF16)
    for jb in range(8):
        for ph in range(4):
            sorted_ref[:, ph * CELLS + jb * 128 : ph * CELLS + (jb + 1) * 128] = pieces[jb][ph].astype(BF16)
        pack2_ref[jb] = ((pieces[jb][0] + pieces[jb][1]) + (pieces[jb][2] + pieces[jb][3])).astype(BF16)
    for copy in started[3:]:
        copy.wait()


def hold(refs, spots, core, put):
    for ref, slots in zip(refs, spots):
        for index, (even, odd) in enumerate(slots):
            slot = even if even == odd else jnp.where(core == 0, even, odd)
            put(slot, ref, index)


def pick_kernel(spots, codes_ref, where_ref, *refs):
    *rims, out_ref, held = refs
    tile, base, core = where_ref[0], where_ref[2], where_ref[1] & 1

    def put(slot, ref, index):
        held[slot] = ref[index]

    hold(rims, spots, core, put)
    lane = iota(out_ref.shape[1:], 1) % HALF
    corners = jnp.zeros(lane.shape, F32)
    for side in range(8):
        partner, turn, there = side_of(codes_ref, tile, side)
        picked = jnp.where(there, held[partner ^ base, turn].astype(F32), 0.0)
        if side < 4:
            out_ref[side] = picked.astype(BF16)
        else:
            shift, spot = ((0, 0), (0, HALF - 1), (1, 1), (127, HALF - 2))[side - 4]
            moved = pltpu.roll(picked, shift, 1) if shift else picked
            corners = corners + jnp.where(lane == spot, moved, 0.0)
    out_ref[4] = corners.astype(BF16)
    for other in range(out_ref.shape[0] - 5):
        out_ref[5 + other] = held[other ^ base, 4]


def stage_kernel(pack_ref, rims_ref, far_ref, near_ref, pair_ref):
    near_ref[...] = pack_ref[...]
    pair_ref[0:1] = rims_ref[...]
    pair_ref[1:2] = far_ref[...]


def fine_center_kernel(nc, where_ref, *refs):
    packs, refs = refs[:nc], refs[nc:]
    x3_ref, z1_ref, w1t, wdt, w1s, wds, f_all = refs
    base = where_ref[3]
    own = packs[0].shape[1]
    for slot, pack in enumerate(packs):
        row = rows_of(slot, base, own)
        for block in range(32):
            f_all[pl.ds(row, own), block * 128 : (block + 1) * 128] = pack[block]
        for a in range(3):
            for b in range(3):
                w1s[pl.ds(a * 128 + row, own), b * 128 : (b + 1) * 128] = pack[32 + 3 * a + b]
        for ph in range(4):
            wds[pl.ds(row, own), ph * 128 : (ph + 1) * 128] = pack[41 + ph]
    for a in range(3):
        w1t[a * 384 : (a + 1) * 384, :] = jnp.transpose(w1s[a * 128 : (a + 1) * 128, :])
    wdt[...] = jnp.transpose(wds[...])
    column = iota((CELLS, 128), 0) % HALF
    for ph in range(4):
        center = jnp.transpose(f_all[:, ph * CELLS : (ph + 1) * CELLS]).astype(F32)
        left = jnp.where(column == 0, 0.0, pltpu.roll(center, 1, 0))
        right = jnp.where(column == HALF - 1, 0.0, pltpu.roll(center, CELLS - 1, 0))
        x3_ref[ph, 0:HALF, :] = jnp.zeros((HALF, 384), BF16)
        x3_ref[ph, HALF : HALF + CELLS, 0:128] = left.astype(BF16)
        x3_ref[ph, HALF : HALF + CELLS, 128:256] = center.astype(BF16)
        x3_ref[ph, HALF : HALF + CELLS, 256:384] = right.astype(BF16)
        x3_ref[ph, HALF + CELLS : PADDED, :] = jnp.zeros((PADDED - HALF - CELLS, 384), BF16)
        for start in range(0, CELLS, 256):
            window = jnp.concatenate(
                [x3_ref[ph, start + a * HALF : start + a * HALF + 256, :] for a in range(3)], axis=1
            )
            z1_ref[ph, start : start + 256, :] = mm(window, w1t[...])


def ring_pieces(ring, ph):
    a, b = ph // 2, ph % 2
    near, far = ph * HALF, ((1 - a) * 2 + (1 - b)) * HALF
    east, west = ((1 - b) * 2 + a) * HALF, (b * 2 + (1 - a)) * HALF
    return (
        ring[0, near : near + HALF],
        ring[1, east : east + HALF],
        ring[2, far : far + HALF],
        ring[3, west : west + HALF],
        (
            ring[4, near : near + 1],
            ring[4, far + HALF - 1 : far + HALF],
            ring[4, far + 1 : far + 2],
            ring[4, near + HALF - 2 : near + HALF - 1],
        ),
    )


def windows_of(row, first, final):
    place = iota((HALF, 128), 0)
    return jnp.concatenate(
        [
            jnp.where(place == 0, first, pltpu.roll(row, 1, 0)),
            row,
            jnp.where(place == HALF - 1, final, pltpu.roll(row, HALF - 1, 0)),
        ],
        axis=1,
    ).astype(BF16)


def fine_ring_kernel(nc, where_ref, z1_in, w1t, wdt, *refs):
    rings, refs = refs[:nc], refs[nc:]
    act_ref, slope2_ref, act2_ref, rims_ref, half_ref, ring, ring_all, z1, wide = refs
    base = where_ref[3]
    own = rings[0].shape[1]
    for slot in range(nc):
        row = rows_of(slot, base, own)
        for side in range(5):
            ring_all[side, pl.ds(row, own), :] = rings[slot][side]
    row, col = iota((128, 128), 0), iota((128, 128), 1)
    same = one_hot(row == col)
    turned = one_hot((row // HALF == col // HALF) & (row % HALF + col % HALF == HALF - 1))
    for side in range(5):
        ring[side] = mm_nt(turned if side in (2, 3) else same, ring_all[side])
    z1[...] = z1_in[...]
    pieces = [ring_pieces(ring, ph) for ph in range(4)]

    def owed(rows, weights):
        return mm(jnp.concatenate(rows, axis=0), weights)

    def column(tap):
        return jnp.concatenate(
            [w1t[a * 384 + tap * 128 : a * 384 + (tap + 1) * 128, :] for a in range(3)], axis=0
        )

    north = owed([windows_of(p[0], p[4][3], p[4][0]) for p in pieces], w1t[0:384, :])
    south = owed([windows_of(p[2], p[4][2], p[4][1]) for p in pieces], w1t[768:1152, :])
    west = owed([windows_of(p[3], 0.0, 0.0) for p in pieces], column(0))
    east = owed([windows_of(p[1], 0.0, 0.0) for p in pieces], column(2))
    first = pl.ds(0, HALF, stride=HALF)
    last = pl.ds(HALF - 1, HALF, stride=HALF)
    for ph in range(4):
        rows = slice(ph * HALF, (ph + 1) * HALF)
        z1[ph, 0:HALF, :] += north[rows]
        z1[ph, CELLS - HALF : CELLS, :] += south[rows]
        z1[ph, first, :] = z1[ph, first, :] + west[rows]
        z1[ph, last, :] = z1[ph, last, :] + east[rows]

    def chunk(index, carry):
        start = index * 256
        acts = []
        for ph in range(4):
            act = gelu(z1[ph, pl.ds(start, 256), :]).astype(BF16)
            act_ref[ph, pl.ds(start, 256), :] = act
            acts.append(act)
        z2 = mm(jnp.concatenate(acts, axis=1), wdt[...])
        value, slope = gelu_and_slope(z2)
        slope2_ref[pl.ds(start, 256), :] = slope
        act2 = value.astype(BF16)
        act2_ref[pl.ds(start, 256), :] = act2
        wide[pl.ds(start, 256), :] = act2.astype(F32)
        return carry

    lax.fori_loop(0, 4, chunk, 0)
    for deep in range(2):
        start = CELLS - (deep + 1) * HALF
        rims_ref[0, deep * 128 : deep * 128 + 32, :] = act2_ref[start : start + HALF, :]
        rims_ref[0, deep * 128 + 32 : deep * 128 + 64, :] = wide[
            pl.ds(deep, HALF, stride=HALF), :
        ].astype(BF16)
        rims_ref[0, deep * 128 + 64 : deep * 128 + 96, :] = flip32(
            act2_ref[deep * HALF : (deep + 1) * HALF, :]
        ).astype(BF16)
        rims_ref[0, deep * 128 + 96 : deep * 128 + 128, :] = flip32(
            wide[pl.ds(HALF - 1 - deep, HALF, stride=HALF), :].astype(BF16)
        ).astype(BF16)
    half_ref[0] = rims_ref[0, pl.ds(pl.multiple_of((where_ref[1] & 1) * 128, 128), 128), :]


def own_fine_kernel(w1_ref, ring, x3_in, act_ref, slope_ref, x3_ref):
    own = w1_ref.shape[1]
    row, col = iota((CELLS, HALF), 0), iota((CELLS, HALF), 1)
    at_first, at_last = one_hot(row == col * HALF), one_hot(row == col * HALF + HALF - 1)
    inner = slice(HALF, HALF + CELLS)
    stack = jnp.concatenate(
        [
            jnp.concatenate([w1_ref[3 * a + b] for b in range(3)], axis=1)
            for a in range(3)
        ],
        axis=0,
    )
    for ph in range(4):
        north, east, south, west, corners = ring_pieces(ring, ph)
        x3_ref[ph, inner, 128:256] = x3_in[ph, inner, 128:256]
        x3_ref[ph, 2 * HALF + CELLS : PADDED, :] = jnp.zeros((PADDED - 2 * HALF - CELLS, 384), BF16)
        x3_ref[ph, 0:HALF, :] = windows_of(north, corners[3], corners[0])
        x3_ref[ph, HALF + CELLS : 2 * HALF + CELLS, :] = windows_of(south, corners[2], corners[1])
        x3_ref[ph, inner, 0:128] = x3_in[ph, inner, 0:128] + mm(at_first, west.astype(BF16)).astype(BF16)
        x3_ref[ph, inner, 256:384] = x3_in[ph, inner, 256:384] + mm(at_last, east.astype(BF16)).astype(
            BF16
        )
        terms = mm_nt(stack, x3_ref[ph])
        total = terms[0:own, 0:CELLS]
        for a in range(1, 3):
            moved = pltpu.roll(terms[a * own : (a + 1) * own], PADDED - a * HALF, 1)
            total = total + moved[:, 0:CELLS]
        value, slope = gelu_and_slope(total)
        act_ref[:, ph * CELLS : (ph + 1) * CELLS] = value.astype(BF16)
        slope_ref[:, ph * CELLS : (ph + 1) * CELLS] = slope


def turned_tap(turn, a, b):
    return ((a, b), (b, 2 - a), (2 - a, 2 - b), (2 - b, a))[turn]


CORNER_ENDS = {4: 0, 5: HALF - 1, 6: 0, 7: HALF - 1}
LOW_LEFT = (4, 5, 6, 7)
LOW_RIGHT = (7, 4, 5, 6)


def is_owing(codes_ref, other, side, tile):
    owing = is_beside(codes_ref, other, side, tile)
    if side in (0, 2):
        owing = owing | is_beside(codes_ref, other, LOW_LEFT[side], tile)
        owing = owing | is_beside(codes_ref, other, LOW_RIGHT[side], tile)
    return owing


def strip_of(side, other, codes_ref, base, rims_all):
    turn = (side + 2) % 4

    def rim(partner, slot):
        return rims_all[partner ^ base, pl.ds(pl.multiple_of(slot * HALF, HALF), HALF), :]

    partner, slot, _ = side_of(codes_ref, other, side)
    left_partner, left_slot, _ = side_of(codes_ref, other, (side + 1) % 4)
    right_partner, right_slot, _ = side_of(codes_ref, other, (side + 3) % 4)
    ends = []
    for corner in (LOW_LEFT[side], LOW_RIGHT[side]):
        corner_partner, corner_slot, there = side_of(codes_ref, other, corner)
        spot = CORNER_ENDS[corner]
        row = rim(corner_partner, corner_slot).astype(F32)[spot : spot + 1]
        ends.append(jnp.where(there, row, 0.0))
    left, right = rim(left_partner, left_slot).astype(F32), rim(right_partner, right_slot).astype(F32)
    last = HALF - 1
    here = rims_all[other ^ base, turn * HALF : (turn + 1) * HALF, :].astype(F32)
    above = rims_all[other ^ base, 128 + turn * HALF : 128 + (turn + 1) * HALF, :].astype(F32)
    below = flip32(rim(partner, slot))
    place = iota((HALF, 128), 0)
    by_tap = {}
    for a, (row, first, final) in enumerate(
        (
            (above, left[1:2], right[last - 1 : last]),
            (here, left[0:1], right[last : last + 1]),
            (below, ends[0], ends[1]),
        )
    ):
        by_tap[turned_tap(turn, a, 0)] = jnp.where(place == 0, first, pltpu.roll(row, 1, 0))
        by_tap[turned_tap(turn, a, 1)] = row
        by_tap[turned_tap(turn, a, 2)] = jnp.where(place == last, final, pltpu.roll(row, last, 0))
    return jnp.concatenate([by_tap[a, b] for a in range(3) for b in range(3)], axis=1).astype(BF16)


def back_from(others, codes_ref, tile, base, rims_all, prims, w2s, w2t, ups, back):
    last = HALF - 1
    place = iota((HALF, 128), 0)
    z3 = mm(
        jnp.concatenate([strip_of(side, others[side], codes_ref, base, rims_all) for side in range(4)], axis=0),
        w2t[...],
    )
    pooled = []
    for side in range(4):
        turn = (side + 2) % 4
        select = one_hot(iota((HALF, 128), 0) + turn * HALF == iota((HALF, 128), 1))
        cells = prims[:, pl.ds(pl.multiple_of(others[side] * 128, 128), 128)]
        pooled.append(mm_nt(select, cells))
    g3 = gelu_slope(z3) * mm(jnp.concatenate(pooled, axis=0).astype(BF16), ups[...])
    row, col = iota((128, 128), 0), iota((128, 128), 1)
    turned = one_hot((row // HALF == col // HALF) & (row % HALF + col % HALF == HALF - 1))
    g3 = mm(turned, g3.astype(BF16)).astype(BF16)
    for side in range(4):
        other = others[side]
        owed = []
        for b in range(3):
            r, c = turned_tap((side + 2) % 4, 2, b)
            owed.append(
                mm(
                    g3[side * HALF : (side + 1) * HALF],
                    w2s[r * 128 : (r + 1) * 128, c * 128 : (c + 1) * 128],
                )
            )
        total = (
            jnp.where(place == 0, 0.0, pltpu.roll(owed[0], 1, 0))
            + owed[1]
            + jnp.where(place == last, 0.0, pltpu.roll(owed[2], last, 0))
        )
        _, slot, _ = side_of(codes_ref, other, side)
        counts = is_beside(codes_ref, other, side, tile) & (others[side + 4] == 1)
        back[pl.ds(pl.multiple_of(slot * HALF, HALF), HALF), :] += jnp.where(counts, total, 0.0)
        if side in (0, 2):
            for corner, line in (
                (LOW_LEFT[side], owed[0][last : last + 1]),
                (LOW_RIGHT[side], owed[2][0:1]),
            ):
                _, corner_slot, _ = side_of(codes_ref, other, corner)
                counts = is_beside(codes_ref, other, corner, tile) & (others[side + 4] == 1)

                @pl.when(counts)
                def _():
                    back[pl.ds(pl.multiple_of(corner_slot * HALF, HALF), HALF), :] += jnp.where(
                        place == CORNER_ENDS[corner], line, 0.0
                    )


def own_taps(grad_ref, start, grads, own):
    for a in range(3):
        for b in range(3):
            row = (start + 3 * a + b) * own
            grad_ref[row : row + own, :] = grads[
                a * own : (a + 1) * own, b * 128 : (b + 1) * 128
            ].astype(BF16)


def shifted_stack(values):
    wide = jnp.concatenate([values, jnp.zeros((values.shape[0], PADDED - CELLS), F32)], axis=1)
    return jnp.concatenate(
        [(pltpu.roll(wide, a * HALF, 1) if a else wide).astype(BF16) for a in range(3)], axis=0
    )


def level_kernel(
    nc,
    spots,
    codes_ref,
    where_ref,
    act2_ref,
    slope2_ref,
    act_ref,
    wdt_ref,
    own_ref,
    slope1_ref,
    og_ref,
    x3_ref,
    m_ref,
    *refs,
):
    packs, mores, refs = refs[:nc], refs[nc : 2 * nc], refs[2 * nc :]
    *rims, out_ref, grad_ref, w2s, w2t, ups, pooled_all, prims, rims_all, left, right, g3pad, sums, a3, coarse, field, back = refs
    tile, me, tile_base, base = where_ref[0], where_ref[1], where_ref[2], where_ref[3]
    own = packs[0].shape[1]
    place_conv(packs, base, 8, w2s)
    for slot in range(nc):
        row = rows_of(slot, base, own)
        ups[pl.ds(row, own), :] = packs[slot][17]
        for jb in range(8):
            pooled_all[pl.ds(row, own), jb * 128 : (jb + 1) * 128] = packs[slot][jb]
        for other in range(mores[slot].shape[0] - 5):
            prims[pl.ds(row, own), other * 128 : (other + 1) * 128] = mores[slot][5 + other]

    def put(slot, ref, index):
        rims_all[slot] = ref[index]

    if len(rims) == 9:
        core = me & 1
        rims_all[1, pl.ds(pl.multiple_of(core * 128, 128), 128), :] = rims[4][0]
        rims_all[1, pl.ds(pl.multiple_of(128 - core * 128, 128), 128), :] = rims[8][0]
        rims = rims[:4] + rims[5:8]
    hold(rims, spots, me & 1, put)
    got = []
    for side in range(8):
        partner, turn, there = side_of(codes_ref, tile, side)
        piece = rims_all[
            partner ^ tile_base, pl.ds(pl.multiple_of(turn * HALF, HALF), HALF), :
        ].astype(F32)
        got.append(jnp.where(there, piece, 0.0))
    spread_columns(
        a3,
        left,
        right,
        act2_ref[...].astype(F32),
        got[0],
        flip32(got[2].astype(BF16)),
        flip32(got[3].astype(BF16)),
        got[1],
        (got[4][0:1], got[5][HALF - 1 : HALF], got[6][0:1], got[7][HALF - 1 : HALF]),
    )
    for a in range(3):
        w2t[a * 384 : (a + 1) * 384, :] = jnp.transpose(w2s[a * 128 : (a + 1) * 128, :])
    pooled = jnp.transpose(pooled_all[...])
    g3pad[0 : 2 * HALF, :] = jnp.zeros((2 * HALF, 128), BF16)
    g3pad[CELLS + 2 * HALF : CELLS + 4 * HALF, :] = jnp.zeros((2 * HALF, 128), BF16)
    for index in range(4):
        start = index * 256
        z3 = mm(
            jnp.concatenate(
                [a3[start + a * HALF : start + a * HALF + 256, :] for a in range(3)], axis=1
            ),
            w2t[...],
        )
        value, slope = gelu_and_slope(z3)
        coarse[start : start + 256, :] = value.astype(BF16)
        back_up = mm(pooled[start : start + 256, :], ups[...])
        g3pad[2 * HALF + start : 2 * HALF + start + 256, :] = (slope * back_up).astype(BF16)
    step = 34 * HALF // 4
    for index in range(4):
        start = index * step
        lhs = jnp.concatenate(
            [g3pad[start + (2 - a) * HALF : start + (2 - a) * HALF + step, :] for a in range(3)], axis=1
        )
        sums[start : start + step, :] = mm(lhs, w2s[...])
    rows = 34 * HALF
    column = iota((rows, 128), 0) % HALF
    middle = (
        sums[:, 128:256]
        + jnp.where(column == HALF - 1, 0.0, pltpu.roll(sums[:, 0:128], rows - 1, 0))
        + jnp.where(column == 0, 0.0, pltpu.roll(sums[:, 256:384], 1, 0))
    )
    field[...] = middle[HALF : HALF + CELLS, :]

    back[...] = jnp.zeros_like(back)
    tiles = codes_ref.shape[0]

    def following(before):
        found = []
        for side in range(4):
            spot = jnp.int32(tiles)
            for other in reversed(range(tiles)):
                take = is_owing(codes_ref, other, side, tile) & (other > before[side])
                spot = jnp.where(take, other, spot)
            found.append(spot)
        return tuple(found)

    def left_over(found):
        return (
            (found[0] < tiles) | (found[1] < tiles) | (found[2] < tiles) | (found[3] < tiles)
        )

    def visit(found):
        others = [jnp.minimum(spot, tiles - 1) for spot in found]
        others = others + [jnp.where(spot < tiles, 1, 0) for spot in found]
        back_from(others, codes_ref, tile, tile_base, rims_all, prims, w2s, w2t, ups, back)
        return following(found)

    lax.while_loop(left_over, visit, following((jnp.int32(-1),) * 4))
    anti = jnp.where(iota((HALF, HALF), 0) + iota((HALF, HALF), 1) == HALF - 1, 1.0, 0.0)

    def flip(values):
        return lax.dot_general(
            anti,
            values,
            (((1,), (0,)), ((), ())),
            preferred_element_type=F32,
            precision=lax.Precision.HIGHEST,
        )

    field[CELLS - HALF : CELLS, :] += back[0:32, :]
    field[0:HALF, :] += flip(back[64:96, :])
    first = pl.ds(0, HALF, stride=HALF)
    last = pl.ds(HALF - 1, HALF, stride=HALF)
    field[first, :] = field[first, :] + back[32:64, :]
    field[last, :] = field[last, :] + flip(back[96:128, :])

    g2 = (slope2_ref[...] * field[...]).astype(BF16)
    pick = own_rows(me, own, 128)
    g2_turned = mm_nt(one_hot(iota((128, 128), 0) == iota((128, 128), 1)), g2).astype(BF16)
    g2_own = mm_nt(pick, g2).astype(BF16)
    grads = jnp.zeros((3 * own, 384), F32)
    for ph in range(4):
        grad_ref[(9 + ph) * own : (10 + ph) * own, :] = mm(g2_own, act_ref[ph]).astype(BF16)
        turned = wdt_ref[pl.ds(pl.multiple_of(ph * 128 + me * own, own), own), :]
        cells = slice(ph * CELLS, (ph + 1) * CELLS)
        g1 = slope1_ref[:, cells] * (og_ref[:, cells].astype(F32) + mm(turned, g2_turned))
        grads = grads + mm(shifted_stack(g1), x3_ref[ph])
    own_taps(grad_ref, 0, grads, own)
    g3 = mm_nt(pick, g3pad[2 * HALF : 2 * HALF + CELLS, :])
    own_taps(grad_ref, 13, mm(shifted_stack(g3), a3[...]), own)
    own_spot = pl.ds(pl.multiple_of(me * own, own), own)
    grad_ref[22 * own : 23 * own, :] = mm(pooled_all[own_spot, :], coarse[...]).astype(BF16)
    if grad_ref.shape[0] > 23 * own:
        grad_ref[23 * own :, :] = jnp.zeros((grad_ref.shape[0] - 23 * own, 128), BF16)

    lifted = mm_nt(ups[own_spot, :], coarse[...])
    total = [
        own_ref[:, ph * CELLS : (ph + 1) * CELLS].astype(F32) + lifted for ph in range(4)
    ]
    stack = jnp.concatenate(
        [
            jnp.concatenate([total[ph][:, jb * 128 : (jb + 1) * 128] for ph in range(4)], axis=1)
            for jb in range(8)
        ],
        axis=0,
    ).astype(BF16)
    natural = mm_nt(stack, m_ref[:, 0:BLOCK]).astype(BF16)
    for jb in range(8):
        out_ref[:, jb * BLOCK : (jb + 1) * BLOCK] = natural[jb * own : (jb + 1) * own]


def sum_kernel(scale, in_ref, out_ref):
    total = in_ref[0].astype(F32)
    for slot in range(1, in_ref.shape[0]):
        total = total + in_ref[slot].astype(F32)
    out_ref[...] = (total * scale).astype(BF16)


def unpack_kernel(flat, one_ref, down_ref, two_ref, up_ref):
    own = up_ref.shape[0]
    for tap in range(9):
        one_ref[tap] = flat[tap * own : (tap + 1) * own, :].astype(F32)
        two_ref[tap] = flat[(13 + tap) * own : (14 + tap) * own, :].astype(F32)
    for ph in range(4):
        down_ref[ph] = flat[(9 + ph) * own : (10 + ph) * own, :].astype(F32)
    up_ref[...] = flat[22 * own : 23 * own, :].astype(F32)


def call(kernel, outs, *args, scratch=(), far=(), room=24, alias={}):
    specs = [
        pl.BlockSpec(
            memory_space=pltpu.SMEM if a.dtype == jnp.int32 else pltpu.HBM if i in far else pltpu.VMEM
        )
        for i, a in enumerate(args)
    ]
    many = isinstance(outs, list)
    vmem = pl.BlockSpec(memory_space=pltpu.VMEM)
    return pl.pallas_call(
        kernel,
        out_shape=outs,
        in_specs=specs,
        out_specs=[vmem] * len(outs) if many else vmem,
        scratch_shapes=list(scratch),
        input_output_aliases=alias,
        compiler_params=pltpu.CompilerParams(vmem_limit_bytes=room * 1024 * 1024),
    )(*args)


def shape(dims, kind=BF16):
    return jax.ShapeDtypeStruct(dims, kind)


def sort_matrix():
    table = np.zeros((BLOCK, 2 * BLOCK), np.float32)

    def lane(a, b, q, k):
        return q * 128 + a * 64 + 2 * k + b

    for a in range(2):
        for b in range(2):
            for q in range(4):
                for k in range(HALF):
                    table[lane(a, b, q, k), (2 * a + b) * 128 + q * HALF + k] = 1
    for x in range(2):
        for y in range(2):
            for j in range(HALF):
                spot = BLOCK + (2 * x + y) * HALF + j
                back = HALF - 1 - j
                table[lane(x, y, 3, j), spot] = 1
                table[lane(y, 1 - x, j % 4, 0), spot + 128] = 1
                table[lane(1 - x, 1 - y, 0, back), spot + 256] = 1
                table[lane(1 - y, x, back % 4, HALF - 1), spot + 384] = 1
    return jnp.asarray(table, BF16)


def paired(values, axis, bit):
    count = lax.axis_size(axis)
    return lax.ppermute(values, axis, [(i, i ^ bit) for i in range(count)])


FIRST, SECOND = (7, 4, 2), (6, 5, 3)


def is_split():
    return lax.axis_size("tile") == 8 and lax.axis_size("chan") % 2 == 0


def spots_of():
    tiles = lax.axis_size("tile")
    if not is_split():
        return [[(slot, slot) for slot in range(tiles)]]
    pairs = list(zip(FIRST, SECOND))
    return [[(0, 0)]] + [[pair] for pair in pairs] + [[pair[::-1]] for pair in pairs]


def copies(block, half=None, beside=()):
    tiles, nc = lax.axis_size("tile"), lax.axis_size("chan")
    if not is_split():
        return [swap(jnp.broadcast_to(block, (tiles,) + block.shape[1:]))], beside
    got = []
    for slots in zip(FIRST, SECOND):
        perm = [
            (tile * nc + chan, (tile ^ slots[chan & 1]) * nc + chan)
            for tile in range(tiles)
            for chan in range(nc)
        ]
        got.append(lax.ppermute(block, ("tile", "chan"), perm))
    got.append(paired(half, "tile", 1))
    got, beside = lax.optimization_barrier((got, beside))
    return [block] + got + [paired(part, "chan", 1) for part in got], beside


def swap(values):
    return lax.all_to_all(values, "tile", split_axis=0, concat_axis=0)


def gathered(values, axis):
    slots = {0: values}
    bit = lax.axis_size(axis) // 2
    while bit:
        slots.update({slot ^ bit: paired(held, axis, bit) for slot, held in list(slots.items())})
        bit //= 2
    return [slots[slot] for slot in range(len(slots))]


def per_device(features, conv1_weight, down_weight, conv2_weight, up_weight, out_grad, adjacency):
    own = features.shape[0]
    tiles, nc = lax.axis_size("tile"), lax.axis_size("chan")
    scale = float((tiles * SIDE * SIDE) ** (-0.5))
    tile, chan = lax.axis_index("tile"), lax.axis_index("chan")
    where = jnp.stack([tile, chan, tile if is_split() else tile * 0, chan]).astype(jnp.int32)
    matrix = sort_matrix()
    half = nc // 2

    pack, rims, sorted_g, pack2 = call(
        sort_kernel,
        [
            shape((45, own, 128)),
            shape((1, 5, own, 128)),
            shape((own, 4 * CELLS)),
            shape((18, own, 128)),
        ],
        features,
        out_grad,
        conv1_weight,
        down_weight,
        conv2_weight,
        up_weight,
        matrix,
        far=range(7),
        room=60,
        scratch=[
            pltpu.VMEM((own, 4 * CELLS), BF16),
            pltpu.VMEM((own, 4 * CELLS), BF16),
            pltpu.VMEM((BLOCK, 2 * BLOCK), BF16),
            pltpu.SemaphoreType.DMA((7,)),
        ],
    )
    pack_far = paired(pack, "chan", half)
    if is_split():
        far, near = paired(rims, "tile", 4), paired(rims, "tile", 2)
        cross = paired(far, "tile", 2)
        pack_near, pair = call(
            stage_kernel, [shape(pack.shape), shape((2,) + rims.shape[1:])], pack, rims, far
        )
        beside = paired(pair, "tile", 1)
        cross, near, pack_near, pack2, adjacency = lax.optimization_barrier(
            (cross, near, pack_near, pack2, adjacency)
        )
        last = [paired(near, "tile", 1), paired(cross, "tile", 1)]
        all_rims = [pair, near, cross, beside] + last
        rim_spots = [[(slot, slot) for slot in group] for group in ((0, 4), (2,), (6,), (1, 5), (3,), (7,))]
    else:
        all_rims, rim_spots = copies(rims)[0], spots_of()
        pack_near = pack
    turns = (adjacency[:, :, 1] + jnp.array(side_turns, jnp.int32)) & 3
    codes = jnp.where(adjacency[:, :, 0] < 0, -1, adjacency[:, :, 0] * 4 + turns)
    ring = call(
        partial(pick_kernel, rim_spots),
        shape((5 + tiles, own, 128)),
        codes,
        where,
        *all_rims,
        scratch=[pltpu.VMEM((tiles + 1, 5, own, 128), BF16)],
    )
    pack_far, ring = lax.optimization_barrier((pack_far, ring))
    ring_far = paired(ring, "chan", half)

    def whole(near, far, held=None):
        return [near if held is None else held, paired(near, "chan", 1), far, paired(far, "chan", 1)]

    packs = whole(pack, pack_far, pack_near)
    x3, z1c, w1t, wdt = call(
        partial(fine_center_kernel, nc),
        [
            shape((4, PADDED, 384)),
            shape((4, CELLS, 128), F32),
            shape((1152, 128)),
            shape((512, 128)),
        ],
        where,
        *packs,
        scratch=[
            pltpu.VMEM((384, 384), BF16),
            pltpu.VMEM((128, 512), BF16),
            pltpu.VMEM((128, 4 * CELLS), BF16),
        ],
    )
    x3, ring_far, pack2 = lax.optimization_barrier((x3, ring_far, pack2))
    pack2_far, pack2_side = paired(pack2, "chan", half), paired(pack2, "chan", 1)
    rings = whole(ring, ring_far)
    act, slope2, act2, rims2, half2, ring_sorted = call(
        partial(fine_ring_kernel, nc),
        [
            shape((4, CELLS, 128)),
            shape((CELLS, 128), F32),
            shape((CELLS, 128)),
            shape((1, 256, 128)),
            shape((1, 128, 128)),
            shape((5, 128, 128), F32),
        ],
        where,
        z1c,
        w1t,
        wdt,
        *rings,
        scratch=[
            pltpu.VMEM((5, 128, 128), BF16),
            pltpu.VMEM((4, CELLS, 128), F32),
            pltpu.VMEM((CELLS, 128), F32),
        ],
    )
    rims2, half2, pack2_side = lax.optimization_barrier((rims2, half2, pack2_side))
    act1, slope1, x3 = call(
        own_fine_kernel,
        [shape((own, 4 * CELLS)), shape((own, 4 * CELLS), F32), shape((4, PADDED, 384))],
        conv1_weight,
        ring_sorted,
        x3,
        alias={2: 2},
    )
    all_rims2, (act1, slope1, x3, pack2_far) = copies(rims2, half2, (act1, slope1, x3, pack2_far))
    packs2 = [pack2, pack2_side, pack2_far, paired(pack2_far, "chan", 1)]
    rows = -(-23 * own // (16 * tiles)) * 16
    output, late = call(
        partial(level_kernel, nc, spots_of()),
        [shape((own, 4 * CELLS)), shape((rows * tiles, 128))],
        codes,
        where,
        act2,
        slope2,
        act,
        wdt,
        act1,
        slope1,
        sorted_g,
        x3,
        matrix,
        *packs2,
        *rings,
        *all_rims2,
        scratch=[
            pltpu.VMEM((384, 384), BF16),
            pltpu.VMEM((1152, 128), BF16),
            pltpu.VMEM((128, 128), BF16),
            pltpu.VMEM((128, CELLS), BF16),
            pltpu.VMEM((128, tiles * 128), BF16),
            pltpu.VMEM((tiles, 256, 128), BF16),
            pltpu.VMEM((34 * HALF, 128), F32),
            pltpu.VMEM((34 * HALF, 128), F32),
            pltpu.VMEM((CELLS + 4 * HALF, 128), BF16),
            pltpu.VMEM((34 * HALF, 384), F32),
            pltpu.VMEM((PADDED, 384), BF16),
            pltpu.VMEM((CELLS, 128), BF16),
            pltpu.VMEM((CELLS, 128), F32),
            pltpu.VMEM((128, 128), F32),
        ],
    )
    pieces = swap(late.reshape(tiles, rows, 128))
    total = call(partial(sum_kernel, scale), shape((rows, 128)), pieces)
    total = swap(jnp.broadcast_to(total[None], (tiles, rows, 128)))
    grads = call(
        unpack_kernel,
        [
            shape((9, own, 128), F32),
            shape((4, own, 128), F32),
            shape((9, own, 128), F32),
            shape((own, 128), F32),
        ],
        total.reshape(tiles * rows, 128),
    )
    return (output, *grads)


def solution(mesh):
    placed = (
        P("chan", "tile"),
        P(None, "chan", None),
        P(None, "chan", None),
        P(None, "chan", None),
        P("chan", None),
        P("chan", "tile"),
        P(),
    )
    return jax.shard_map(
        per_device,
        mesh=mesh,
        in_specs=placed,
        out_specs=(
            P("chan", "tile"),
            P(None, "chan", None),
            P(None, "chan", None),
            P(None, "chan", None),
            P("chan", None),
        ),
        check_vma=False,
    )
```

profile of v0, /device:TPU:0, one launch (start us, length us, event | category | flops | bytes accessed | tf_op | source)
XLA Modules:
  0.0 75.1 jit_solution(1856465463258870337)
XLA Ops:
  0.6 3.3 %shard_map.128 = (bf16[45,32,128]{2,1,0:T(8,128)(2,1)}, bf16[1,5,32,128]{3,2,1,0:T(8,128)(2,1)}, bf16[32,4096]{1,0:T(8,128)(2,1)}, bf16[18,32,128]{2,1,0:T(8,128)(2,1)}) custom-call(bf16[32,4096]{1,0:T(8,128)(2,1)} %f_hbm.1, bf16[32,4096]{1,0:T(8,128)(2,1)} %g_hbm.1, bf16[9,32,128]{2,1,0:T(8,128)(2,1)} %w1_ref.1, bf16[4,32,128]{2,1,0:T(8,128)(2,1)} %wd_hbm.1, ...), custom_call_target="tpu_custom_call" | custom-call | tf_op jit(solution)/shard_map/pallas_call | solution.py:687
  4.0 4.1 %collective-permute-start = (bf16[1,5,32,128]{3,2,1,0:T(8,128)(2,1)}, bf16[1,5,32,128]{3,2,1,0:T(8,128)(2,1)S(1)}, u32[]{:S(2)}, u32[]{:S(2)}) collective-permute-start(bf16[1,5,32,128]{3,2,1,0:T(8,128)(2,1)} %get-tuple-element.51.rims_ref), channel_id=1, source_target_pairs={{0,16},{4,20},{8,24},{12,28},{16,0},{20,4},{24,8},{28,12},{1,17},{... | collective-permute-start | bytes 122888 | tf_op jit(solution)/shard_map/ppermute | solution.py:727
  8.1 1.5 %collective-permute-start.4 = (bf16[45,32,128]{2,1,0:T(8,128)(2,1)}, bf16[45,32,128]{2,1,0:T(8,128)(2,1)S(1)}, u32[]{:S(2)}, u32[]{:S(2)}) collective-permute-start(bf16[45,32,128]{2,1,0:T(8,128)(2,1)} %get-tuple-element.52.pack_ref), channel_id=1, source_target_pairs={{0,2},{1,3},{2,0},{3,1},{4,6},{5,7},{6,4},{7,5},{8,10},{9,11},{10,... | collective-permute-start | bytes 1105928 | tf_op jit(solution)/shard_map/ppermute | solution.py:727
  9.6 1.6 %collective-permute-start.2 = (bf16[1,5,32,128]{3,2,1,0:T(8,128)(2,1)}, bf16[1,5,32,128]{3,2,1,0:T(8,128)(2,1)S(1)}, u32[]{:S(2)}, u32[]{:S(2)}) collective-permute-start(bf16[1,5,32,128]{3,2,1,0:T(8,128)(2,1)} %get-tuple-element.51.rims_ref), channel_id=1, source_target_pairs={{0,8},{4,12},{8,0},{12,4},{16,24},{20,28},{24,16},{28,20},{1,9},{5... | collective-permute-start | bytes 122888 | tf_op jit(solution)/shard_map/ppermute | solution.py:727
  11.1 1.2 %collective-permute-start.1 = (bf16[1,5,32,128]{3,2,1,0:T(8,128)(2,1)S(1)}, bf16[1,5,32,128]{3,2,1,0:T(8,128)(2,1)S(1)}, u32[]{:S(2)}, u32[]{:S(2)}) collective-permute-start(bf16[1,5,32,128]{3,2,1,0:T(8,128)(2,1)S(1)} %collective-permute-done.far_ref), channel_id=1, source_target_pairs={{0,8},{4,12},{8,0},{12,4},{16,24},{20,28},{24,16},{28,20},{1,9},{5... | collective-permute-start | bytes 122888 | tf_op jit(solution)/shard_map/ppermute | solution.py:727
  12.4 1.0 %copy-done.1 = bf16[45,32,128]{2,1,0:T(8,128)(2,1)S(1)} copy-done((bf16[45,32,128]{2,1,0:T(8,128)(2,1)S(1)}, bf16[45,32,128]{2,1,0:T(8,128)(2,1)}, u32[]{:S(2)}) %copy-start.1) | copy-done | bytes 368664
  13.4 0.8 %copy-done.5 = bf16[1,5,32,128]{3,2,1,0:T(8,128)(2,1)S(1)} copy-done((bf16[1,5,32,128]{3,2,1,0:T(8,128)(2,1)S(1)}, bf16[1,5,32,128]{3,2,1,0:T(8,128)(2,1)}, u32[]{:S(2)}) %copy-start.5) | copy-done | bytes 40984
  14.2 1.6 %collective-permute-start.5 = (bf16[2,5,32,128]{3,2,1,0:T(8,128)(2,1)S(1)}, bf16[2,5,32,128]{3,2,1,0:T(8,128)(2,1)S(1)}, u32[]{:S(2)}, u32[]{:S(2)}) collective-permute-start(bf16[2,5,32,128]{3,2,1,0:T(8,128)(2,1)S(1)} %get-tuple-element.57.refs_0_), channel_id=1, source_target_pairs={{0,4},{4,0},{8,12},{12,8},{16,20},{20,16},{24,28},{28,24},{1,5},{5... | collective-permute-start | bytes 245768 | tf_op jit(solution)/shard_map/ppermute | solution.py:727
  15.8 0.9 %collective-permute-start.6 = (bf16[1,5,32,128]{3,2,1,0:T(8,128)(2,1)S(1)}, bf16[1,5,32,128]{3,2,1,0:T(8,128)(2,1)S(1)}, u32[]{:S(2)}, u32[]{:S(2)}) collective-permute-start(bf16[1,5,32,128]{3,2,1,0:T(8,128)(2,1)S(1)} %collective-permute-done.2.refs_1_), channel_id=1, source_target_pairs={{0,4},{4,0},{8,12},{12,8},{16,20},{20,16},{24,28},{28,24},{1,5},{5... | collective-permute-start | bytes 122888 | tf_op jit(solution)/shard_map/ppermute | solution.py:727
  16.7 1.2 %collective-permute-start.7 = (bf16[1,5,32,128]{3,2,1,0:T(8,128)(2,1)S(1)}, bf16[1,5,32,128]{3,2,1,0:T(8,128)(2,1)S(1)}, u32[]{:S(2)}, u32[]{:S(2)}) collective-permute-start(bf16[1,5,32,128]{3,2,1,0:T(8,128)(2,1)S(1)} %collective-permute-done.1.refs_2_), channel_id=1, source_target_pairs={{0,4},{4,0},{8,12},{12,8},{16,20},{20,16},{24,28},{28,24},{1,5},{5... | collective-permute-start | bytes 122888 | tf_op jit(solution)/shard_map/ppermute | solution.py:727
  17.8 0.7 copy.15
  18.5 0.7 fusion.3.codes_ref
  19.2 0.6 collective-permute-done.6.refs_4_
  19.8 0.9 %collective-permute-done.7.refs_5_ = bf16[1,5,32,128]{3,2,1,0:T(8,128)(2,1)S(1)} collective-permute-done((bf16[1,5,32,128]{3,2,1,0:T(8,128)(2,1)S(1)}, bf16[1,5,32,128]{3,2,1,0:T(8,128)(2,1)S(1)}, u32[]{:S(2)}, u32[]{:S(2)}) %collective-permute-start.7) | collective-permute-done | bytes 40992 | tf_op jit(solution)/shard_map/ppermute | solution.py:727
  20.7 0.7 shard_map.130.refs_0_.refs_4_
  21.5 1.3 %collective-permute-start.10 = (bf16[13,32,128]{2,1,0:T(8,128)(2,1)S(1)}, bf16[13,32,128]{2,1,0:T(8,128)(2,1)S(1)}, u32[]{:S(2)}, u32[]{:S(2)}) collective-permute-start(bf16[13,32,128]{2,1,0:T(8,128)(2,1)S(1)} %shard_map.130.refs_0_.refs_4_), channel_id=1, source_target_pairs={{0,2},{1,3},{2,0},{3,1},{4,6},{5,7},{6,4},{7,5},{8,10},{9,11},{10,... | collective-permute-start | bytes 319496 | tf_op jit(solution)/shard_map/ppermute | solution.py:727
  23.1 3.6 %shard_map.131 = (bf16[4,1152,384]{2,1,0:T(8,128)(2,1)S(1)}, f32[4,1024,128]{2,1,0:T(8,128)S(1)}, bf16[1152,128]{1,0:T(8,128)(2,1)S(1)}, bf16[512,128]{1,0:T(8,128)(2,1)S(1)}) custom-call(s32[4]{0:T(128)S(1)} %pad_add_fusion.where_ref, bf16[45,32,128]{2,1,0:T(8,128)(2,1)S(1)} %get-tuple-element.56.refs_0_, ...), custom_call_target="tpu_custom_call" | custom-call | tf_op jit(solution)/shard_map/pallas_call | solution.py:687
  27.0 0.4 collective-permute-start.9
  27.5 1.3 %collective-permute-start.17 = (bf16[18,32,128]{2,1,0:T(8,128)(2,1)}, bf16[18,32,128]{2,1,0:T(8,128)(2,1)S(1)}, u32[]{:S(2)}, u32[]{:S(2)}) collective-permute-start(bf16[18,32,128]{2,1,0:T(8,128)(2,1)} %get-tuple-element.73.refs_0_), channel_id=1, source_target_pairs={{0,2},{1,3},{2,0},{3,1},{4,6},{5,7},{6,4},{7,5},{8,10},{9,11},{10,... | collective-permute-start | bytes 442376 | tf_op jit(solution)/shard_map/ppermute | solution.py:727
  28.8 2.6 %shard_map.132 = (bf16[4,1024,128]{2,1,0:T(8,128)(2,1)S(1)}, f32[1024,128]{1,0:T(8,128)S(1)}, bf16[1024,128]{1,0:T(8,128)(2,1)S(1)}, bf16[1,256,128]{2,1,0:T(8,1...) custom-call(s32[4]{0:T(128)S(1)} %pad_add_fusion.where_ref, ...), custom_call_target="tpu_custom_call" | custom-call | tf_op jit(solution)/shard_map/pallas_call | solution.py:687
  31.4 3.7 %collective-permute-start.13 = (bf16[1,256,128]{2,1,0:T(8,128)(2,1)S(1)}, bf16[1,256,128]{2,1,0:T(8,128)(2,1)S(1)}, u32[]{:S(2)}, u32[]{:S(2)}) collective-permute-start(bf16[1,256,128]{2,1,0:T(8,128)(2,1)S(1)} %get-tuple-element.74.refs_8_), channel_id=1, source_target_pairs={{0,28},{1,25},{2,30},{3,27},{4,24},{5,29},{6,26},{7,31},{8,20},{9,... | collective-permute-start | bytes 196616 | tf_op jit(solution)/shard_map/ppermute | solution.py:756
  35.1 1.4 %collective-permute-start.15 = (bf16[1,256,128]{2,1,0:T(8,128)(2,1)S(1)}, bf16[1,256,128]{2,1,0:T(8,128)(2,1)S(1)}, u32[]{:S(2)}, u32[]{:S(2)}) collective-permute-start(bf16[1,256,128]{2,1,0:T(8,128)(2,1)S(1)} %get-tuple-element.74.refs_8_), channel_id=1, source_target_pairs={{0,8},{1,13},{2,10},{3,15},{4,12},{5,9},{6,14},{7,11},{8,0},{9,5},... | collective-permute-start | bytes 196616 | tf_op jit(solution)/shard_map/ppermute | solution.py:756
  36.5 0.8 %collective-permute-start.16 = (bf16[1,128,128]{2,1,0:T(8,128)(2,1)S(1)}, bf16[1,128,128]{2,1,0:T(8,128)(2,1)S(1)}, u32[]{:S(2)}, u32[]{:S(2)}) collective-permute-start(bf16[1,128,128]{2,1,0:T(8,128)(2,1)S(1)} %get-tuple-element.75), channel_id=1, source_target_pairs={{0,4},{4,0},{8,12},{12,8},{16,20},{20,16},{24,28},{28,24},{1,5},{5... | collective-permute-start | bytes 98312 | tf_op jit(solution)/shard_map/ppermute | solution.py:727
  37.3 3.0 %shard_map.133 = (bf16[32,4096]{1,0:T(8,128)(2,1)S(1)}, f32[32,4096]{1,0:T(8,128)S(1)}, bf16[4,1152,384]{2,1,0:T(8,128)(2,1)S(1)}) custom-call(bf16[9,32,128]{2,1,0:T(8,128)(2,1)S(1)} %copy-done.2, f32[5,128,128]{2,1,0:T(8,128)S(1)} %get-tuple-element.76.ring, bf16[4,1152,384]{2,1,0:T(8,128)(2,1)S(1)} %get-tuple-element.77.x3_in), custom_call_target="tpu_custom_call", output_to_operand_aliasing={{2}: (2, {})} | custom-call | tf_op jit(solution)/shard_map/pallas_call | solution.py:687
  40.6 0.7 collective-permute-done.14.refs_10_
  41.3 0.5 collective-permute-start.19
  41.8 0.5 collective-permute-start.21
  42.3 1.1 %collective-permute-done.22.refs_16_ = bf16[1,128,128]{2,1,0:T(8,128)(2,1)S(1)} collective-permute-done((bf16[1,128,128]{2,1,0:T(8,128)(2,1)S(1)}, bf16[1,128,128]{2,1,0:T(8,128)(2,1)S(1)}, u32[]{:S(2)}, u32[]{:S(2)}) %collective-permute-start.22) | collective-permute-done | bytes 32800 | tf_op jit(solution)/shard_map/ppermute | solution.py:727
  43.5 7.3 %shard_map.134 = (bf16[32,4096]{1,0:T(8,128)(2,1)}, bf16[768,128]{1,0:T(8,128)(2,1)S(1)}) custom-call(s32[8,8]{1,0:T(8,128)S(1)} %fusion.3.codes_ref, s32[4]{0:T(128)S(1)} %pad_add_fusion.where_ref, bf16[1024,128]{1,0:T(8,128)(2,1)S(1)} %get-tuple-element.68.act2_ref, f32[1024,128]{1,0:T(8,128)S(1)} %get-tuple-element.69.slope2_ref, ...), custom_call_target="tpu_custom_call" | custom-call | tf_op jit(solution)/shard_map/pallas_call | solution.py:687
  50.8 12.7 %all_to_all.10.in_ref = bf16[8,96,128]{2,1,0:T(8,128)(2,1)S(1)} all-to-all(bf16[8,96,128]{2,1,0:T(8,128)(2,1)S(1)} %bitcast.19), channel_id=1, replica_groups=mesh['tile'=8,'chan'=4] {'tile'}, dimensions={0} | all-to-all | bytes 393216 | tf_op jit(solution)/shard_map/all_to_all | solution.py:763
  63.6 10.7 %all_to_all.11 = bf16[8,96,128]{2,1,0:T(8,128)(2,1)S(1)} all-to-all(bf16[8,96,128]{2,1,0:T(8,128)(2,1)S(1)} %broadcast_in_dim.12), channel_id=1, replica_groups=mesh['tile'=8,'chan'=4] {'tile'}, dimensions={0} | all-to-all | bytes 393216 | tf_op jit(solution)/shard_map/all_to_all | solution.py:763
  74.3 0.7 shard_map.136
  (41 shorter events, 1.3 us)
Async XLA Ops:
  0.6 36.7 %copy-start.2 = (bf16[9,32,128]{2,1,0:T(8,128)(2,1)S(1)}, bf16[9,32,128]{2,1,0:T(8,128)(2,1)}, u32[]{:S(2)}) copy-start(bf16[9,32,128]{2,1,0:T(8,128)(2,1)} %w1_ref.1) | copy-start | bytes 221188
  4.0 7.2 %collective-permute-start = (bf16[1,5,32,128]{3,2,1,0:T(8,128)(2,1)}, bf16[1,5,32,128]{3,2,1,0:T(8,128)(2,1)S(1)}, u32[]{:S(2)}, u32[]{:S(2)}) collective-permute-start(bf16[1,5,32,128]{3,2,1,0:T(8,128)(2,1)} %get-tuple-element.51.rims_ref), channel_id=1, source_target_pairs={{0,16},{4,20},{8,24},{12,28},{16,0},{20,4},{24,8},{28,12},{1,17},{... | collective-permute-start | bytes 122888 | tf_op jit(solution)/shard_map/ppermute | solution.py:727
  8.1 13.3 %collective-permute-start.4 = (bf16[45,32,128]{2,1,0:T(8,128)(2,1)}, bf16[45,32,128]{2,1,0:T(8,128)(2,1)S(1)}, u32[]{:S(2)}, u32[]{:S(2)}) collective-permute-start(bf16[45,32,128]{2,1,0:T(8,128)(2,1)} %get-tuple-element.52.pack_ref), channel_id=1, source_target_pairs={{0,2},{1,3},{2,0},{3,1},{4,6},{5,7},{6,4},{7,5},{8,10},{9,11},{10,... | collective-permute-start | bytes 1105928 | tf_op jit(solution)/shard_map/ppermute | solution.py:727
  9.6 6.2 %collective-permute-start.2 = (bf16[1,5,32,128]{3,2,1,0:T(8,128)(2,1)}, bf16[1,5,32,128]{3,2,1,0:T(8,128)(2,1)S(1)}, u32[]{:S(2)}, u32[]{:S(2)}) collective-permute-start(bf16[1,5,32,128]{3,2,1,0:T(8,128)(2,1)} %get-tuple-element.51.rims_ref), channel_id=1, source_target_pairs={{0,8},{4,12},{8,0},{12,4},{16,24},{20,28},{24,16},{28,20},{1,9},{5... | collective-permute-start | bytes 122888 | tf_op jit(solution)/shard_map/ppermute | solution.py:727
  11.1 11.7 %collective-permute-start.3 = (bf16[45,32,128]{2,1,0:T(8,128)(2,1)}, bf16[45,32,128]{2,1,0:T(8,128)(2,1)S(1)}, u32[]{:S(2)}, u32[]{:S(2)}) collective-permute-start(bf16[45,32,128]{2,1,0:T(8,128)(2,1)} %get-tuple-element.52.pack_ref), channel_id=1, source_target_pairs={{0,1},{1,0},{2,3},{3,2},{4,5},{5,4},{6,7},{7,6},{8,9},{9,8},{10,11... | collective-permute-start | bytes 1105928 | tf_op jit(solution)/shard_map/ppermute | solution.py:727
  11.1 4.7 %collective-permute-start.1 = (bf16[1,5,32,128]{3,2,1,0:T(8,128)(2,1)S(1)}, bf16[1,5,32,128]{3,2,1,0:T(8,128)(2,1)S(1)}, u32[]{:S(2)}, u32[]{:S(2)}) collective-permute-start(bf16[1,5,32,128]{3,2,1,0:T(8,128)(2,1)S(1)} %collective-permute-done.far_ref), channel_id=1, source_target_pairs={{0,8},{4,12},{8,0},{12,4},{16,24},{20,28},{24,16},{28,20},{1,9},{5... | collective-permute-start | bytes 122888 | tf_op jit(solution)/shard_map/ppermute | solution.py:727
  12.4 1.0 %copy-start.1 = (bf16[45,32,128]{2,1,0:T(8,128)(2,1)S(1)}, bf16[45,32,128]{2,1,0:T(8,128)(2,1)}, u32[]{:S(2)}) copy-start(bf16[45,32,128]{2,1,0:T(8,128)(2,1)} %get-tuple-element.52.pack_ref) | copy-start | bytes 1105924
  13.4 0.8 %copy-start.5 = (bf16[1,5,32,128]{3,2,1,0:T(8,128)(2,1)S(1)}, bf16[1,5,32,128]{3,2,1,0:T(8,128)(2,1)}, u32[]{:S(2)}) copy-start(bf16[1,5,32,128]{3,2,1,0:T(8,128)(2,1)} %get-tuple-element.51.rims_ref) | copy-start | bytes 122884
  14.2 6.5 %collective-permute-start.5 = (bf16[2,5,32,128]{3,2,1,0:T(8,128)(2,1)S(1)}, bf16[2,5,32,128]{3,2,1,0:T(8,128)(2,1)S(1)}, u32[]{:S(2)}, u32[]{:S(2)}) collective-permute-start(bf16[2,5,32,128]{3,2,1,0:T(8,128)(2,1)S(1)} %get-tuple-element.57.refs_0_), channel_id=1, source_target_pairs={{0,4},{4,0},{8,12},{12,8},{16,20},{20,16},{24,28},{28,24},{1,5},{5... | collective-permute-start | bytes 245768 | tf_op jit(solution)/shard_map/ppermute | solution.py:727
  15.8 4.0 %collective-permute-start.6 = (bf16[1,5,32,128]{3,2,1,0:T(8,128)(2,1)S(1)}, bf16[1,5,32,128]{3,2,1,0:T(8,128)(2,1)S(1)}, u32[]{:S(2)}, u32[]{:S(2)}) collective-permute-start(bf16[1,5,32,128]{3,2,1,0:T(8,128)(2,1)S(1)} %collective-permute-done.2.refs_1_), channel_id=1, source_target_pairs={{0,4},{4,0},{8,12},{12,8},{16,20},{20,16},{24,28},{28,24},{1,5},{5... | collective-permute-start | bytes 122888 | tf_op jit(solution)/shard_map/ppermute | solution.py:727
  16.7 4.0 %collective-permute-start.7 = (bf16[1,5,32,128]{3,2,1,0:T(8,128)(2,1)S(1)}, bf16[1,5,32,128]{3,2,1,0:T(8,128)(2,1)S(1)}, u32[]{:S(2)}, u32[]{:S(2)}) collective-permute-start(bf16[1,5,32,128]{3,2,1,0:T(8,128)(2,1)S(1)} %collective-permute-done.1.refs_2_), channel_id=1, source_target_pairs={{0,4},{4,0},{8,12},{12,8},{16,20},{20,16},{24,28},{28,24},{1,5},{5... | collective-permute-start | bytes 122888 | tf_op jit(solution)/shard_map/ppermute | solution.py:727
  21.4 1.8 %collective-permute-start.8 = (bf16[45,32,128]{2,1,0:T(8,128)(2,1)S(1)}, bf16[45,32,128]{2,1,0:T(8,128)(2,1)S(1)}, u32[]{:S(2)}, u32[]{:S(2)}) collective-permute-start(bf16[45,32,128]{2,1,0:T(8,128)(2,1)S(1)} %collective-permute-done.4.refs_2_), channel_id=1, source_target_pairs={{0,1},{1,0},{2,3},{3,2},{4,5},{5,4},{6,7},{7,6},{8,9},{9,8},{10,11... | collective-permute-start | bytes 1105928 | tf_op jit(solution)/shard_map/ppermute | solution.py:727
  21.5 5.4 %collective-permute-start.10 = (bf16[13,32,128]{2,1,0:T(8,128)(2,1)S(1)}, bf16[13,32,128]{2,1,0:T(8,128)(2,1)S(1)}, u32[]{:S(2)}, u32[]{:S(2)}) collective-permute-start(bf16[13,32,128]{2,1,0:T(8,128)(2,1)S(1)} %shard_map.130.refs_0_.refs_4_), channel_id=1, source_target_pairs={{0,2},{1,3},{2,0},{3,1},{4,6},{5,7},{6,4},{7,5},{8,10},{9,11},{10,... | collective-permute-start | bytes 319496 | tf_op jit(solution)/shard_map/ppermute | solution.py:727
  26.7 16.7 %copy-start = (bf16[512,1024]{1,0:T(8,128)(2,1)S(1)}, bf16[512,1024]{1,0:T(8,128)(2,1)}, u32[]{:S(2)}) copy-start(bf16[512,1024]{1,0:T(8,128)(2,1)} %constant.21.clone.m_hbm.m_ref) | copy-start | bytes 3145732
  26.8 16.7 %copy-start.3 = (bf16[32,4096]{1,0:T(8,128)(2,1)S(1)}, bf16[32,4096]{1,0:T(8,128)(2,1)}, u32[]{:S(2)}) copy-start(bf16[32,4096]{1,0:T(8,128)(2,1)} %get-tuple-element.83.og_ref) | copy-start | bytes 786436
  26.8 16.7 %copy-start.4 = (bf16[18,32,128]{2,1,0:T(8,128)(2,1)S(1)}, bf16[18,32,128]{2,1,0:T(8,128)(2,1)}, u32[]{:S(2)}) copy-start(bf16[18,32,128]{2,1,0:T(8,128)(2,1)} %get-tuple-element.73.refs_0_) | copy-start | bytes 442372
  26.8 4.6 %collective-permute-start.12 = (bf16[18,32,128]{2,1,0:T(8,128)(2,1)}, bf16[18,32,128]{2,1,0:T(8,128)(2,1)S(1)}, u32[]{:S(2)}, u32[]{:S(2)}) collective-permute-start(bf16[18,32,128]{2,1,0:T(8,128)(2,1)} %get-tuple-element.73.refs_0_), channel_id=1, source_target_pairs={{0,1},{1,0},{2,3},{3,2},{4,5},{5,4},{6,7},{7,6},{8,9},{9,8},{10,11... | collective-permute-start | bytes 442376 | tf_op jit(solution)/shard_map/ppermute | solution.py:727
  27.0 1.8 %collective-permute-start.9 = (bf16[13,32,128]{2,1,0:T(8,128)(2,1)S(1)}, bf16[13,32,128]{2,1,0:T(8,128)(2,1)S(1)}, u32[]{:S(2)}, u32[]{:S(2)}) collective-permute-start(bf16[13,32,128]{2,1,0:T(8,128)(2,1)S(1)} %shard_map.130.refs_0_.refs_4_), channel_id=1, source_target_pairs={{0,1},{1,0},{2,3},{3,2},{4,5},{5,4},{6,7},{7,6},{8,9},{9,8},{10,11... | collective-permute-start | bytes 319496 | tf_op jit(solution)/shard_map/ppermute | solution.py:727
  27.4 1.4 %collective-permute-start.11 = (bf16[13,32,128]{2,1,0:T(8,128)(2,1)S(1)}, bf16[13,32,128]{2,1,0:T(8,128)(2,1)S(1)}, u32[]{:S(2)}, u32[]{:S(2)}) collective-permute-start(bf16[13,32,128]{2,1,0:T(8,128)(2,1)S(1)} %collective-permute-done.10.refs_2_.refs_6_), channel_id=1, source_target_pairs={{0,1},{1,0},{2,3},{3,2},{4,5},{5,4},{6,7},{7,6},{8,9},{9,8},{10,11... | collective-permute-start | bytes 319496 | tf_op jit(solution)/shard_map/ppermute | solution.py:727
  27.5 12.9 %collective-permute-start.17 = (bf16[18,32,128]{2,1,0:T(8,128)(2,1)}, bf16[18,32,128]{2,1,0:T(8,128)(2,1)S(1)}, u32[]{:S(2)}, u32[]{:S(2)}) collective-permute-start(bf16[18,32,128]{2,1,0:T(8,128)(2,1)} %get-tuple-element.73.refs_0_), channel_id=1, source_target_pairs={{0,2},{1,3},{2,0},{3,1},{4,6},{5,7},{6,4},{7,5},{8,10},{9,11},{10,... | collective-permute-start | bytes 442376 | tf_op jit(solution)/shard_map/ppermute | solution.py:727
  31.4 9.1 %collective-permute-start.13 = (bf16[1,256,128]{2,1,0:T(8,128)(2,1)S(1)}, bf16[1,256,128]{2,1,0:T(8,128)(2,1)S(1)}, u32[]{:S(2)}, u32[]{:S(2)}) collective-permute-start(bf16[1,256,128]{2,1,0:T(8,128)(2,1)S(1)} %get-tuple-element.74.refs_8_), channel_id=1, source_target_pairs={{0,28},{1,25},{2,30},{3,27},{4,24},{5,29},{6,26},{7,31},{8,20},{9,... | collective-permute-start | bytes 196616 | tf_op jit(solution)/shard_map/ppermute | solution.py:756
  35.1 6.1 %collective-permute-start.14 = (bf16[1,256,128]{2,1,0:T(8,128)(2,1)S(1)}, bf16[1,256,128]{2,1,0:T(8,128)(2,1)S(1)}, u32[]{:S(2)}, u32[]{:S(2)}) collective-permute-start(bf16[1,256,128]{2,1,0:T(8,128)(2,1)S(1)} %get-tuple-element.74.refs_8_), channel_id=1, source_target_pairs={{0,16},{1,21},{2,18},{3,23},{4,20},{5,17},{6,22},{7,19},{8,24},{9,... | collective-permute-start | bytes 196616 | tf_op jit(solution)/shard_map/ppermute | solution.py:756
  35.1 6.1 %collective-permute-start.15 = (bf16[1,256,128]{2,1,0:T(8,128)(2,1)S(1)}, bf16[1,256,128]{2,1,0:T(8,128)(2,1)S(1)}, u32[]{:S(2)}, u32[]{:S(2)}) collective-permute-start(bf16[1,256,128]{2,1,0:T(8,128)(2,1)S(1)} %get-tuple-element.74.refs_8_), channel_id=1, source_target_pairs={{0,8},{1,13},{2,10},{3,15},{4,12},{5,9},{6,14},{7,11},{8,0},{9,5},... | collective-permute-start | bytes 196616 | tf_op jit(solution)/shard_map/ppermute | solution.py:756
  36.5 4.0 %collective-permute-start.16 = (bf16[1,128,128]{2,1,0:T(8,128)(2,1)S(1)}, bf16[1,128,128]{2,1,0:T(8,128)(2,1)S(1)}, u32[]{:S(2)}, u32[]{:S(2)}) collective-permute-start(bf16[1,128,128]{2,1,0:T(8,128)(2,1)S(1)} %get-tuple-element.75), channel_id=1, source_target_pairs={{0,4},{4,0},{8,12},{12,8},{16,20},{20,16},{24,28},{28,24},{1,5},{5... | collective-permute-start | bytes 98312 | tf_op jit(solution)/shard_map/ppermute | solution.py:727
  41.2 2.2 %collective-permute-start.18 = (bf16[18,32,128]{2,1,0:T(8,128)(2,1)S(1)}, bf16[18,32,128]{2,1,0:T(8,128)(2,1)S(1)}, u32[]{:S(2)}, u32[]{:S(2)}) collective-permute-start(bf16[18,32,128]{2,1,0:T(8,128)(2,1)S(1)} %collective-permute-done.17.refs_2_), channel_id=1, source_target_pairs={{0,1},{1,0},{2,3},{3,2},{4,5},{5,4},{6,7},{7,6},{8,9},{9,8},{10,11... | collective-permute-start | bytes 442376 | tf_op jit(solution)/shard_map/ppermute | solution.py:727
  41.3 2.2 %collective-permute-start.19 = (bf16[1,256,128]{2,1,0:T(8,128)(2,1)S(1)}, bf16[1,256,128]{2,1,0:T(8,128)(2,1)S(1)}, u32[]{:S(2)}, u32[]{:S(2)}) collective-permute-start(bf16[1,256,128]{2,1,0:T(8,128)(2,1)S(1)} %collective-permute-done.13.refs_9_), channel_id=1, source_target_pairs={{0,1},{1,0},{2,3},{3,2},{4,5},{5,4},{6,7},{7,6},{8,9},{9,8},{10,11... | collective-permute-start | bytes 196616 | tf_op jit(solution)/shard_map/ppermute | solution.py:727
  41.7 1.7 %collective-permute-start.20 = (bf16[1,256,128]{2,1,0:T(8,128)(2,1)S(1)}, bf16[1,256,128]{2,1,0:T(8,128)(2,1)S(1)}, u32[]{:S(2)}, u32[]{:S(2)}) collective-permute-start(bf16[1,256,128]{2,1,0:T(8,128)(2,1)S(1)} %collective-permute-done.14.refs_10_), channel_id=1, source_target_pairs={{0,1},{1,0},{2,3},{3,2},{4,5},{5,4},{6,7},{7,6},{8,9},{9,8},{10,11... | collective-permute-start | bytes 196616 | tf_op jit(solution)/shard_map/ppermute | solution.py:727
  41.8 1.7 %collective-permute-start.21 = (bf16[1,256,128]{2,1,0:T(8,128)(2,1)S(1)}, bf16[1,256,128]{2,1,0:T(8,128)(2,1)S(1)}, u32[]{:S(2)}, u32[]{:S(2)}) collective-permute-start(bf16[1,256,128]{2,1,0:T(8,128)(2,1)S(1)} %collective-permute-done.15.refs_11_), channel_id=1, source_target_pairs={{0,1},{1,0},{2,3},{3,2},{4,5},{5,4},{6,7},{7,6},{8,9},{9,8},{10,11... | collective-permute-start | bytes 196616 | tf_op jit(solution)/shard_map/ppermute | solution.py:727
  42.2 1.2 %collective-permute-start.22 = (bf16[1,128,128]{2,1,0:T(8,128)(2,1)S(1)}, bf16[1,128,128]{2,1,0:T(8,128)(2,1)S(1)}, u32[]{:S(2)}, u32[]{:S(2)}) collective-permute-start(bf16[1,128,128]{2,1,0:T(8,128)(2,1)S(1)} %collective-permute-done.16.refs_12_), channel_id=1, source_target_pairs={{0,1},{1,0},{2,3},{3,2},{4,5},{5,4},{6,7},{7,6},{8,9},{9,8},{10,11... | collective-permute-start | bytes 98312 | tf_op jit(solution)/shard_map/ppermute | solution.py:727
where the time goes:
time: 75.4 us; the launch traced here: 75.1 us
  blocking collectives  23.4 us (31%)
  starting transfers between devices  22.3 us (30%)
  Pallas kernels  21.4 us (28%)
  waiting for transfers between devices  3.87 us (5%)
  local copies, waits for them, and re-layouts  2.51 us (3%)
  between operations  0.79 us (1%)
    all_to_all x2, blocking collectives, swap(): return lax.all_to_all(values, 'tile', split_axis=0, concat_axis=0)  23.4 us
    pallas_call x9, Pallas kernels, call(): pl.pallas_call(kernel, out_shape=outs, in_specs=specs, out_specs=[vmem] *...  21.4 us
    ppermute x20, starting transfers between devices, paired(): return lax.ppermute(values, axis, [(i, i ^ bit) for i in range(count)])  17.2 us
    ppermute x3, starting transfers between devices, copies(): got.append(lax.ppermute(block, ('tile', 'chan'), perm))  5.1 us
    ppermute x20, waiting for transfers between devices, paired(): return lax.ppermute(values, axis, [(i, i ^ bit) for i in range(count)])  3.21 us
    unnamed x12, local copies, waits for them, and re-layouts  1.79 us
  transfers between devices with their start and end apart: 23, of which 7 were waited for; matrix products, arithmetic and copies ran while one was open for 2% of the time, Pallas kernels for 13%

commit v1 on v0

--- a/solution.py
+++ b/solution.py
@@ -119,7 +119,7 @@
 
 
 def sort_kernel(
-    f_hbm, g_hbm, w1_hbm, wd_hbm, w2_hbm, up_hbm, m_hbm, pack_ref, rims_ref, sorted_ref, pack2_ref, f_ref, g_ref, m_ref, sems
+    f_hbm, g_hbm, w1_hbm, wd_hbm, w2_hbm, up_hbm, m_hbm, pack_ref, rims_ref, sorted_ref, f_ref, g_ref, m_ref, sems
 ):
     count = f_ref.shape[0]
     started = fetch(
@@ -129,8 +129,8 @@
             (g_hbm, g_ref),
             (w1_hbm, pack_ref.at[32:41]),
             (wd_hbm, pack_ref.at[41:45]),
-            (w2_hbm, pack2_ref.at[8:17]),
-            (up_hbm, pack2_ref.at[17]),
+            (w2_hbm, pack_ref.at[53:62]),
+            (up_hbm, pack_ref.at[62]),
         ],
         sems,
     )
@@ -165,7 +165,7 @@
     for jb in range(8):
         for ph in range(4):
             sorted_ref[:, ph * CELLS + jb * 128 : ph * CELLS + (jb + 1) * 128] = pieces[jb][ph].astype(BF16)
-        pack2_ref[jb] = ((pieces[jb][0] + pieces[jb][1]) + (pieces[jb][2] + pieces[jb][3])).astype(BF16)
+        pack_ref[45 + jb] = ((pieces[jb][0] + pieces[jb][1]) + (pieces[jb][2] + pieces[jb][3])).astype(BF16)
     for copy in started[3:]:
         copy.wait()
 
@@ -511,12 +511,12 @@
     *rims, out_ref, grad_ref, w2s, w2t, ups, pooled_all, prims, rims_all, left, right, g3pad, sums, a3, coarse, field, back = refs
     tile, me, tile_base, base = where_ref[0], where_ref[1], where_ref[2], where_ref[3]
     own = packs[0].shape[1]
-    place_conv(packs, base, 8, w2s)
+    place_conv(packs, base, 53, w2s)
     for slot in range(nc):
         row = rows_of(slot, base, own)
-        ups[pl.ds(row, own), :] = packs[slot][17]
+        ups[pl.ds(row, own), :] = packs[slot][62]
         for jb in range(8):
-            pooled_all[pl.ds(row, own), jb * 128 : (jb + 1) * 128] = packs[slot][jb]
+            pooled_all[pl.ds(row, own), jb * 128 : (jb + 1) * 128] = packs[slot][45 + jb]
         for other in range(mores[slot].shape[0] - 5):
             prims[pl.ds(row, own), other * 128 : (other + 1) * 128] = mores[slot][5 + other]
 
@@ -781,14 +781,9 @@
     matrix = sort_matrix()
     half = nc // 2
 
-    pack, rims, sorted_g, pack2 = call(
+    pack, rims, sorted_g = call(
         sort_kernel,
-        [
-            shape((45, own, 128)),
-            shape((1, 5, own, 128)),
-            shape((own, 4 * CELLS)),
-            shape((18, own, 128)),
-        ],
+        [shape((63, own, 128)), shape((1, 5, own, 128)), shape((own, 4 * CELLS))],
         features,
         out_grad,
         conv1_weight,
@@ -813,9 +808,7 @@
             stage_kernel, [shape(pack.shape), shape((2,) + rims.shape[1:])], pack, rims, far
         )
         beside = paired(pair, "tile", 1)
-        cross, near, pack_near, pack2, adjacency = lax.optimization_barrier(
-            (cross, near, pack_near, pack2, adjacency)
-        )
+        cross, near, pack_near, adjacency = lax.optimization_barrier((cross, near, pack_near, adjacency))
         last = [paired(near, "tile", 1), paired(cross, "tile", 1)]
         all_rims = [pair, near, cross, beside] + last
         rim_spots = [[(slot, slot) for slot in group] for group in ((0, 4), (2,), (6,), (1, 5), (3,), (7,))]
@@ -855,8 +848,7 @@
             pltpu.VMEM((128, 4 * CELLS), BF16),
         ],
     )
-    x3, ring_far, pack2 = lax.optimization_barrier((x3, ring_far, pack2))
-    pack2_far, pack2_side = paired(pack2, "chan", half), paired(pack2, "chan", 1)
+    x3, ring_far = lax.optimization_barrier((x3, ring_far))
     rings = whole(ring, ring_far)
     act, slope2, act2, rims2, half2, ring_sorted = call(
         partial(fine_ring_kernel, nc),
@@ -879,7 +871,6 @@
             pltpu.VMEM((CELLS, 128), F32),
         ],
     )
-    rims2, half2, pack2_side = lax.optimization_barrier((rims2, half2, pack2_side))
     act1, slope1, x3 = call(
         own_fine_kernel,
         [shape((own, 4 * CELLS)), shape((own, 4 * CELLS), F32), shape((4, PADDED, 384))],
@@ -888,8 +879,7 @@
         x3,
         alias={2: 2},
     )
-    all_rims2, (act1, slope1, x3, pack2_far) = copies(rims2, half2, (act1, slope1, x3, pack2_far))
-    packs2 = [pack2, pack2_side, pack2_far, paired(pack2_far, "chan", 1)]
+    all_rims2, (act1, slope1, x3) = copies(rims2, half2, (act1, slope1, x3))
     rows = -(-23 * own // (16 * tiles)) * 16
     output, late = call(
         partial(level_kernel, nc, spots_of()),
@@ -905,7 +895,7 @@
         sorted_g,
         x3,
         matrix,
-        *packs2,
+        *packs,
         *rings,
         *all_rims2,
         scratch=[

time: 75.4 us -> 76 us (level)
  waiting for transfers between devices: 3.87 us -> 6.51 us
  starting transfers between devices: 22.3 us -> 20.2 us
    ppermute x20 -> x17, waiting for transfers between devices: 3.21 us -> 5.96 us  [paired(): return lax.ppermute(values, axis, [(i, i ^ bit) for i in range(count)])]
    ppermute x20 -> x17, starting transfers between devices: 17.2 us -> 14.8 us  [paired(): return lax.ppermute(values, axis, [(i, i ^ bit) for i in range(count)])]
    unnamed x12 -> x10, local copies, waits for them, and re-layouts: 1.79 us -> 1.83 us
  transfers between devices with their start and end apart: 23 -> 20, of which waited for: 7 -> 8; matrix products, arithmetic and copies ran while one was open for 2% -> 2% of each run, Pallas kernels for 13% -> 10%
where the time goes in v1:
time: 76 us; the launch traced here: 75.6 us
  blocking collectives  23.7 us (31%)
  Pallas kernels  21.2 us (28%)
  starting transfers between devices  20.2 us (27%)
  waiting for transfers between devices  6.51 us (9%)
  local copies, waits for them, and re-layouts  2.56 us (3%)
  between operations  0.76 us (1%)
    all_to_all x2, blocking collectives, swap(): return lax.all_to_all(values, 'tile', split_axis=0, concat_axis=0)  23.7 us
    pallas_call x9, Pallas kernels, call(): pl.pallas_call(kernel, out_shape=outs, in_specs=specs, out_specs=[vmem] *...  21.2 us
    ppermute x17, starting transfers between devices, paired(): return lax.ppermute(values, axis, [(i, i ^ bit) for i in range(count)])  14.8 us
    ppermute x17, waiting for transfers between devices, paired(): return lax.ppermute(values, axis, [(i, i ^ bit) for i in range(count)])  5.96 us
    ppermute x3, starting transfers between devices, copies(): got.append(lax.ppermute(block, ('tile', 'chan'), perm))  5.36 us
    unnamed x10, local copies, waits for them, and re-layouts  1.83 us
  transfers between devices with their start and end apart: 20, of which 8 were waited for; matrix products, arithmetic and copies ran while one was open for 2% of the time, Pallas kernels for 10%

profile of v1, /device:TPU:0, one launch (start us, length us, event | category | flops | bytes accessed | tf_op | source)
XLA Modules:
  0.0 75.6 jit_solution(12637199697524854278)
XLA Ops:
  0.6 3.3 %shard_map.128 = (bf16[63,32,128]{2,1,0:T(8,128)(2,1)}, bf16[1,5,32,128]{3,2,1,0:T(8,128)(2,1)}, bf16[32,4096]{1,0:T(8,128)(2,1)}) custom-call(bf16[32,4096]{1,0:T(8,128)(2,1)} %f_hbm.1, bf16[32,4096]{1,0:T(8,128)(2,1)} %g_hbm.1, bf16[9,32,128]{2,1,0:T(8,128)(2,1)} %w1_ref.1, bf16[4,32,128]{2,1,0:T(8,128)(2,1)} %wd_hbm.1, bf16[9,32,128]{2,1,0:T(8,128)(2,1)} %w2_hbm.1, ...), custom_call_target="tpu_custom_call" | custom-call | tf_op jit(solution)/shard_map/pallas_call | solution.py:687
  4.0 3.0 %collective-permute-start.4 = (bf16[63,32,128]{2,1,0:T(8,128)(2,1)}, bf16[63,32,128]{2,1,0:T(8,128)(2,1)S(1)}, u32[]{:S(2)}, u32[]{:S(2)}) collective-permute-start(bf16[63,32,128]{2,1,0:T(8,128)(2,1)} %get-tuple-element.45.pack_ref), channel_id=1, source_target_pairs={{0,2},{1,3},{2,0},{3,1},{4,6},{5,7},{6,4},{7,5},{8,10},{9,11},{10,... | collective-permute-start | bytes 1548296 | tf_op jit(solution)/shard_map/ppermute | solution.py:727
  7.0 2.6 %collective-permute-start = (bf16[1,5,32,128]{3,2,1,0:T(8,128)(2,1)}, bf16[1,5,32,128]{3,2,1,0:T(8,128)(2,1)S(1)}, u32[]{:S(2)}, u32[]{:S(2)}) collective-permute-start(bf16[1,5,32,128]{3,2,1,0:T(8,128)(2,1)} %get-tuple-element.44.rims_ref), channel_id=1, source_target_pairs={{0,16},{4,20},{8,24},{12,28},{16,0},{20,4},{24,8},{28,12},{1,17},{... | collective-permute-start | bytes 122888 | tf_op jit(solution)/shard_map/ppermute | solution.py:727
  9.6 1.6 %collective-permute-start.2 = (bf16[1,5,32,128]{3,2,1,0:T(8,128)(2,1)}, bf16[1,5,32,128]{3,2,1,0:T(8,128)(2,1)S(1)}, u32[]{:S(2)}, u32[]{:S(2)}) collective-permute-start(bf16[1,5,32,128]{3,2,1,0:T(8,128)(2,1)} %get-tuple-element.44.rims_ref), channel_id=1, source_target_pairs={{0,8},{4,12},{8,0},{12,4},{16,24},{20,28},{24,16},{28,20},{1,9},{5... | collective-permute-start | bytes 122888 | tf_op jit(solution)/shard_map/ppermute | solution.py:727
  11.1 1.1 %collective-permute-done.far_ref = bf16[1,5,32,128]{3,2,1,0:T(8,128)(2,1)S(1)} collective-permute-done((bf16[1,5,32,128]{3,2,1,0:T(8,128)(2,1)}, bf16[1,5,32,128]{3,2,1,0:T(8,128)(2,1)S(1)}, u32[]{:S(2)}, u32[]{:S(2)}) %collective-permute-start) | collective-permute-done | bytes 40992 | tf_op jit(solution)/shard_map/ppermute | solution.py:727
  12.2 1.4 %collective-permute-start.1 = (bf16[1,5,32,128]{3,2,1,0:T(8,128)(2,1)S(1)}, bf16[1,5,32,128]{3,2,1,0:T(8,128)(2,1)S(1)}, u32[]{:S(2)}, u32[]{:S(2)}) collective-permute-start(bf16[1,5,32,128]{3,2,1,0:T(8,128)(2,1)S(1)} %collective-permute-done.far_ref), channel_id=1, source_target_pairs={{0,8},{4,12},{8,0},{12,4},{16,24},{20,28},{24,16},{28,20},{1,9},{5... | collective-permute-start | bytes 122888 | tf_op jit(solution)/shard_map/ppermute | solution.py:727
  13.7 1.0 %copy-done.1 = bf16[63,32,128]{2,1,0:T(8,128)(2,1)S(1)} copy-done((bf16[63,32,128]{2,1,0:T(8,128)(2,1)S(1)}, bf16[63,32,128]{2,1,0:T(8,128)(2,1)}, u32[]{:S(2)}) %copy-start.1) | copy-done | bytes 516120
  14.8 0.8 %copy-done.4 = bf16[1,5,32,128]{3,2,1,0:T(8,128)(2,1)S(1)} copy-done((bf16[1,5,32,128]{3,2,1,0:T(8,128)(2,1)S(1)}, bf16[1,5,32,128]{3,2,1,0:T(8,128)(2,1)}, u32[]{:S(2)}) %copy-start.4) | copy-done | bytes 40984
  15.6 1.6 %collective-permute-start.5 = (bf16[2,5,32,128]{3,2,1,0:T(8,128)(2,1)S(1)}, bf16[2,5,32,128]{3,2,1,0:T(8,128)(2,1)S(1)}, u32[]{:S(2)}, u32[]{:S(2)}) collective-permute-start(bf16[2,5,32,128]{3,2,1,0:T(8,128)(2,1)S(1)} %get-tuple-element.49.refs_0_), channel_id=1, source_target_pairs={{0,4},{4,0},{8,12},{12,8},{16,20},{20,16},{24,28},{28,24},{1,5},{5... | collective-permute-start | bytes 245768 | tf_op jit(solution)/shard_map/ppermute | solution.py:727
  17.2 0.6 collective-permute-start.6
  17.8 1.5 %collective-permute-start.7 = (bf16[1,5,32,128]{3,2,1,0:T(8,128)(2,1)S(1)}, bf16[1,5,32,128]{3,2,1,0:T(8,128)(2,1)S(1)}, u32[]{:S(2)}, u32[]{:S(2)}) collective-permute-start(bf16[1,5,32,128]{3,2,1,0:T(8,128)(2,1)S(1)} %collective-permute-done.1.refs_2_), channel_id=1, source_target_pairs={{0,4},{4,0},{8,12},{12,8},{16,20},{20,16},{24,28},{28,24},{1,5},{5... | collective-permute-start | bytes 122888 | tf_op jit(solution)/shard_map/ppermute | solution.py:727
  19.2 0.7 copy.15
  19.9 0.7 fusion.3.codes_ref
  20.6 0.6 collective-permute-done.6.refs_4_
  21.2 0.6 collective-permute-done.7.refs_5_
  21.8 0.7 shard_map.130.refs_0_.refs_4_
  22.5 0.6 collective-permute-start.10
  23.3 1.1 %collective-permute-done.8.refs_3_ = bf16[63,32,128]{2,1,0:T(8,128)(2,1)S(1)} collective-permute-done((bf16[63,32,128]{2,1,0:T(8,128)(2,1)S(1)}, bf16[63,32,128]{2,1,0:T(8,128)(2,1)S(1)}, u32[]{:S(2)}, u32[]{:S(2)}) %collective-permute-start.8) | collective-permute-done | bytes 516128 | tf_op jit(solution)/shard_map/ppermute | solution.py:727
  24.4 3.6 %shard_map.131 = (bf16[4,1152,384]{2,1,0:T(8,128)(2,1)S(1)}, f32[4,1024,128]{2,1,0:T(8,128)S(1)}, bf16[1152,128]{1,0:T(8,128)(2,1)S(1)}, bf16[512,128]{1,0:T(8,128)(2,1)S(1)}) custom-call(s32[4]{0:T(128)S(1)} %pad_add_fusion.where_ref, bf16[63,32,128]{2,1,0:T(8,128)(2,1)S(1)} %get-tuple-element.48.refs_0_, ...), custom_call_target="tpu_custom_call" | custom-call | tf_op jit(solution)/shard_map/pallas_call | solution.py:687
  28.3 1.2 %collective-permute-done.11.refs_3_.refs_7_ = bf16[13,32,128]{2,1,0:T(8,128)(2,1)S(1)} collective-permute-done((bf16[13,32,128]{2,1,0:T(8,128)(2,1)S(1)}, bf16[13,32,128]{2,1,0:T(8,128)(2,1)S(1)}, u32[]{:S(2)}, u32[]{:S(2)}) %collective-permute-start.11) | collective-permute-done | bytes 106528 | tf_op jit(solution)/shard_map/ppermute | solution.py:727
  29.4 2.6 %shard_map.132 = (bf16[4,1024,128]{2,1,0:T(8,128)(2,1)S(1)}, f32[1024,128]{1,0:T(8,128)S(1)}, bf16[1024,128]{1,0:T(8,128)(2,1)S(1)}, bf16[1,256,128]{2,1,0:T(8,1...) custom-call(s32[4]{0:T(128)S(1)} %pad_add_fusion.where_ref, ...), custom_call_target="tpu_custom_call" | custom-call | tf_op jit(solution)/shard_map/pallas_call | solution.py:687
  32.1 3.9 %collective-permute-start.12 = (bf16[1,256,128]{2,1,0:T(8,128)(2,1)S(1)}, bf16[1,256,128]{2,1,0:T(8,128)(2,1)S(1)}, u32[]{:S(2)}, u32[]{:S(2)}) collective-permute-start(bf16[1,256,128]{2,1,0:T(8,128)(2,1)S(1)} %get-tuple-element.62.refs_8_), channel_id=1, source_target_pairs={{0,28},{1,25},{2,30},{3,27},{4,24},{5,29},{6,26},{7,31},{8,20},{9,... | collective-permute-start | bytes 196616 | tf_op jit(solution)/shard_map/ppermute | solution.py:756
  35.9 1.5 %collective-permute-start.14 = (bf16[1,256,128]{2,1,0:T(8,128)(2,1)S(1)}, bf16[1,256,128]{2,1,0:T(8,128)(2,1)S(1)}, u32[]{:S(2)}, u32[]{:S(2)}) collective-permute-start(bf16[1,256,128]{2,1,0:T(8,128)(2,1)S(1)} %get-tuple-element.62.refs_8_), channel_id=1, source_target_pairs={{0,8},{1,13},{2,10},{3,15},{4,12},{5,9},{6,14},{7,11},{8,0},{9,5},... | collective-permute-start | bytes 196616 | tf_op jit(solution)/shard_map/ppermute | solution.py:756
  37.4 0.6 collective-permute-start.15
  38.0 3.0 %shard_map.133 = (bf16[32,4096]{1,0:T(8,128)(2,1)S(1)}, f32[32,4096]{1,0:T(8,128)S(1)}, bf16[4,1152,384]{2,1,0:T(8,128)(2,1)S(1)}) custom-call(bf16[9,32,128]{2,1,0:T(8,128)(2,1)S(1)} %copy-done.2, f32[5,128,128]{2,1,0:T(8,128)S(1)} %get-tuple-element.64.ring, bf16[4,1152,384]{2,1,0:T(8,128)(2,1)S(1)} %get-tuple-element.65.x3_in), custom_call_target="tpu_custom_call", output_to_operand_aliasing={{2}: (2, {})} | custom-call | tf_op jit(solution)/shard_map/pallas_call | solution.py:687
  41.0 0.5 collective-permute-done.15.refs_12_
  41.6 0.5 collective-permute-done.13.refs_10_
  43.1 0.9 %collective-permute-done.19.refs_16_ = bf16[1,128,128]{2,1,0:T(8,128)(2,1)S(1)} collective-permute-done((bf16[1,128,128]{2,1,0:T(8,128)(2,1)S(1)}, bf16[1,128,128]{2,1,0:T(8,128)(2,1)S(1)}, u32[]{:S(2)}, u32[]{:S(2)}) %collective-permute-start.19) | collective-permute-done | bytes 32800 | tf_op jit(solution)/shard_map/ppermute | solution.py:727
  44.0 7.1 %shard_map.134 = (bf16[32,4096]{1,0:T(8,128)(2,1)}, bf16[768,128]{1,0:T(8,128)(2,1)S(1)}) custom-call(s32[8,8]{1,0:T(8,128)S(1)} %fusion.3.codes_ref, s32[4]{0:T(128)S(1)} %pad_add_fusion.where_ref, bf16[1024,128]{1,0:T(8,128)(2,1)S(1)} %get-tuple-element.59.act2_ref, f32[1024,128]{1,0:T(8,128)S(1)} %get-tuple-element.60.slope2_ref, ...), custom_call_target="tpu_custom_call" | custom-call | tf_op jit(solution)/shard_map/pallas_call | solution.py:687
  51.1 12.9 %all_to_all.10.in_ref = bf16[8,96,128]{2,1,0:T(8,128)(2,1)S(1)} all-to-all(bf16[8,96,128]{2,1,0:T(8,128)(2,1)S(1)} %bitcast.19), channel_id=1, replica_groups=mesh['tile'=8,'chan'=4] {'tile'}, dimensions={0} | all-to-all | bytes 393216 | tf_op jit(solution)/shard_map/all_to_all | solution.py:763
  64.1 10.7 %all_to_all.11 = bf16[8,96,128]{2,1,0:T(8,128)(2,1)S(1)} all-to-all(bf16[8,96,128]{2,1,0:T(8,128)(2,1)S(1)} %broadcast_in_dim.12), channel_id=1, replica_groups=mesh['tile'=8,'chan'=4] {'tile'}, dimensions={0} | all-to-all | bytes 393216 | tf_op jit(solution)/shard_map/all_to_all | solution.py:763
  74.8 0.7 shard_map.136
  (33 shorter events, 1.7 us)
Async XLA Ops:
  0.6 37.3 %copy-start.2 = (bf16[9,32,128]{2,1,0:T(8,128)(2,1)S(1)}, bf16[9,32,128]{2,1,0:T(8,128)(2,1)}, u32[]{:S(2)}) copy-start(bf16[9,32,128]{2,1,0:T(8,128)(2,1)} %w1_ref.1) | copy-start | bytes 221188
  4.0 18.5 %collective-permute-start.4 = (bf16[63,32,128]{2,1,0:T(8,128)(2,1)}, bf16[63,32,128]{2,1,0:T(8,128)(2,1)S(1)}, u32[]{:S(2)}, u32[]{:S(2)}) collective-permute-start(bf16[63,32,128]{2,1,0:T(8,128)(2,1)} %get-tuple-element.45.pack_ref), channel_id=1, source_target_pairs={{0,2},{1,3},{2,0},{3,1},{4,6},{5,7},{6,4},{7,5},{8,10},{9,11},{10,... | collective-permute-start | bytes 1548296 | tf_op jit(solution)/shard_map/ppermute | solution.py:727
  7.0 5.3 %collective-permute-start = (bf16[1,5,32,128]{3,2,1,0:T(8,128)(2,1)}, bf16[1,5,32,128]{3,2,1,0:T(8,128)(2,1)S(1)}, u32[]{:S(2)}, u32[]{:S(2)}) collective-permute-start(bf16[1,5,32,128]{3,2,1,0:T(8,128)(2,1)} %get-tuple-element.44.rims_ref), channel_id=1, source_target_pairs={{0,16},{4,20},{8,24},{12,28},{16,0},{20,4},{24,8},{28,12},{1,17},{... | collective-permute-start | bytes 122888 | tf_op jit(solution)/shard_map/ppermute | solution.py:727
  9.6 7.6 %collective-permute-start.2 = (bf16[1,5,32,128]{3,2,1,0:T(8,128)(2,1)}, bf16[1,5,32,128]{3,2,1,0:T(8,128)(2,1)S(1)}, u32[]{:S(2)}, u32[]{:S(2)}) collective-permute-start(bf16[1,5,32,128]{3,2,1,0:T(8,128)(2,1)} %get-tuple-element.44.rims_ref), channel_id=1, source_target_pairs={{0,8},{4,12},{8,0},{12,4},{16,24},{20,28},{24,16},{28,20},{1,9},{5... | collective-permute-start | bytes 122888 | tf_op jit(solution)/shard_map/ppermute | solution.py:727
  11.1 12.2 %collective-permute-start.3 = (bf16[63,32,128]{2,1,0:T(8,128)(2,1)}, bf16[63,32,128]{2,1,0:T(8,128)(2,1)S(1)}, u32[]{:S(2)}, u32[]{:S(2)}) collective-permute-start(bf16[63,32,128]{2,1,0:T(8,128)(2,1)} %get-tuple-element.45.pack_ref), channel_id=1, source_target_pairs={{0,1},{1,0},{2,3},{3,2},{4,5},{5,4},{6,7},{7,6},{8,9},{9,8},{10,11... | collective-permute-start | bytes 1548296 | tf_op jit(solution)/shard_map/ppermute | solution.py:727
  12.2 5.0 %collective-permute-start.1 = (bf16[1,5,32,128]{3,2,1,0:T(8,128)(2,1)S(1)}, bf16[1,5,32,128]{3,2,1,0:T(8,128)(2,1)S(1)}, u32[]{:S(2)}, u32[]{:S(2)}) collective-permute-start(bf16[1,5,32,128]{3,2,1,0:T(8,128)(2,1)S(1)} %collective-permute-done.far_ref), channel_id=1, source_target_pairs={{0,8},{4,12},{8,0},{12,4},{16,24},{20,28},{24,16},{28,20},{1,9},{5... | collective-permute-start | bytes 122888 | tf_op jit(solution)/shard_map/ppermute | solution.py:727
  13.7 1.0 %copy-start.1 = (bf16[63,32,128]{2,1,0:T(8,128)(2,1)S(1)}, bf16[63,32,128]{2,1,0:T(8,128)(2,1)}, u32[]{:S(2)}) copy-start(bf16[63,32,128]{2,1,0:T(8,128)(2,1)} %get-tuple-element.45.pack_ref) | copy-start | bytes 1548292
  14.8 0.8 %copy-start.4 = (bf16[1,5,32,128]{3,2,1,0:T(8,128)(2,1)S(1)}, bf16[1,5,32,128]{3,2,1,0:T(8,128)(2,1)}, u32[]{:S(2)}) copy-start(bf16[1,5,32,128]{3,2,1,0:T(8,128)(2,1)} %get-tuple-element.44.rims_ref) | copy-start | bytes 122884
  15.6 6.2 %collective-permute-start.5 = (bf16[2,5,32,128]{3,2,1,0:T(8,128)(2,1)S(1)}, bf16[2,5,32,128]{3,2,1,0:T(8,128)(2,1)S(1)}, u32[]{:S(2)}, u32[]{:S(2)}) collective-permute-start(bf16[2,5,32,128]{3,2,1,0:T(8,128)(2,1)S(1)} %get-tuple-element.49.refs_0_), channel_id=1, source_target_pairs={{0,4},{4,0},{8,12},{12,8},{16,20},{20,16},{24,28},{28,24},{1,5},{5... | collective-permute-start | bytes 245768 | tf_op jit(solution)/shard_map/ppermute | solution.py:727
  17.2 4.0 %collective-permute-start.6 = (bf16[1,5,32,128]{3,2,1,0:T(8,128)(2,1)S(1)}, bf16[1,5,32,128]{3,2,1,0:T(8,128)(2,1)S(1)}, u32[]{:S(2)}, u32[]{:S(2)}) collective-permute-start(bf16[1,5,32,128]{3,2,1,0:T(8,128)(2,1)S(1)} %collective-permute-done.2.refs_1_), channel_id=1, source_target_pairs={{0,4},{4,0},{8,12},{12,8},{16,20},{20,16},{24,28},{28,24},{1,5},{5... | collective-permute-start | bytes 122888 | tf_op jit(solution)/shard_map/ppermute | solution.py:727
  17.8 4.0 %collective-permute-start.7 = (bf16[1,5,32,128]{3,2,1,0:T(8,128)(2,1)S(1)}, bf16[1,5,32,128]{3,2,1,0:T(8,128)(2,1)S(1)}, u32[]{:S(2)}, u32[]{:S(2)}) collective-permute-start(bf16[1,5,32,128]{3,2,1,0:T(8,128)(2,1)S(1)} %collective-permute-done.1.refs_2_), channel_id=1, source_target_pairs={{0,4},{4,0},{8,12},{12,8},{16,20},{20,16},{24,28},{28,24},{1,5},{5... | collective-permute-start | bytes 122888 | tf_op jit(solution)/shard_map/ppermute | solution.py:727
  22.5 2.0 %collective-permute-start.8 = (bf16[63,32,128]{2,1,0:T(8,128)(2,1)S(1)}, bf16[63,32,128]{2,1,0:T(8,128)(2,1)S(1)}, u32[]{:S(2)}, u32[]{:S(2)}) collective-permute-start(bf16[63,32,128]{2,1,0:T(8,128)(2,1)S(1)} %collective-permute-done.4.refs_2_), channel_id=1, source_target_pairs={{0,1},{1,0},{2,3},{3,2},{4,5},{5,4},{6,7},{7,6},{8,9},{9,8},{10,11... | collective-permute-start | bytes 1548296 | tf_op jit(solution)/shard_map/ppermute | solution.py:727
  22.5 5.5 %collective-permute-start.10 = (bf16[13,32,128]{2,1,0:T(8,128)(2,1)S(1)}, bf16[13,32,128]{2,1,0:T(8,128)(2,1)S(1)}, u32[]{:S(2)}, u32[]{:S(2)}) collective-permute-start(bf16[13,32,128]{2,1,0:T(8,128)(2,1)S(1)} %shard_map.130.refs_0_.refs_4_), channel_id=1, source_target_pairs={{0,2},{1,3},{2,0},{3,1},{4,6},{5,7},{6,4},{7,5},{8,10},{9,11},{10,... | collective-permute-start | bytes 319496 | tf_op jit(solution)/shard_map/ppermute | solution.py:727
  23.1 5.1 %collective-permute-start.9 = (bf16[13,32,128]{2,1,0:T(8,128)(2,1)S(1)}, bf16[13,32,128]{2,1,0:T(8,128)(2,1)S(1)}, u32[]{:S(2)}, u32[]{:S(2)}) collective-permute-start(bf16[13,32,128]{2,1,0:T(8,128)(2,1)S(1)} %shard_map.130.refs_0_.refs_4_), channel_id=1, source_target_pairs={{0,1},{1,0},{2,3},{3,2},{4,5},{5,4},{6,7},{7,6},{8,9},{9,8},{10,11... | collective-permute-start | bytes 319496 | tf_op jit(solution)/shard_map/ppermute | solution.py:727
  28.0 16.0 %copy-start = (bf16[512,1024]{1,0:T(8,128)(2,1)S(1)}, bf16[512,1024]{1,0:T(8,128)(2,1)}, u32[]{:S(2)}) copy-start(bf16[512,1024]{1,0:T(8,128)(2,1)} %constant.21.clone.m_hbm.m_ref) | copy-start | bytes 3145732
  28.0 16.0 %copy-start.3 = (bf16[32,4096]{1,0:T(8,128)(2,1)S(1)}, bf16[32,4096]{1,0:T(8,128)(2,1)}, u32[]{:S(2)}) copy-start(bf16[32,4096]{1,0:T(8,128)(2,1)} %get-tuple-element.71.og_ref) | copy-start | bytes 786436
  28.1 1.4 %collective-permute-start.11 = (bf16[13,32,128]{2,1,0:T(8,128)(2,1)S(1)}, bf16[13,32,128]{2,1,0:T(8,128)(2,1)S(1)}, u32[]{:S(2)}, u32[]{:S(2)}) collective-permute-start(bf16[13,32,128]{2,1,0:T(8,128)(2,1)S(1)} %collective-permute-done.10.refs_2_.refs_6_), channel_id=1, source_target_pairs={{0,1},{1,0},{2,3},{3,2},{4,5},{5,4},{6,7},{7,6},{8,9},{9,8},{10,11... | collective-permute-start | bytes 319496 | tf_op jit(solution)/shard_map/ppermute | solution.py:727
  32.1 9.5 %collective-permute-start.12 = (bf16[1,256,128]{2,1,0:T(8,128)(2,1)S(1)}, bf16[1,256,128]{2,1,0:T(8,128)(2,1)S(1)}, u32[]{:S(2)}, u32[]{:S(2)}) collective-permute-start(bf16[1,256,128]{2,1,0:T(8,128)(2,1)S(1)} %get-tuple-element.62.refs_8_), channel_id=1, source_target_pairs={{0,28},{1,25},{2,30},{3,27},{4,24},{5,29},{6,26},{7,31},{8,20},{9,... | collective-permute-start | bytes 196616 | tf_op jit(solution)/shard_map/ppermute | solution.py:756
  35.9 6.2 %collective-permute-start.13 = (bf16[1,256,128]{2,1,0:T(8,128)(2,1)S(1)}, bf16[1,256,128]{2,1,0:T(8,128)(2,1)S(1)}, u32[]{:S(2)}, u32[]{:S(2)}) collective-permute-start(bf16[1,256,128]{2,1,0:T(8,128)(2,1)S(1)} %get-tuple-element.62.refs_8_), channel_id=1, source_target_pairs={{0,16},{1,21},{2,18},{3,23},{4,20},{5,17},{6,22},{7,19},{8,24},{9,... | collective-permute-start | bytes 196616 | tf_op jit(solution)/shard_map/ppermute | solution.py:756
  35.9 6.2 %collective-permute-start.14 = (bf16[1,256,128]{2,1,0:T(8,128)(2,1)S(1)}, bf16[1,256,128]{2,1,0:T(8,128)(2,1)S(1)}, u32[]{:S(2)}, u32[]{:S(2)}) collective-permute-start(bf16[1,256,128]{2,1,0:T(8,128)(2,1)S(1)} %get-tuple-element.62.refs_8_), channel_id=1, source_target_pairs={{0,8},{1,13},{2,10},{3,15},{4,12},{5,9},{6,14},{7,11},{8,0},{9,5},... | collective-permute-start | bytes 196616 | tf_op jit(solution)/shard_map/ppermute | solution.py:756
  37.4 4.1 %collective-permute-start.15 = (bf16[1,128,128]{2,1,0:T(8,128)(2,1)S(1)}, bf16[1,128,128]{2,1,0:T(8,128)(2,1)S(1)}, u32[]{:S(2)}, u32[]{:S(2)}) collective-permute-start(bf16[1,128,128]{2,1,0:T(8,128)(2,1)S(1)} %get-tuple-element.63), channel_id=1, source_target_pairs={{0,4},{4,0},{8,12},{12,8},{16,20},{20,16},{24,28},{28,24},{1,5},{5... | collective-permute-start | bytes 98312 | tf_op jit(solution)/shard_map/ppermute | solution.py:727
  42.1 1.9 %collective-permute-start.16 = (bf16[1,256,128]{2,1,0:T(8,128)(2,1)S(1)}, bf16[1,256,128]{2,1,0:T(8,128)(2,1)S(1)}, u32[]{:S(2)}, u32[]{:S(2)}) collective-permute-start(bf16[1,256,128]{2,1,0:T(8,128)(2,1)S(1)} %collective-permute-done.12.refs_9_), channel_id=1, source_target_pairs={{0,1},{1,0},{2,3},{3,2},{4,5},{5,4},{6,7},{7,6},{8,9},{9,8},{10,11... | collective-permute-start | bytes 196616 | tf_op jit(solution)/shard_map/ppermute | solution.py:727
  42.2 1.8 %collective-permute-start.17 = (bf16[1,256,128]{2,1,0:T(8,128)(2,1)S(1)}, bf16[1,256,128]{2,1,0:T(8,128)(2,1)S(1)}, u32[]{:S(2)}, u32[]{:S(2)}) collective-permute-start(bf16[1,256,128]{2,1,0:T(8,128)(2,1)S(1)} %collective-permute-done.13.refs_10_), channel_id=1, source_target_pairs={{0,1},{1,0},{2,3},{3,2},{4,5},{5,4},{6,7},{7,6},{8,9},{9,8},{10,11... | collective-permute-start | bytes 196616 | tf_op jit(solution)/shard_map/ppermute | solution.py:727
  42.6 1.4 %collective-permute-start.18 = (bf16[1,256,128]{2,1,0:T(8,128)(2,1)S(1)}, bf16[1,256,128]{2,1,0:T(8,128)(2,1)S(1)}, u32[]{:S(2)}, u32[]{:S(2)}) collective-permute-start(bf16[1,256,128]{2,1,0:T(8,128)(2,1)S(1)} %collective-permute-done.14.refs_11_), channel_id=1, source_target_pairs={{0,1},{1,0},{2,3},{3,2},{4,5},{5,4},{6,7},{7,6},{8,9},{9,8},{10,11... | collective-permute-start | bytes 196616 | tf_op jit(solution)/shard_map/ppermute | solution.py:727
  42.7 1.2 %collective-permute-start.19 = (bf16[1,128,128]{2,1,0:T(8,128)(2,1)S(1)}, bf16[1,128,128]{2,1,0:T(8,128)(2,1)S(1)}, u32[]{:S(2)}, u32[]{:S(2)}) collective-permute-start(bf16[1,128,128]{2,1,0:T(8,128)(2,1)S(1)} %collective-permute-done.15.refs_12_), channel_id=1, source_target_pairs={{0,1},{1,0},{2,3},{3,2},{4,5},{5,4},{6,7},{7,6},{8,9},{9,8},{10,11... | collective-permute-start | bytes 98312 | tf_op jit(solution)/shard_map/ppermute | solution.py:727

commit v2 on v0

--- a/solution.py
+++ b/solution.py
@@ -118,14 +118,37 @@
     return jnp.concatenate([ref[:, jb * BLOCK : (jb + 1) * BLOCK] for jb in range(8)], axis=0)
 
 
+def fill_table(m_ref):
+    lane = iota((16, BLOCK), 1)
+    quarter, k = (lane >> 5) & 3, lane & 31
+    sort_place = quarter * 128 + (lane >> 8) * 64 + 2 * k + ((lane >> 7) & 1)
+    turn, x, y, back = lane >> 7, (lane >> 6) & 1, (lane >> 5) & 1, 31 - k
+    rim_place = jnp.where(
+        turn == 0,
+        384 + x * 64 + 2 * k + y,
+        jnp.where(
+            turn == 1,
+            (k & 3) * 128 + y * 64 + 1 - x,
+            jnp.where(
+                turn == 2,
+                (1 - x) * 64 + 2 * back + 1 - y,
+                (back & 3) * 128 + (1 - y) * 64 + 62 + x,
+            ),
+        ),
+    )
+    place = jnp.concatenate([sort_place, rim_place], axis=1)
+    row = iota((16, 2 * BLOCK), 0)
+    for group in range(BLOCK // 16):
+        m_ref[group * 16 : (group + 1) * 16, :] = one_hot(row + group * 16 == place)
+
+
 def sort_kernel(
-    f_hbm, g_hbm, w1_hbm, wd_hbm, w2_hbm, up_hbm, m_hbm, pack_ref, rims_ref, sorted_ref, pack2_ref, f_ref, g_ref, m_ref, sems
+    f_hbm, g_hbm, w1_hbm, wd_hbm, w2_hbm, up_hbm, pack_ref, rims_ref, sorted_ref, pack2_ref, f_ref, g_ref, m_ref, sems
 ):
     count = f_ref.shape[0]
     started = fetch(
         [
             (f_hbm, f_ref),
-            (m_hbm, m_ref),
             (g_hbm, g_ref),
             (w1_hbm, pack_ref.at[32:41]),
             (wd_hbm, pack_ref.at[41:45]),
@@ -151,22 +174,22 @@
             rims = rims + jnp.where(wanted == jb, parts[jb][:, BLOCK:], 0.0)
         return [[part[:, ph * 128 : (ph + 1) * 128] for ph in range(4)] for part in parts], rims.astype(BF16)
 
+    fill_table(m_ref)
     started[0].wait()
-    started[1].wait()
     pieces, rims = moved(f_ref)
     for turn_index in range(4):
         rims_ref[0, turn_index] = rims[:, turn_index * 128 : (turn_index + 1) * 128]
     for jb in range(8):
         for ph in range(4):
             pack_ref[ph * 8 + jb] = pieces[jb][ph].astype(BF16)
-    started[2].wait()
+    started[1].wait()
     pieces, rims = moved(g_ref)
     rims_ref[0, 4] = mm(rims, pooling).astype(BF16)
     for jb in range(8):
         for ph in range(4):
             sorted_ref[:, ph * CELLS + jb * 128 : ph * CELLS + (jb + 1) * 128] = pieces[jb][ph].astype(BF16)
         pack2_ref[jb] = ((pieces[jb][0] + pieces[jb][1]) + (pieces[jb][2] + pieces[jb][3])).astype(BF16)
-    for copy in started[3:]:
+    for copy in started[2:]:
         copy.wait()
 
 
@@ -653,7 +676,7 @@
         ],
         axis=0,
     ).astype(BF16)
-    natural = mm_nt(stack, m_ref[:, 0:BLOCK]).astype(BF16)
+    natural = mm_nt(stack, m_ref[...]).astype(BF16)
     for jb in range(8):
         out_ref[:, jb * BLOCK : (jb + 1) * BLOCK] = natural[jb * own : (jb + 1) * own]
 
@@ -700,25 +723,12 @@
 
 
 def sort_matrix():
-    table = np.zeros((BLOCK, 2 * BLOCK), np.float32)
-
-    def lane(a, b, q, k):
-        return q * 128 + a * 64 + 2 * k + b
-
+    table = np.zeros((BLOCK, BLOCK), np.float32)
     for a in range(2):
         for b in range(2):
             for q in range(4):
                 for k in range(HALF):
-                    table[lane(a, b, q, k), (2 * a + b) * 128 + q * HALF + k] = 1
-    for x in range(2):
-        for y in range(2):
-            for j in range(HALF):
-                spot = BLOCK + (2 * x + y) * HALF + j
-                back = HALF - 1 - j
-                table[lane(x, y, 3, j), spot] = 1
-                table[lane(y, 1 - x, j % 4, 0), spot + 128] = 1
-                table[lane(1 - x, 1 - y, 0, back), spot + 256] = 1
-                table[lane(1 - y, x, back % 4, HALF - 1), spot + 384] = 1
+                    table[q * 128 + a * 64 + 2 * k + b, (2 * a + b) * 128 + q * HALF + k] = 1
     return jnp.asarray(table, BF16)
 
 
@@ -795,14 +805,13 @@
         down_weight,
         conv2_weight,
         up_weight,
-        matrix,
-        far=range(7),
+        far=range(6),
         room=60,
         scratch=[
             pltpu.VMEM((own, 4 * CELLS), BF16),
             pltpu.VMEM((own, 4 * CELLS), BF16),
             pltpu.VMEM((BLOCK, 2 * BLOCK), BF16),
-            pltpu.SemaphoreType.DMA((7,)),
+            pltpu.SemaphoreType.DMA((6,)),
         ],
     )
     pack_far = paired(pack, "chan", half)

time: 75.4 us -> 75 us (level)
  no operation moved by 1% of the time
where the time goes in v2:
time: 75 us; the launch traced here: 74.7 us
  blocking collectives  23.5 us (31%)
  starting transfers between devices  22.3 us (30%)
  Pallas kernels  21 us (28%)
  waiting for transfers between devices  3.87 us (5%)
  local copies, waits for them, and re-layouts  2.51 us (3%)
  between operations  0.79 us (1%)
    all_to_all x2, blocking collectives, swap(): return lax.all_to_all(values, 'tile', split_axis=0, concat_axis=0)  23.5 us
    pallas_call x9, Pallas kernels, call(): pl.pallas_call(kernel, out_shape=outs, in_specs=specs, out_specs=[vmem] *...  21 us
    ppermute x20, starting transfers between devices, paired(): return lax.ppermute(values, axis, [(i, i ^ bit) for i in range(count)])  17.2 us
    ppermute x3, starting transfers between devices, copies(): got.append(lax.ppermute(block, ('tile', 'chan'), perm))  5.1 us
    ppermute x20, waiting for transfers between devices, paired(): return lax.ppermute(values, axis, [(i, i ^ bit) for i in range(count)])  3.35 us
    unnamed x12, local copies, waits for them, and re-layouts  1.79 us
  transfers between devices with their start and end apart: 23, of which 7 were waited for; matrix products, arithmetic and copies ran while one was open for 2% of the time, Pallas kernels for 13%

profile of v2, /device:TPU:0, one launch (start us, length us, event | category | flops | bytes accessed | tf_op | source)
XLA Modules:
  0.0 74.7 jit_solution(7169383935136369865)
XLA Ops:
  0.6 2.9 %shard_map.128 = (bf16[45,32,128]{2,1,0:T(8,128)(2,1)}, bf16[1,5,32,128]{3,2,1,0:T(8,128)(2,1)}, bf16[32,4096]{1,0:T(8,128)(2,1)}, bf16[18,32,128]{2,1,0:T(8,128)(2,1)}) custom-call(bf16[32,4096]{1,0:T(8,128)(2,1)} %f_hbm.1, bf16[32,4096]{1,0:T(8,128)(2,1)} %g_hbm.1, bf16[9,32,128]{2,1,0:T(8,128)(2,1)} %w1_ref.1, bf16[4,32,128]{2,1,0:T(8,128)(2,1)} %wd_hbm.1, ...), custom_call_target="tpu_custom_call" | custom-call | tf_op jit(solution)/shard_map/pallas_call | solution.py:710
  3.6 4.1 %collective-permute-start = (bf16[1,5,32,128]{3,2,1,0:T(8,128)(2,1)}, bf16[1,5,32,128]{3,2,1,0:T(8,128)(2,1)S(1)}, u32[]{:S(2)}, u32[]{:S(2)}) collective-permute-start(bf16[1,5,32,128]{3,2,1,0:T(8,128)(2,1)} %get-tuple-element.51.rims_ref), channel_id=1, source_target_pairs={{0,16},{4,20},{8,24},{12,28},{16,0},{20,4},{24,8},{28,12},{1,17},{... | collective-permute-start | bytes 122888 | tf_op jit(solution)/shard_map/ppermute | solution.py:737
  7.7 1.5 %collective-permute-start.4 = (bf16[45,32,128]{2,1,0:T(8,128)(2,1)}, bf16[45,32,128]{2,1,0:T(8,128)(2,1)S(1)}, u32[]{:S(2)}, u32[]{:S(2)}) collective-permute-start(bf16[45,32,128]{2,1,0:T(8,128)(2,1)} %get-tuple-element.52.pack_ref), channel_id=1, source_target_pairs={{0,2},{1,3},{2,0},{3,1},{4,6},{5,7},{6,4},{7,5},{8,10},{9,11},{10,... | collective-permute-start | bytes 1105928 | tf_op jit(solution)/shard_map/ppermute | solution.py:737
  9.2 1.6 %collective-permute-start.2 = (bf16[1,5,32,128]{3,2,1,0:T(8,128)(2,1)}, bf16[1,5,32,128]{3,2,1,0:T(8,128)(2,1)S(1)}, u32[]{:S(2)}, u32[]{:S(2)}) collective-permute-start(bf16[1,5,32,128]{3,2,1,0:T(8,128)(2,1)} %get-tuple-element.51.rims_ref), channel_id=1, source_target_pairs={{0,8},{4,12},{8,0},{12,4},{16,24},{20,28},{24,16},{28,20},{1,9},{5... | collective-permute-start | bytes 122888 | tf_op jit(solution)/shard_map/ppermute | solution.py:737
  10.8 1.2 %collective-permute-start.1 = (bf16[1,5,32,128]{3,2,1,0:T(8,128)(2,1)S(1)}, bf16[1,5,32,128]{3,2,1,0:T(8,128)(2,1)S(1)}, u32[]{:S(2)}, u32[]{:S(2)}) collective-permute-start(bf16[1,5,32,128]{3,2,1,0:T(8,128)(2,1)S(1)} %collective-permute-done.far_ref), channel_id=1, source_target_pairs={{0,8},{4,12},{8,0},{12,4},{16,24},{20,28},{24,16},{28,20},{1,9},{5... | collective-permute-start | bytes 122888 | tf_op jit(solution)/shard_map/ppermute | solution.py:737
  12.0 1.0 %copy-done.1 = bf16[45,32,128]{2,1,0:T(8,128)(2,1)S(1)} copy-done((bf16[45,32,128]{2,1,0:T(8,128)(2,1)S(1)}, bf16[45,32,128]{2,1,0:T(8,128)(2,1)}, u32[]{:S(2)}) %copy-start.1) | copy-done | bytes 368664
  13.0 0.8 %copy-done.5 = bf16[1,5,32,128]{3,2,1,0:T(8,128)(2,1)S(1)} copy-done((bf16[1,5,32,128]{3,2,1,0:T(8,128)(2,1)S(1)}, bf16[1,5,32,128]{3,2,1,0:T(8,128)(2,1)}, u32[]{:S(2)}) %copy-start.5) | copy-done | bytes 40984
  13.8 1.6 %collective-permute-start.5 = (bf16[2,5,32,128]{3,2,1,0:T(8,128)(2,1)S(1)}, bf16[2,5,32,128]{3,2,1,0:T(8,128)(2,1)S(1)}, u32[]{:S(2)}, u32[]{:S(2)}) collective-permute-start(bf16[2,5,32,128]{3,2,1,0:T(8,128)(2,1)S(1)} %get-tuple-element.57.refs_0_), channel_id=1, source_target_pairs={{0,4},{4,0},{8,12},{12,8},{16,20},{20,16},{24,28},{28,24},{1,5},{5... | collective-permute-start | bytes 245768 | tf_op jit(solution)/shard_map/ppermute | solution.py:737
  15.4 0.9 %collective-permute-start.6 = (bf16[1,5,32,128]{3,2,1,0:T(8,128)(2,1)S(1)}, bf16[1,5,32,128]{3,2,1,0:T(8,128)(2,1)S(1)}, u32[]{:S(2)}, u32[]{:S(2)}) collective-permute-start(bf16[1,5,32,128]{3,2,1,0:T(8,128)(2,1)S(1)} %collective-permute-done.2.refs_1_), channel_id=1, source_target_pairs={{0,4},{4,0},{8,12},{12,8},{16,20},{20,16},{24,28},{28,24},{1,5},{5... | collective-permute-start | bytes 122888 | tf_op jit(solution)/shard_map/ppermute | solution.py:737
  16.3 1.2 %collective-permute-start.7 = (bf16[1,5,32,128]{3,2,1,0:T(8,128)(2,1)S(1)}, bf16[1,5,32,128]{3,2,1,0:T(8,128)(2,1)S(1)}, u32[]{:S(2)}, u32[]{:S(2)}) collective-permute-start(bf16[1,5,32,128]{3,2,1,0:T(8,128)(2,1)S(1)} %collective-permute-done.1.refs_2_), channel_id=1, source_target_pairs={{0,4},{4,0},{8,12},{12,8},{16,20},{20,16},{24,28},{28,24},{1,5},{5... | collective-permute-start | bytes 122888 | tf_op jit(solution)/shard_map/ppermute | solution.py:737
  17.4 0.7 copy.15
  18.1 0.7 fusion.3.codes_ref
  18.8 0.6 collective-permute-done.6.refs_4_
  19.4 0.9 %collective-permute-done.7.refs_5_ = bf16[1,5,32,128]{3,2,1,0:T(8,128)(2,1)S(1)} collective-permute-done((bf16[1,5,32,128]{3,2,1,0:T(8,128)(2,1)S(1)}, bf16[1,5,32,128]{3,2,1,0:T(8,128)(2,1)S(1)}, u32[]{:S(2)}, u32[]{:S(2)}) %collective-permute-start.7) | collective-permute-done | bytes 40992 | tf_op jit(solution)/shard_map/ppermute | solution.py:737
  20.3 0.7 shard_map.130.refs_0_.refs_4_
  21.1 1.3 %collective-permute-start.10 = (bf16[13,32,128]{2,1,0:T(8,128)(2,1)S(1)}, bf16[13,32,128]{2,1,0:T(8,128)(2,1)S(1)}, u32[]{:S(2)}, u32[]{:S(2)}) collective-permute-start(bf16[13,32,128]{2,1,0:T(8,128)(2,1)S(1)} %shard_map.130.refs_0_.refs_4_), channel_id=1, source_target_pairs={{0,2},{1,3},{2,0},{3,1},{4,6},{5,7},{6,4},{7,5},{8,10},{9,11},{10,... | collective-permute-start | bytes 319496 | tf_op jit(solution)/shard_map/ppermute | solution.py:737
  22.8 3.6 %shard_map.131 = (bf16[4,1152,384]{2,1,0:T(8,128)(2,1)S(1)}, f32[4,1024,128]{2,1,0:T(8,128)S(1)}, bf16[1152,128]{1,0:T(8,128)(2,1)S(1)}, bf16[512,128]{1,0:T(8,128)(2,1)S(1)}) custom-call(s32[4]{0:T(128)S(1)} %pad_add_fusion.where_ref, bf16[45,32,128]{2,1,0:T(8,128)(2,1)S(1)} %get-tuple-element.56.refs_0_, ...), custom_call_target="tpu_custom_call" | custom-call | tf_op jit(solution)/shard_map/pallas_call | solution.py:710
  26.6 0.4 collective-permute-start.9
  27.1 1.3 %collective-permute-start.17 = (bf16[18,32,128]{2,1,0:T(8,128)(2,1)}, bf16[18,32,128]{2,1,0:T(8,128)(2,1)S(1)}, u32[]{:S(2)}, u32[]{:S(2)}) collective-permute-start(bf16[18,32,128]{2,1,0:T(8,128)(2,1)} %get-tuple-element.73.refs_0_), channel_id=1, source_target_pairs={{0,2},{1,3},{2,0},{3,1},{4,6},{5,7},{6,4},{7,5},{8,10},{9,11},{10,... | collective-permute-start | bytes 442376 | tf_op jit(solution)/shard_map/ppermute | solution.py:737
  28.4 2.6 %shard_map.132 = (bf16[4,1024,128]{2,1,0:T(8,128)(2,1)S(1)}, f32[1024,128]{1,0:T(8,128)S(1)}, bf16[1024,128]{1,0:T(8,128)(2,1)S(1)}, bf16[1,256,128]{2,1,0:T(8,1...) custom-call(s32[4]{0:T(128)S(1)} %pad_add_fusion.where_ref, ...), custom_call_target="tpu_custom_call" | custom-call | tf_op jit(solution)/shard_map/pallas_call | solution.py:710
  31.0 3.7 %collective-permute-start.13 = (bf16[1,256,128]{2,1,0:T(8,128)(2,1)S(1)}, bf16[1,256,128]{2,1,0:T(8,128)(2,1)S(1)}, u32[]{:S(2)}, u32[]{:S(2)}) collective-permute-start(bf16[1,256,128]{2,1,0:T(8,128)(2,1)S(1)} %get-tuple-element.74.refs_8_), channel_id=1, source_target_pairs={{0,28},{1,25},{2,30},{3,27},{4,24},{5,29},{6,26},{7,31},{8,20},{9,... | collective-permute-start | bytes 196616 | tf_op jit(solution)/shard_map/ppermute | solution.py:766
  34.7 1.4 %collective-permute-start.15 = (bf16[1,256,128]{2,1,0:T(8,128)(2,1)S(1)}, bf16[1,256,128]{2,1,0:T(8,128)(2,1)S(1)}, u32[]{:S(2)}, u32[]{:S(2)}) collective-permute-start(bf16[1,256,128]{2,1,0:T(8,128)(2,1)S(1)} %get-tuple-element.74.refs_8_), channel_id=1, source_target_pairs={{0,8},{1,13},{2,10},{3,15},{4,12},{5,9},{6,14},{7,11},{8,0},{9,5},... | collective-permute-start | bytes 196616 | tf_op jit(solution)/shard_map/ppermute | solution.py:766
  36.1 0.8 %collective-permute-start.16 = (bf16[1,128,128]{2,1,0:T(8,128)(2,1)S(1)}, bf16[1,128,128]{2,1,0:T(8,128)(2,1)S(1)}, u32[]{:S(2)}, u32[]{:S(2)}) collective-permute-start(bf16[1,128,128]{2,1,0:T(8,128)(2,1)S(1)} %get-tuple-element.75), channel_id=1, source_target_pairs={{0,4},{4,0},{8,12},{12,8},{16,20},{20,16},{24,28},{28,24},{1,5},{5... | collective-permute-start | bytes 98312 | tf_op jit(solution)/shard_map/ppermute | solution.py:737
  37.0 3.0 %shard_map.133 = (bf16[32,4096]{1,0:T(8,128)(2,1)S(1)}, f32[32,4096]{1,0:T(8,128)S(1)}, bf16[4,1152,384]{2,1,0:T(8,128)(2,1)S(1)}) custom-call(bf16[9,32,128]{2,1,0:T(8,128)(2,1)S(1)} %copy-done.2, f32[5,128,128]{2,1,0:T(8,128)S(1)} %get-tuple-element.76.ring, bf16[4,1152,384]{2,1,0:T(8,128)(2,1)S(1)} %get-tuple-element.77.x3_in), custom_call_target="tpu_custom_call", output_to_operand_aliasing={{2}: (2, {})} | custom-call | tf_op jit(solution)/shard_map/pallas_call | solution.py:710
  40.3 0.5 collective-permute-done.14.refs_10_
  40.9 0.4 collective-permute-start.19
  41.4 0.4 collective-permute-start.21
  41.9 1.1 %collective-permute-done.22.refs_16_ = bf16[1,128,128]{2,1,0:T(8,128)(2,1)S(1)} collective-permute-done((bf16[1,128,128]{2,1,0:T(8,128)(2,1)S(1)}, bf16[1,128,128]{2,1,0:T(8,128)(2,1)S(1)}, u32[]{:S(2)}, u32[]{:S(2)}) %collective-permute-start.22) | collective-permute-done | bytes 32800 | tf_op jit(solution)/shard_map/ppermute | solution.py:737
  43.1 7.3 %shard_map.134 = (bf16[32,4096]{1,0:T(8,128)(2,1)}, bf16[768,128]{1,0:T(8,128)(2,1)S(1)}) custom-call(s32[8,8]{1,0:T(8,128)S(1)} %fusion.3.codes_ref, s32[4]{0:T(128)S(1)} %pad_add_fusion.where_ref, bf16[1024,128]{1,0:T(8,128)(2,1)S(1)} %get-tuple-element.68.act2_ref, f32[1024,128]{1,0:T(8,128)S(1)} %get-tuple-element.69.slope2_ref, ...), custom_call_target="tpu_custom_call" | custom-call | tf_op jit(solution)/shard_map/pallas_call | solution.py:710
  50.4 12.7 %all_to_all.10.in_ref = bf16[8,96,128]{2,1,0:T(8,128)(2,1)S(1)} all-to-all(bf16[8,96,128]{2,1,0:T(8,128)(2,1)S(1)} %bitcast.19), channel_id=1, replica_groups=mesh['tile'=8,'chan'=4] {'tile'}, dimensions={0} | all-to-all | bytes 393216 | tf_op jit(solution)/shard_map/all_to_all | solution.py:773
  63.2 10.7 %all_to_all.11 = bf16[8,96,128]{2,1,0:T(8,128)(2,1)S(1)} all-to-all(bf16[8,96,128]{2,1,0:T(8,128)(2,1)S(1)} %broadcast_in_dim.12), channel_id=1, replica_groups=mesh['tile'=8,'chan'=4] {'tile'}, dimensions={0} | all-to-all | bytes 393216 | tf_op jit(solution)/shard_map/all_to_all | solution.py:773
  73.9 0.7 %shard_map.136 = (f32[9,32,128]{2,1,0:T(8,128)}, f32[4,32,128]{2,1,0:T(8,128)}, f32[9,32,128]{2,1,0:T(8,128)}, f32[32,128]{1,0:T(8,128)}) custom-call(bf16[768,128]{1,0:T(8,128)(2,1)S(1)} %bitcast.18), custom_call_target="tpu_custom_call" | custom-call | tf_op jit(solution)/shard_map/pallas_call | solution.py:710
  (41 shorter events, 1.5 us)
Async XLA Ops:
  0.6 36.3 %copy-start.2 = (bf16[9,32,128]{2,1,0:T(8,128)(2,1)S(1)}, bf16[9,32,128]{2,1,0:T(8,128)(2,1)}, u32[]{:S(2)}) copy-start(bf16[9,32,128]{2,1,0:T(8,128)(2,1)} %w1_ref.1) | copy-start | bytes 221188
  3.6 7.2 %collective-permute-start = (bf16[1,5,32,128]{3,2,1,0:T(8,128)(2,1)}, bf16[1,5,32,128]{3,2,1,0:T(8,128)(2,1)S(1)}, u32[]{:S(2)}, u32[]{:S(2)}) collective-permute-start(bf16[1,5,32,128]{3,2,1,0:T(8,128)(2,1)} %get-tuple-element.51.rims_ref), channel_id=1, source_target_pairs={{0,16},{4,20},{8,24},{12,28},{16,0},{20,4},{24,8},{28,12},{1,17},{... | collective-permute-start | bytes 122888 | tf_op jit(solution)/shard_map/ppermute | solution.py:737
  7.7 13.3 %collective-permute-start.4 = (bf16[45,32,128]{2,1,0:T(8,128)(2,1)}, bf16[45,32,128]{2,1,0:T(8,128)(2,1)S(1)}, u32[]{:S(2)}, u32[]{:S(2)}) collective-permute-start(bf16[45,32,128]{2,1,0:T(8,128)(2,1)} %get-tuple-element.52.pack_ref), channel_id=1, source_target_pairs={{0,2},{1,3},{2,0},{3,1},{4,6},{5,7},{6,4},{7,5},{8,10},{9,11},{10,... | collective-permute-start | bytes 1105928 | tf_op jit(solution)/shard_map/ppermute | solution.py:737
  9.2 6.2 %collective-permute-start.2 = (bf16[1,5,32,128]{3,2,1,0:T(8,128)(2,1)}, bf16[1,5,32,128]{3,2,1,0:T(8,128)(2,1)S(1)}, u32[]{:S(2)}, u32[]{:S(2)}) collective-permute-start(bf16[1,5,32,128]{3,2,1,0:T(8,128)(2,1)} %get-tuple-element.51.rims_ref), channel_id=1, source_target_pairs={{0,8},{4,12},{8,0},{12,4},{16,24},{20,28},{24,16},{28,20},{1,9},{5... | collective-permute-start | bytes 122888 | tf_op jit(solution)/shard_map/ppermute | solution.py:737
  10.8 11.7 %collective-permute-start.3 = (bf16[45,32,128]{2,1,0:T(8,128)(2,1)}, bf16[45,32,128]{2,1,0:T(8,128)(2,1)S(1)}, u32[]{:S(2)}, u32[]{:S(2)}) collective-permute-start(bf16[45,32,128]{2,1,0:T(8,128)(2,1)} %get-tuple-element.52.pack_ref), channel_id=1, source_target_pairs={{0,1},{1,0},{2,3},{3,2},{4,5},{5,4},{6,7},{7,6},{8,9},{9,8},{10,11... | collective-permute-start | bytes 1105928 | tf_op jit(solution)/shard_map/ppermute | solution.py:737
  10.8 4.7 %collective-permute-start.1 = (bf16[1,5,32,128]{3,2,1,0:T(8,128)(2,1)S(1)}, bf16[1,5,32,128]{3,2,1,0:T(8,128)(2,1)S(1)}, u32[]{:S(2)}, u32[]{:S(2)}) collective-permute-start(bf16[1,5,32,128]{3,2,1,0:T(8,128)(2,1)S(1)} %collective-permute-done.far_ref), channel_id=1, source_target_pairs={{0,8},{4,12},{8,0},{12,4},{16,24},{20,28},{24,16},{28,20},{1,9},{5... | collective-permute-start | bytes 122888 | tf_op jit(solution)/shard_map/ppermute | solution.py:737
  12.0 1.0 %copy-start.1 = (bf16[45,32,128]{2,1,0:T(8,128)(2,1)S(1)}, bf16[45,32,128]{2,1,0:T(8,128)(2,1)}, u32[]{:S(2)}) copy-start(bf16[45,32,128]{2,1,0:T(8,128)(2,1)} %get-tuple-element.52.pack_ref) | copy-start | bytes 1105924
  13.0 0.8 %copy-start.5 = (bf16[1,5,32,128]{3,2,1,0:T(8,128)(2,1)S(1)}, bf16[1,5,32,128]{3,2,1,0:T(8,128)(2,1)}, u32[]{:S(2)}) copy-start(bf16[1,5,32,128]{3,2,1,0:T(8,128)(2,1)} %get-tuple-element.51.rims_ref) | copy-start | bytes 122884
  13.8 6.5 %collective-permute-start.5 = (bf16[2,5,32,128]{3,2,1,0:T(8,128)(2,1)S(1)}, bf16[2,5,32,128]{3,2,1,0:T(8,128)(2,1)S(1)}, u32[]{:S(2)}, u32[]{:S(2)}) collective-permute-start(bf16[2,5,32,128]{3,2,1,0:T(8,128)(2,1)S(1)} %get-tuple-element.57.refs_0_), channel_id=1, source_target_pairs={{0,4},{4,0},{8,12},{12,8},{16,20},{20,16},{24,28},{28,24},{1,5},{5... | collective-permute-start | bytes 245768 | tf_op jit(solution)/shard_map/ppermute | solution.py:737
  15.4 4.0 %collective-permute-start.6 = (bf16[1,5,32,128]{3,2,1,0:T(8,128)(2,1)S(1)}, bf16[1,5,32,128]{3,2,1,0:T(8,128)(2,1)S(1)}, u32[]{:S(2)}, u32[]{:S(2)}) collective-permute-start(bf16[1,5,32,128]{3,2,1,0:T(8,128)(2,1)S(1)} %collective-permute-done.2.refs_1_), channel_id=1, source_target_pairs={{0,4},{4,0},{8,12},{12,8},{16,20},{20,16},{24,28},{28,24},{1,5},{5... | collective-permute-start | bytes 122888 | tf_op jit(solution)/shard_map/ppermute | solution.py:737
  16.3 4.0 %collective-permute-start.7 = (bf16[1,5,32,128]{3,2,1,0:T(8,128)(2,1)S(1)}, bf16[1,5,32,128]{3,2,1,0:T(8,128)(2,1)S(1)}, u32[]{:S(2)}, u32[]{:S(2)}) collective-permute-start(bf16[1,5,32,128]{3,2,1,0:T(8,128)(2,1)S(1)} %collective-permute-done.1.refs_2_), channel_id=1, source_target_pairs={{0,4},{4,0},{8,12},{12,8},{16,20},{20,16},{24,28},{28,24},{1,5},{5... | collective-permute-start | bytes 122888 | tf_op jit(solution)/shard_map/ppermute | solution.py:737
  21.0 1.8 %collective-permute-start.8 = (bf16[45,32,128]{2,1,0:T(8,128)(2,1)S(1)}, bf16[45,32,128]{2,1,0:T(8,128)(2,1)S(1)}, u32[]{:S(2)}, u32[]{:S(2)}) collective-permute-start(bf16[45,32,128]{2,1,0:T(8,128)(2,1)S(1)} %collective-permute-done.4.refs_2_), channel_id=1, source_target_pairs={{0,1},{1,0},{2,3},{3,2},{4,5},{5,4},{6,7},{7,6},{8,9},{9,8},{10,11... | collective-permute-start | bytes 1105928 | tf_op jit(solution)/shard_map/ppermute | solution.py:737
  21.1 5.4 %collective-permute-start.10 = (bf16[13,32,128]{2,1,0:T(8,128)(2,1)S(1)}, bf16[13,32,128]{2,1,0:T(8,128)(2,1)S(1)}, u32[]{:S(2)}, u32[]{:S(2)}) collective-permute-start(bf16[13,32,128]{2,1,0:T(8,128)(2,1)S(1)} %shard_map.130.refs_0_.refs_4_), channel_id=1, source_target_pairs={{0,2},{1,3},{2,0},{3,1},{4,6},{5,7},{6,4},{7,5},{8,10},{9,11},{10,... | collective-permute-start | bytes 319496 | tf_op jit(solution)/shard_map/ppermute | solution.py:737
  26.4 16.7 %copy-start = (bf16[512,512]{1,0:T(8,128)(2,1)S(1)}, bf16[512,512]{1,0:T(8,128)(2,1)}, u32[]{:S(2)}) copy-start(bf16[512,512]{1,0:T(8,128)(2,1)} %constant.21.clone.m_ref) | copy-start | bytes 1572868
  26.4 16.7 %copy-start.3 = (bf16[32,4096]{1,0:T(8,128)(2,1)S(1)}, bf16[32,4096]{1,0:T(8,128)(2,1)}, u32[]{:S(2)}) copy-start(bf16[32,4096]{1,0:T(8,128)(2,1)} %get-tuple-element.83.og_ref) | copy-start | bytes 786436
  26.4 16.7 %copy-start.4 = (bf16[18,32,128]{2,1,0:T(8,128)(2,1)S(1)}, bf16[18,32,128]{2,1,0:T(8,128)(2,1)}, u32[]{:S(2)}) copy-start(bf16[18,32,128]{2,1,0:T(8,128)(2,1)} %get-tuple-element.73.refs_0_) | copy-start | bytes 442372
  26.5 4.6 %collective-permute-start.12 = (bf16[18,32,128]{2,1,0:T(8,128)(2,1)}, bf16[18,32,128]{2,1,0:T(8,128)(2,1)S(1)}, u32[]{:S(2)}, u32[]{:S(2)}) collective-permute-start(bf16[18,32,128]{2,1,0:T(8,128)(2,1)} %get-tuple-element.73.refs_0_), channel_id=1, source_target_pairs={{0,1},{1,0},{2,3},{3,2},{4,5},{5,4},{6,7},{7,6},{8,9},{9,8},{10,11... | collective-permute-start | bytes 442376 | tf_op jit(solution)/shard_map/ppermute | solution.py:737
  26.6 1.8 %collective-permute-start.9 = (bf16[13,32,128]{2,1,0:T(8,128)(2,1)S(1)}, bf16[13,32,128]{2,1,0:T(8,128)(2,1)S(1)}, u32[]{:S(2)}, u32[]{:S(2)}) collective-permute-start(bf16[13,32,128]{2,1,0:T(8,128)(2,1)S(1)} %shard_map.130.refs_0_.refs_4_), channel_id=1, source_target_pairs={{0,1},{1,0},{2,3},{3,2},{4,5},{5,4},{6,7},{7,6},{8,9},{9,8},{10,11... | collective-permute-start | bytes 319496 | tf_op jit(solution)/shard_map/ppermute | solution.py:737
  27.0 1.4 %collective-permute-start.11 = (bf16[13,32,128]{2,1,0:T(8,128)(2,1)S(1)}, bf16[13,32,128]{2,1,0:T(8,128)(2,1)S(1)}, u32[]{:S(2)}, u32[]{:S(2)}) collective-permute-start(bf16[13,32,128]{2,1,0:T(8,128)(2,1)S(1)} %collective-permute-done.10.refs_2_.refs_6_), channel_id=1, source_target_pairs={{0,1},{1,0},{2,3},{3,2},{4,5},{5,4},{6,7},{7,6},{8,9},{9,8},{10,11... | collective-permute-start | bytes 319496 | tf_op jit(solution)/shard_map/ppermute | solution.py:737
  27.1 12.9 %collective-permute-start.17 = (bf16[18,32,128]{2,1,0:T(8,128)(2,1)}, bf16[18,32,128]{2,1,0:T(8,128)(2,1)S(1)}, u32[]{:S(2)}, u32[]{:S(2)}) collective-permute-start(bf16[18,32,128]{2,1,0:T(8,128)(2,1)} %get-tuple-element.73.refs_0_), channel_id=1, source_target_pairs={{0,2},{1,3},{2,0},{3,1},{4,6},{5,7},{6,4},{7,5},{8,10},{9,11},{10,... | collective-permute-start | bytes 442376 | tf_op jit(solution)/shard_map/ppermute | solution.py:737
  31.0 9.3 %collective-permute-start.13 = (bf16[1,256,128]{2,1,0:T(8,128)(2,1)S(1)}, bf16[1,256,128]{2,1,0:T(8,128)(2,1)S(1)}, u32[]{:S(2)}, u32[]{:S(2)}) collective-permute-start(bf16[1,256,128]{2,1,0:T(8,128)(2,1)S(1)} %get-tuple-element.74.refs_8_), channel_id=1, source_target_pairs={{0,28},{1,25},{2,30},{3,27},{4,24},{5,29},{6,26},{7,31},{8,20},{9,... | collective-permute-start | bytes 196616 | tf_op jit(solution)/shard_map/ppermute | solution.py:766
  34.7 6.1 %collective-permute-start.14 = (bf16[1,256,128]{2,1,0:T(8,128)(2,1)S(1)}, bf16[1,256,128]{2,1,0:T(8,128)(2,1)S(1)}, u32[]{:S(2)}, u32[]{:S(2)}) collective-permute-start(bf16[1,256,128]{2,1,0:T(8,128)(2,1)S(1)} %get-tuple-element.74.refs_8_), channel_id=1, source_target_pairs={{0,16},{1,21},{2,18},{3,23},{4,20},{5,17},{6,22},{7,19},{8,24},{9,... | collective-permute-start | bytes 196616 | tf_op jit(solution)/shard_map/ppermute | solution.py:766
  34.7 6.1 %collective-permute-start.15 = (bf16[1,256,128]{2,1,0:T(8,128)(2,1)S(1)}, bf16[1,256,128]{2,1,0:T(8,128)(2,1)S(1)}, u32[]{:S(2)}, u32[]{:S(2)}) collective-permute-start(bf16[1,256,128]{2,1,0:T(8,128)(2,1)S(1)} %get-tuple-element.74.refs_8_), channel_id=1, source_target_pairs={{0,8},{1,13},{2,10},{3,15},{4,12},{5,9},{6,14},{7,11},{8,0},{9,5},... | collective-permute-start | bytes 196616 | tf_op jit(solution)/shard_map/ppermute | solution.py:766
  36.1 4.2 %collective-permute-start.16 = (bf16[1,128,128]{2,1,0:T(8,128)(2,1)S(1)}, bf16[1,128,128]{2,1,0:T(8,128)(2,1)S(1)}, u32[]{:S(2)}, u32[]{:S(2)}) collective-permute-start(bf16[1,128,128]{2,1,0:T(8,128)(2,1)S(1)} %get-tuple-element.75), channel_id=1, source_target_pairs={{0,4},{4,0},{8,12},{12,8},{16,20},{20,16},{24,28},{28,24},{1,5},{5... | collective-permute-start | bytes 98312 | tf_op jit(solution)/shard_map/ppermute | solution.py:737
  40.8 2.2 %collective-permute-start.18 = (bf16[18,32,128]{2,1,0:T(8,128)(2,1)S(1)}, bf16[18,32,128]{2,1,0:T(8,128)(2,1)S(1)}, u32[]{:S(2)}, u32[]{:S(2)}) collective-permute-start(bf16[18,32,128]{2,1,0:T(8,128)(2,1)S(1)} %collective-permute-done.17.refs_2_), channel_id=1, source_target_pairs={{0,1},{1,0},{2,3},{3,2},{4,5},{5,4},{6,7},{7,6},{8,9},{9,8},{10,11... | collective-permute-start | bytes 442376 | tf_op jit(solution)/shard_map/ppermute | solution.py:737
  40.9 2.2 %collective-permute-start.19 = (bf16[1,256,128]{2,1,0:T(8,128)(2,1)S(1)}, bf16[1,256,128]{2,1,0:T(8,128)(2,1)S(1)}, u32[]{:S(2)}, u32[]{:S(2)}) collective-permute-start(bf16[1,256,128]{2,1,0:T(8,128)(2,1)S(1)} %collective-permute-done.13.refs_9_), channel_id=1, source_target_pairs={{0,1},{1,0},{2,3},{3,2},{4,5},{5,4},{6,7},{7,6},{8,9},{9,8},{10,11... | collective-permute-start | bytes 196616 | tf_op jit(solution)/shard_map/ppermute | solution.py:737
  41.3 1.7 %collective-permute-start.20 = (bf16[1,256,128]{2,1,0:T(8,128)(2,1)S(1)}, bf16[1,256,128]{2,1,0:T(8,128)(2,1)S(1)}, u32[]{:S(2)}, u32[]{:S(2)}) collective-permute-start(bf16[1,256,128]{2,1,0:T(8,128)(2,1)S(1)} %collective-permute-done.14.refs_10_), channel_id=1, source_target_pairs={{0,1},{1,0},{2,3},{3,2},{4,5},{5,4},{6,7},{7,6},{8,9},{9,8},{10,11... | collective-permute-start | bytes 196616 | tf_op jit(solution)/shard_map/ppermute | solution.py:737
  41.4 1.7 %collective-permute-start.21 = (bf16[1,256,128]{2,1,0:T(8,128)(2,1)S(1)}, bf16[1,256,128]{2,1,0:T(8,128)(2,1)S(1)}, u32[]{:S(2)}, u32[]{:S(2)}) collective-permute-start(bf16[1,256,128]{2,1,0:T(8,128)(2,1)S(1)} %collective-permute-done.15.refs_11_), channel_id=1, source_target_pairs={{0,1},{1,0},{2,3},{3,2},{4,5},{5,4},{6,7},{7,6},{8,9},{9,8},{10,11... | collective-permute-start | bytes 196616 | tf_op jit(solution)/shard_map/ppermute | solution.py:737
  41.9 1.2 %collective-permute-start.22 = (bf16[1,128,128]{2,1,0:T(8,128)(2,1)S(1)}, bf16[1,128,128]{2,1,0:T(8,128)(2,1)S(1)}, u32[]{:S(2)}, u32[]{:S(2)}) collective-permute-start(bf16[1,128,128]{2,1,0:T(8,128)(2,1)S(1)} %collective-permute-done.16.refs_12_), channel_id=1, source_target_pairs={{0,1},{1,0},{2,3},{3,2},{4,5},{5,4},{6,7},{7,6},{8,9},{9,8},{10,11... | collective-permute-start | bytes 98312 | tf_op jit(solution)/shard_map/ppermute | solution.py:737

commit v3 on v2

--- a/solution.py
+++ b/solution.py
@@ -737,7 +737,7 @@
     return lax.ppermute(values, axis, [(i, i ^ bit) for i in range(count)])
 
 
-FIRST, SECOND = (7, 4, 2), (6, 5, 3)
+FIRST, SECOND = (2, 4, 7), (3, 5, 6)
 
 
 def is_split():

time: 75 us -> 75.9 us (1.012)
  waiting for transfers between devices: 3.87 us -> 5.5 us
    ppermute x3, waiting for transfers between devices: 0.52 us -> 2.27 us  [copies(): got.append(lax.ppermute(block, ('tile', 'chan'), perm))]
where the time goes in v3:
time: 75.9 us; the launch traced here: 75.6 us
  blocking collectives  22.8 us (30%)
  starting transfers between devices  22.3 us (29%)
  Pallas kernels  21 us (28%)
  waiting for transfers between devices  5.5 us (7%)
  local copies, waits for them, and re-layouts  2.51 us (3%)
  between operations  0.79 us (1%)
    all_to_all x2, blocking collectives, swap(): return lax.all_to_all(values, 'tile', split_axis=0, concat_axis=0)  22.8 us
    pallas_call x9, Pallas kernels, call(): pl.pallas_call(kernel, out_shape=outs, in_specs=specs, out_specs=[vmem] *...  21 us
    ppermute x20, starting transfers between devices, paired(): return lax.ppermute(values, axis, [(i, i ^ bit) for i in range(count)])  17.1 us
    ppermute x3, starting transfers between devices, copies(): got.append(lax.ppermute(block, ('tile', 'chan'), perm))  5.18 us
    ppermute x20, waiting for transfers between devices, paired(): return lax.ppermute(values, axis, [(i, i ^ bit) for i in range(count)])  3.24 us
    ppermute x3, waiting for transfers between devices, copies(): got.append(lax.ppermute(block, ('tile', 'chan'), perm))  2.27 us
    unnamed x12, local copies, waits for them, and re-layouts  1.79 us
  transfers between devices with their start and end apart: 23, of which 7 were waited for; matrix products, arithmetic and copies ran while one was open for 2% of the time, Pallas kernels for 13%

profile of v3, /device:TPU:0, one launch (start us, length us, event | category | flops | bytes accessed | tf_op | source)
XLA Modules:
  0.0 75.6 jit_solution(6849391316022172259)
XLA Ops:
  0.6 2.9 %shard_map.128 = (bf16[45,32,128]{2,1,0:T(8,128)(2,1)}, bf16[1,5,32,128]{3,2,1,0:T(8,128)(2,1)}, bf16[32,4096]{1,0:T(8,128)(2,1)}, bf16[18,32,128]{2,1,0:T(8,128)(2,1)}) custom-call(bf16[32,4096]{1,0:T(8,128)(2,1)} %f_hbm.1, bf16[32,4096]{1,0:T(8,128)(2,1)} %g_hbm.1, bf16[9,32,128]{2,1,0:T(8,128)(2,1)} %w1_ref.1, bf16[4,32,128]{2,1,0:T(8,128)(2,1)} %wd_hbm.1, ...), custom_call_target="tpu_custom_call" | custom-call | tf_op jit(solution)/shard_map/pallas_call | solution.py:710
  3.6 4.1 %collective-permute-start = (bf16[1,5,32,128]{3,2,1,0:T(8,128)(2,1)}, bf16[1,5,32,128]{3,2,1,0:T(8,128)(2,1)S(1)}, u32[]{:S(2)}, u32[]{:S(2)}) collective-permute-start(bf16[1,5,32,128]{3,2,1,0:T(8,128)(2,1)} %get-tuple-element.51.rims_ref), channel_id=1, source_target_pairs={{0,16},{4,20},{8,24},{12,28},{16,0},{20,4},{24,8},{28,12},{1,17},{... | collective-permute-start | bytes 122888 | tf_op jit(solution)/shard_map/ppermute | solution.py:737
  7.7 1.5 %collective-permute-start.4 = (bf16[45,32,128]{2,1,0:T(8,128)(2,1)}, bf16[45,32,128]{2,1,0:T(8,128)(2,1)S(1)}, u32[]{:S(2)}, u32[]{:S(2)}) collective-permute-start(bf16[45,32,128]{2,1,0:T(8,128)(2,1)} %get-tuple-element.52.pack_ref), channel_id=1, source_target_pairs={{0,2},{1,3},{2,0},{3,1},{4,6},{5,7},{6,4},{7,5},{8,10},{9,11},{10,... | collective-permute-start | bytes 1105928 | tf_op jit(solution)/shard_map/ppermute | solution.py:737
  9.2 1.6 %collective-permute-start.2 = (bf16[1,5,32,128]{3,2,1,0:T(8,128)(2,1)}, bf16[1,5,32,128]{3,2,1,0:T(8,128)(2,1)S(1)}, u32[]{:S(2)}, u32[]{:S(2)}) collective-permute-start(bf16[1,5,32,128]{3,2,1,0:T(8,128)(2,1)} %get-tuple-element.51.rims_ref), channel_id=1, source_target_pairs={{0,8},{4,12},{8,0},{12,4},{16,24},{20,28},{24,16},{28,20},{1,9},{5... | collective-permute-start | bytes 122888 | tf_op jit(solution)/shard_map/ppermute | solution.py:737
  10.8 1.2 %collective-permute-start.1 = (bf16[1,5,32,128]{3,2,1,0:T(8,128)(2,1)S(1)}, bf16[1,5,32,128]{3,2,1,0:T(8,128)(2,1)S(1)}, u32[]{:S(2)}, u32[]{:S(2)}) collective-permute-start(bf16[1,5,32,128]{3,2,1,0:T(8,128)(2,1)S(1)} %collective-permute-done.far_ref), channel_id=1, source_target_pairs={{0,8},{4,12},{8,0},{12,4},{16,24},{20,28},{24,16},{28,20},{1,9},{5... | collective-permute-start | bytes 122888 | tf_op jit(solution)/shard_map/ppermute | solution.py:737
  12.0 1.0 %copy-done.1 = bf16[45,32,128]{2,1,0:T(8,128)(2,1)S(1)} copy-done((bf16[45,32,128]{2,1,0:T(8,128)(2,1)S(1)}, bf16[45,32,128]{2,1,0:T(8,128)(2,1)}, u32[]{:S(2)}) %copy-start.1) | copy-done | bytes 368664
  13.0 0.8 %copy-done.5 = bf16[1,5,32,128]{3,2,1,0:T(8,128)(2,1)S(1)} copy-done((bf16[1,5,32,128]{3,2,1,0:T(8,128)(2,1)S(1)}, bf16[1,5,32,128]{3,2,1,0:T(8,128)(2,1)}, u32[]{:S(2)}) %copy-start.5) | copy-done | bytes 40984
  13.8 1.6 %collective-permute-start.5 = (bf16[2,5,32,128]{3,2,1,0:T(8,128)(2,1)S(1)}, bf16[2,5,32,128]{3,2,1,0:T(8,128)(2,1)S(1)}, u32[]{:S(2)}, u32[]{:S(2)}) collective-permute-start(bf16[2,5,32,128]{3,2,1,0:T(8,128)(2,1)S(1)} %get-tuple-element.57.refs_0_), channel_id=1, source_target_pairs={{0,4},{4,0},{8,12},{12,8},{16,20},{20,16},{24,28},{28,24},{1,5},{5... | collective-permute-start | bytes 245768 | tf_op jit(solution)/shard_map/ppermute | solution.py:737
  15.4 0.9 %collective-permute-start.6 = (bf16[1,5,32,128]{3,2,1,0:T(8,128)(2,1)S(1)}, bf16[1,5,32,128]{3,2,1,0:T(8,128)(2,1)S(1)}, u32[]{:S(2)}, u32[]{:S(2)}) collective-permute-start(bf16[1,5,32,128]{3,2,1,0:T(8,128)(2,1)S(1)} %collective-permute-done.2.refs_1_), channel_id=1, source_target_pairs={{0,4},{4,0},{8,12},{12,8},{16,20},{20,16},{24,28},{28,24},{1,5},{5... | collective-permute-start | bytes 122888 | tf_op jit(solution)/shard_map/ppermute | solution.py:737
  16.3 1.2 %collective-permute-start.7 = (bf16[1,5,32,128]{3,2,1,0:T(8,128)(2,1)S(1)}, bf16[1,5,32,128]{3,2,1,0:T(8,128)(2,1)S(1)}, u32[]{:S(2)}, u32[]{:S(2)}) collective-permute-start(bf16[1,5,32,128]{3,2,1,0:T(8,128)(2,1)S(1)} %collective-permute-done.1.refs_2_), channel_id=1, source_target_pairs={{0,4},{4,0},{8,12},{12,8},{16,20},{20,16},{24,28},{28,24},{1,5},{5... | collective-permute-start | bytes 122888 | tf_op jit(solution)/shard_map/ppermute | solution.py:737
  17.4 0.7 copy.15
  18.1 0.7 fusion.3.codes_ref
  18.8 0.6 collective-permute-done.6.refs_4_
  19.4 0.9 %collective-permute-done.7.refs_5_ = bf16[1,5,32,128]{3,2,1,0:T(8,128)(2,1)S(1)} collective-permute-done((bf16[1,5,32,128]{3,2,1,0:T(8,128)(2,1)S(1)}, bf16[1,5,32,128]{3,2,1,0:T(8,128)(2,1)S(1)}, u32[]{:S(2)}, u32[]{:S(2)}) %collective-permute-start.7) | collective-permute-done | bytes 40992 | tf_op jit(solution)/shard_map/ppermute | solution.py:737
  20.3 0.7 shard_map.130.refs_0_.refs_4_
  21.1 1.3 %collective-permute-start.10 = (bf16[13,32,128]{2,1,0:T(8,128)(2,1)S(1)}, bf16[13,32,128]{2,1,0:T(8,128)(2,1)S(1)}, u32[]{:S(2)}, u32[]{:S(2)}) collective-permute-start(bf16[13,32,128]{2,1,0:T(8,128)(2,1)S(1)} %shard_map.130.refs_0_.refs_4_), channel_id=1, source_target_pairs={{0,2},{1,3},{2,0},{3,1},{4,6},{5,7},{6,4},{7,5},{8,10},{9,11},{10,... | collective-permute-start | bytes 319496 | tf_op jit(solution)/shard_map/ppermute | solution.py:737
  22.8 3.6 %shard_map.131 = (bf16[4,1152,384]{2,1,0:T(8,128)(2,1)S(1)}, f32[4,1024,128]{2,1,0:T(8,128)S(1)}, bf16[1152,128]{1,0:T(8,128)(2,1)S(1)}, bf16[512,128]{1,0:T(8,128)(2,1)S(1)}) custom-call(s32[4]{0:T(128)S(1)} %pad_add_fusion.where_ref, bf16[45,32,128]{2,1,0:T(8,128)(2,1)S(1)} %get-tuple-element.56.refs_0_, ...), custom_call_target="tpu_custom_call" | custom-call | tf_op jit(solution)/shard_map/pallas_call | solution.py:710
  27.1 1.3 %collective-permute-start.17 = (bf16[18,32,128]{2,1,0:T(8,128)(2,1)}, bf16[18,32,128]{2,1,0:T(8,128)(2,1)S(1)}, u32[]{:S(2)}, u32[]{:S(2)}) collective-permute-start(bf16[18,32,128]{2,1,0:T(8,128)(2,1)} %get-tuple-element.73.refs_0_), channel_id=1, source_target_pairs={{0,2},{1,3},{2,0},{3,1},{4,6},{5,7},{6,4},{7,5},{8,10},{9,11},{10,... | collective-permute-start | bytes 442376 | tf_op jit(solution)/shard_map/ppermute | solution.py:737
  28.4 2.6 %shard_map.132 = (bf16[4,1024,128]{2,1,0:T(8,128)(2,1)S(1)}, f32[1024,128]{1,0:T(8,128)S(1)}, bf16[1024,128]{1,0:T(8,128)(2,1)S(1)}, bf16[1,256,128]{2,1,0:T(8,1...) custom-call(s32[4]{0:T(128)S(1)} %pad_add_fusion.where_ref, ...), custom_call_target="tpu_custom_call" | custom-call | tf_op jit(solution)/shard_map/pallas_call | solution.py:710
  31.0 1.3 %collective-permute-start.13 = (bf16[1,256,128]{2,1,0:T(8,128)(2,1)S(1)}, bf16[1,256,128]{2,1,0:T(8,128)(2,1)S(1)}, u32[]{:S(2)}, u32[]{:S(2)}) collective-permute-start(bf16[1,256,128]{2,1,0:T(8,128)(2,1)S(1)} %get-tuple-element.74.refs_8_), channel_id=1, source_target_pairs={{0,8},{1,13},{2,10},{3,15},{4,12},{5,9},{6,14},{7,11},{8,0},{9,5},... | collective-permute-start | bytes 196616 | tf_op jit(solution)/shard_map/ppermute | solution.py:766
  32.3 3.0 %collective-permute-start.14 = (bf16[1,256,128]{2,1,0:T(8,128)(2,1)S(1)}, bf16[1,256,128]{2,1,0:T(8,128)(2,1)S(1)}, u32[]{:S(2)}, u32[]{:S(2)}) collective-permute-start(bf16[1,256,128]{2,1,0:T(8,128)(2,1)S(1)} %get-tuple-element.74.refs_8_), channel_id=1, source_target_pairs={{0,16},{1,21},{2,18},{3,23},{4,20},{5,17},{6,22},{7,19},{8,24},{9,... | collective-permute-start | bytes 196616 | tf_op jit(solution)/shard_map/ppermute | solution.py:766
  35.3 0.9 %collective-permute-start.15 = (bf16[1,256,128]{2,1,0:T(8,128)(2,1)S(1)}, bf16[1,256,128]{2,1,0:T(8,128)(2,1)S(1)}, u32[]{:S(2)}, u32[]{:S(2)}) collective-permute-start(bf16[1,256,128]{2,1,0:T(8,128)(2,1)S(1)} %get-tuple-element.74.refs_8_), channel_id=1, source_target_pairs={{0,28},{1,25},{2,30},{3,27},{4,24},{5,29},{6,26},{7,31},{8,20},{9,... | collective-permute-start | bytes 196616 | tf_op jit(solution)/shard_map/ppermute | solution.py:766
  36.2 0.7 collective-permute-start.16
  37.0 3.0 %shard_map.133 = (bf16[32,4096]{1,0:T(8,128)(2,1)S(1)}, f32[32,4096]{1,0:T(8,128)S(1)}, bf16[4,1152,384]{2,1,0:T(8,128)(2,1)S(1)}) custom-call(bf16[9,32,128]{2,1,0:T(8,128)(2,1)S(1)} %copy-done.2, f32[5,128,128]{2,1,0:T(8,128)S(1)} %get-tuple-element.76.ring, bf16[4,1152,384]{2,1,0:T(8,128)(2,1)S(1)} %get-tuple-element.77.x3_in), custom_call_target="tpu_custom_call", output_to_operand_aliasing={{2}: (2, {})} | custom-call | tf_op jit(solution)/shard_map/pallas_call | solution.py:710
  40.1 2.3 %collective-permute-done.15.refs_11_ = bf16[1,256,128]{2,1,0:T(8,128)(2,1)S(1)} collective-permute-done((bf16[1,256,128]{2,1,0:T(8,128)(2,1)S(1)}, bf16[1,256,128]{2,1,0:T(8,128)(2,1)S(1)}, u32[]{:S(2)}, u32[]{:S(2)}) %collective-permute-start.15) | collective-permute-done | bytes 65568 | tf_op jit(solution)/shard_map/ppermute | solution.py:766
  42.4 0.5 collective-permute-start.19
  42.9 0.5 collective-permute-start.21
  43.4 1.2 %collective-permute-done.22.refs_16_ = bf16[1,128,128]{2,1,0:T(8,128)(2,1)S(1)} collective-permute-done((bf16[1,128,128]{2,1,0:T(8,128)(2,1)S(1)}, bf16[1,128,128]{2,1,0:T(8,128)(2,1)S(1)}, u32[]{:S(2)}, u32[]{:S(2)}) %collective-permute-start.22) | collective-permute-done | bytes 32800 | tf_op jit(solution)/shard_map/ppermute | solution.py:737
  44.7 7.3 %shard_map.134 = (bf16[32,4096]{1,0:T(8,128)(2,1)}, bf16[768,128]{1,0:T(8,128)(2,1)S(1)}) custom-call(s32[8,8]{1,0:T(8,128)S(1)} %fusion.3.codes_ref, s32[4]{0:T(128)S(1)} %pad_add_fusion.where_ref, bf16[1024,128]{1,0:T(8,128)(2,1)S(1)} %get-tuple-element.68.act2_ref, f32[1024,128]{1,0:T(8,128)S(1)} %get-tuple-element.69.slope2_ref, ...), custom_call_target="tpu_custom_call" | custom-call | tf_op jit(solution)/shard_map/pallas_call | solution.py:710
  52.0 12.0 %all_to_all.10.in_ref = bf16[8,96,128]{2,1,0:T(8,128)(2,1)S(1)} all-to-all(bf16[8,96,128]{2,1,0:T(8,128)(2,1)S(1)} %bitcast.19), channel_id=1, replica_groups=mesh['tile'=8,'chan'=4] {'tile'}, dimensions={0} | all-to-all | bytes 393216 | tf_op jit(solution)/shard_map/all_to_all | solution.py:773
  64.1 10.7 %all_to_all.11 = bf16[8,96,128]{2,1,0:T(8,128)(2,1)S(1)} all-to-all(bf16[8,96,128]{2,1,0:T(8,128)(2,1)S(1)} %broadcast_in_dim.12), channel_id=1, replica_groups=mesh['tile'=8,'chan'=4] {'tile'}, dimensions={0} | all-to-all | bytes 393216 | tf_op jit(solution)/shard_map/all_to_all | solution.py:773
  74.8 0.7 shard_map.136
  (41 shorter events, 1.5 us)
Async XLA Ops:
  0.6 36.3 %copy-start.2 = (bf16[9,32,128]{2,1,0:T(8,128)(2,1)S(1)}, bf16[9,32,128]{2,1,0:T(8,128)(2,1)}, u32[]{:S(2)}) copy-start(bf16[9,32,128]{2,1,0:T(8,128)(2,1)} %w1_ref.1) | copy-start | bytes 221188
  3.6 7.2 %collective-permute-start = (bf16[1,5,32,128]{3,2,1,0:T(8,128)(2,1)}, bf16[1,5,32,128]{3,2,1,0:T(8,128)(2,1)S(1)}, u32[]{:S(2)}, u32[]{:S(2)}) collective-permute-start(bf16[1,5,32,128]{3,2,1,0:T(8,128)(2,1)} %get-tuple-element.51.rims_ref), channel_id=1, source_target_pairs={{0,16},{4,20},{8,24},{12,28},{16,0},{20,4},{24,8},{28,12},{1,17},{... | collective-permute-start | bytes 122888 | tf_op jit(solution)/shard_map/ppermute | solution.py:737
  7.7 13.3 %collective-permute-start.4 = (bf16[45,32,128]{2,1,0:T(8,128)(2,1)}, bf16[45,32,128]{2,1,0:T(8,128)(2,1)S(1)}, u32[]{:S(2)}, u32[]{:S(2)}) collective-permute-start(bf16[45,32,128]{2,1,0:T(8,128)(2,1)} %get-tuple-element.52.pack_ref), channel_id=1, source_target_pairs={{0,2},{1,3},{2,0},{3,1},{4,6},{5,7},{6,4},{7,5},{8,10},{9,11},{10,... | collective-permute-start | bytes 1105928 | tf_op jit(solution)/shard_map/ppermute | solution.py:737
  9.2 6.2 %collective-permute-start.2 = (bf16[1,5,32,128]{3,2,1,0:T(8,128)(2,1)}, bf16[1,5,32,128]{3,2,1,0:T(8,128)(2,1)S(1)}, u32[]{:S(2)}, u32[]{:S(2)}) collective-permute-start(bf16[1,5,32,128]{3,2,1,0:T(8,128)(2,1)} %get-tuple-element.51.rims_ref), channel_id=1, source_target_pairs={{0,8},{4,12},{8,0},{12,4},{16,24},{20,28},{24,16},{28,20},{1,9},{5... | collective-permute-start | bytes 122888 | tf_op jit(solution)/shard_map/ppermute | solution.py:737
  10.8 11.7 %collective-permute-start.3 = (bf16[45,32,128]{2,1,0:T(8,128)(2,1)}, bf16[45,32,128]{2,1,0:T(8,128)(2,1)S(1)}, u32[]{:S(2)}, u32[]{:S(2)}) collective-permute-start(bf16[45,32,128]{2,1,0:T(8,128)(2,1)} %get-tuple-element.52.pack_ref), channel_id=1, source_target_pairs={{0,1},{1,0},{2,3},{3,2},{4,5},{5,4},{6,7},{7,6},{8,9},{9,8},{10,11... | collective-permute-start | bytes 1105928 | tf_op jit(solution)/shard_map/ppermute | solution.py:737
  10.8 4.7 %collective-permute-start.1 = (bf16[1,5,32,128]{3,2,1,0:T(8,128)(2,1)S(1)}, bf16[1,5,32,128]{3,2,1,0:T(8,128)(2,1)S(1)}, u32[]{:S(2)}, u32[]{:S(2)}) collective-permute-start(bf16[1,5,32,128]{3,2,1,0:T(8,128)(2,1)S(1)} %collective-permute-done.far_ref), channel_id=1, source_target_pairs={{0,8},{4,12},{8,0},{12,4},{16,24},{20,28},{24,16},{28,20},{1,9},{5... | collective-permute-start | bytes 122888 | tf_op jit(solution)/shard_map/ppermute | solution.py:737
  12.0 1.0 %copy-start.1 = (bf16[45,32,128]{2,1,0:T(8,128)(2,1)S(1)}, bf16[45,32,128]{2,1,0:T(8,128)(2,1)}, u32[]{:S(2)}) copy-start(bf16[45,32,128]{2,1,0:T(8,128)(2,1)} %get-tuple-element.52.pack_ref) | copy-start | bytes 1105924
  13.0 0.8 %copy-start.5 = (bf16[1,5,32,128]{3,2,1,0:T(8,128)(2,1)S(1)}, bf16[1,5,32,128]{3,2,1,0:T(8,128)(2,1)}, u32[]{:S(2)}) copy-start(bf16[1,5,32,128]{3,2,1,0:T(8,128)(2,1)} %get-tuple-element.51.rims_ref) | copy-start | bytes 122884
  13.8 6.5 %collective-permute-start.5 = (bf16[2,5,32,128]{3,2,1,0:T(8,128)(2,1)S(1)}, bf16[2,5,32,128]{3,2,1,0:T(8,128)(2,1)S(1)}, u32[]{:S(2)}, u32[]{:S(2)}) collective-permute-start(bf16[2,5,32,128]{3,2,1,0:T(8,128)(2,1)S(1)} %get-tuple-element.57.refs_0_), channel_id=1, source_target_pairs={{0,4},{4,0},{8,12},{12,8},{16,20},{20,16},{24,28},{28,24},{1,5},{5... | collective-permute-start | bytes 245768 | tf_op jit(solution)/shard_map/ppermute | solution.py:737
  15.4 4.0 %collective-permute-start.6 = (bf16[1,5,32,128]{3,2,1,0:T(8,128)(2,1)S(1)}, bf16[1,5,32,128]{3,2,1,0:T(8,128)(2,1)S(1)}, u32[]{:S(2)}, u32[]{:S(2)}) collective-permute-start(bf16[1,5,32,128]{3,2,1,0:T(8,128)(2,1)S(1)} %collective-permute-done.2.refs_1_), channel_id=1, source_target_pairs={{0,4},{4,0},{8,12},{12,8},{16,20},{20,16},{24,28},{28,24},{1,5},{5... | collective-permute-start | bytes 122888 | tf_op jit(solution)/shard_map/ppermute | solution.py:737
  16.3 4.0 %collective-permute-start.7 = (bf16[1,5,32,128]{3,2,1,0:T(8,128)(2,1)S(1)}, bf16[1,5,32,128]{3,2,1,0:T(8,128)(2,1)S(1)}, u32[]{:S(2)}, u32[]{:S(2)}) collective-permute-start(bf16[1,5,32,128]{3,2,1,0:T(8,128)(2,1)S(1)} %collective-permute-done.1.refs_2_), channel_id=1, source_target_pairs={{0,4},{4,0},{8,12},{12,8},{16,20},{20,16},{24,28},{28,24},{1,5},{5... | collective-permute-start | bytes 122888 | tf_op jit(solution)/shard_map/ppermute | solution.py:737
  21.0 1.8 %collective-permute-start.8 = (bf16[45,32,128]{2,1,0:T(8,128)(2,1)S(1)}, bf16[45,32,128]{2,1,0:T(8,128)(2,1)S(1)}, u32[]{:S(2)}, u32[]{:S(2)}) collective-permute-start(bf16[45,32,128]{2,1,0:T(8,128)(2,1)S(1)} %collective-permute-done.4.refs_2_), channel_id=1, source_target_pairs={{0,1},{1,0},{2,3},{3,2},{4,5},{5,4},{6,7},{7,6},{8,9},{9,8},{10,11... | collective-permute-start | bytes 1105928 | tf_op jit(solution)/shard_map/ppermute | solution.py:737
  21.1 5.4 %collective-permute-start.10 = (bf16[13,32,128]{2,1,0:T(8,128)(2,1)S(1)}, bf16[13,32,128]{2,1,0:T(8,128)(2,1)S(1)}, u32[]{:S(2)}, u32[]{:S(2)}) collective-permute-start(bf16[13,32,128]{2,1,0:T(8,128)(2,1)S(1)} %shard_map.130.refs_0_.refs_4_), channel_id=1, source_target_pairs={{0,2},{1,3},{2,0},{3,1},{4,6},{5,7},{6,4},{7,5},{8,10},{9,11},{10,... | collective-permute-start | bytes 319496 | tf_op jit(solution)/shard_map/ppermute | solution.py:737
  26.4 18.3 %copy-start = (bf16[512,512]{1,0:T(8,128)(2,1)S(1)}, bf16[512,512]{1,0:T(8,128)(2,1)}, u32[]{:S(2)}) copy-start(bf16[512,512]{1,0:T(8,128)(2,1)} %constant.21.clone.m_ref) | copy-start | bytes 1572868
  26.4 18.3 %copy-start.3 = (bf16[32,4096]{1,0:T(8,128)(2,1)S(1)}, bf16[32,4096]{1,0:T(8,128)(2,1)}, u32[]{:S(2)}) copy-start(bf16[32,4096]{1,0:T(8,128)(2,1)} %get-tuple-element.83.og_ref) | copy-start | bytes 786436
  26.4 18.3 %copy-start.4 = (bf16[18,32,128]{2,1,0:T(8,128)(2,1)S(1)}, bf16[18,32,128]{2,1,0:T(8,128)(2,1)}, u32[]{:S(2)}) copy-start(bf16[18,32,128]{2,1,0:T(8,128)(2,1)} %get-tuple-element.73.refs_0_) | copy-start | bytes 442372
  26.5 4.6 %collective-permute-start.12 = (bf16[18,32,128]{2,1,0:T(8,128)(2,1)}, bf16[18,32,128]{2,1,0:T(8,128)(2,1)S(1)}, u32[]{:S(2)}, u32[]{:S(2)}) collective-permute-start(bf16[18,32,128]{2,1,0:T(8,128)(2,1)} %get-tuple-element.73.refs_0_), channel_id=1, source_target_pairs={{0,1},{1,0},{2,3},{3,2},{4,5},{5,4},{6,7},{7,6},{8,9},{9,8},{10,11... | collective-permute-start | bytes 442376 | tf_op jit(solution)/shard_map/ppermute | solution.py:737
  26.6 1.8 %collective-permute-start.9 = (bf16[13,32,128]{2,1,0:T(8,128)(2,1)S(1)}, bf16[13,32,128]{2,1,0:T(8,128)(2,1)S(1)}, u32[]{:S(2)}, u32[]{:S(2)}) collective-permute-start(bf16[13,32,128]{2,1,0:T(8,128)(2,1)S(1)} %shard_map.130.refs_0_.refs_4_), channel_id=1, source_target_pairs={{0,1},{1,0},{2,3},{3,2},{4,5},{5,4},{6,7},{7,6},{8,9},{9,8},{10,11... | collective-permute-start | bytes 319496 | tf_op jit(solution)/shard_map/ppermute | solution.py:737
  27.0 1.4 %collective-permute-start.11 = (bf16[13,32,128]{2,1,0:T(8,128)(2,1)S(1)}, bf16[13,32,128]{2,1,0:T(8,128)(2,1)S(1)}, u32[]{:S(2)}, u32[]{:S(2)}) collective-permute-start(bf16[13,32,128]{2,1,0:T(8,128)(2,1)S(1)} %collective-permute-done.10.refs_2_.refs_6_), channel_id=1, source_target_pairs={{0,1},{1,0},{2,3},{3,2},{4,5},{5,4},{6,7},{7,6},{8,9},{9,8},{10,11... | collective-permute-start | bytes 319496 | tf_op jit(solution)/shard_map/ppermute | solution.py:737
  27.1 12.9 %collective-permute-start.17 = (bf16[18,32,128]{2,1,0:T(8,128)(2,1)}, bf16[18,32,128]{2,1,0:T(8,128)(2,1)S(1)}, u32[]{:S(2)}, u32[]{:S(2)}) collective-permute-start(bf16[18,32,128]{2,1,0:T(8,128)(2,1)} %get-tuple-element.73.refs_0_), channel_id=1, source_target_pairs={{0,2},{1,3},{2,0},{3,1},{4,6},{5,7},{6,4},{7,5},{8,10},{9,11},{10,... | collective-permute-start | bytes 442376 | tf_op jit(solution)/shard_map/ppermute | solution.py:737
  31.0 9.1 %collective-permute-start.13 = (bf16[1,256,128]{2,1,0:T(8,128)(2,1)S(1)}, bf16[1,256,128]{2,1,0:T(8,128)(2,1)S(1)}, u32[]{:S(2)}, u32[]{:S(2)}) collective-permute-start(bf16[1,256,128]{2,1,0:T(8,128)(2,1)S(1)} %get-tuple-element.74.refs_8_), channel_id=1, source_target_pairs={{0,8},{1,13},{2,10},{3,15},{4,12},{5,9},{6,14},{7,11},{8,0},{9,5},... | collective-permute-start | bytes 196616 | tf_op jit(solution)/shard_map/ppermute | solution.py:766
  32.3 7.8 %collective-permute-start.14 = (bf16[1,256,128]{2,1,0:T(8,128)(2,1)S(1)}, bf16[1,256,128]{2,1,0:T(8,128)(2,1)S(1)}, u32[]{:S(2)}, u32[]{:S(2)}) collective-permute-start(bf16[1,256,128]{2,1,0:T(8,128)(2,1)S(1)} %get-tuple-element.74.refs_8_), channel_id=1, source_target_pairs={{0,16},{1,21},{2,18},{3,23},{4,20},{5,17},{6,22},{7,19},{8,24},{9,... | collective-permute-start | bytes 196616 | tf_op jit(solution)/shard_map/ppermute | solution.py:766
  35.3 7.1 %collective-permute-start.15 = (bf16[1,256,128]{2,1,0:T(8,128)(2,1)S(1)}, bf16[1,256,128]{2,1,0:T(8,128)(2,1)S(1)}, u32[]{:S(2)}, u32[]{:S(2)}) collective-permute-start(bf16[1,256,128]{2,1,0:T(8,128)(2,1)S(1)} %get-tuple-element.74.refs_8_), channel_id=1, source_target_pairs={{0,28},{1,25},{2,30},{3,27},{4,24},{5,29},{6,26},{7,31},{8,20},{9,... | collective-permute-start | bytes 196616 | tf_op jit(solution)/shard_map/ppermute | solution.py:766
  36.2 3.9 %collective-permute-start.16 = (bf16[1,128,128]{2,1,0:T(8,128)(2,1)S(1)}, bf16[1,128,128]{2,1,0:T(8,128)(2,1)S(1)}, u32[]{:S(2)}, u32[]{:S(2)}) collective-permute-start(bf16[1,128,128]{2,1,0:T(8,128)(2,1)S(1)} %get-tuple-element.75), channel_id=1, source_target_pairs={{0,4},{4,0},{8,12},{12,8},{16,20},{20,16},{24,28},{28,24},{1,5},{5... | collective-permute-start | bytes 98312 | tf_op jit(solution)/shard_map/ppermute | solution.py:737
  42.4 2.2 %collective-permute-start.18 = (bf16[18,32,128]{2,1,0:T(8,128)(2,1)S(1)}, bf16[18,32,128]{2,1,0:T(8,128)(2,1)S(1)}, u32[]{:S(2)}, u32[]{:S(2)}) collective-permute-start(bf16[18,32,128]{2,1,0:T(8,128)(2,1)S(1)} %collective-permute-done.17.refs_2_), channel_id=1, source_target_pairs={{0,1},{1,0},{2,3},{3,2},{4,5},{5,4},{6,7},{7,6},{8,9},{9,8},{10,11... | collective-permute-start | bytes 442376 | tf_op jit(solution)/shard_map/ppermute | solution.py:737
  42.4 2.2 %collective-permute-start.19 = (bf16[1,256,128]{2,1,0:T(8,128)(2,1)S(1)}, bf16[1,256,128]{2,1,0:T(8,128)(2,1)S(1)}, u32[]{:S(2)}, u32[]{:S(2)}) collective-permute-start(bf16[1,256,128]{2,1,0:T(8,128)(2,1)S(1)} %collective-permute-done.13.refs_9_), channel_id=1, source_target_pairs={{0,1},{1,0},{2,3},{3,2},{4,5},{5,4},{6,7},{7,6},{8,9},{9,8},{10,11... | collective-permute-start | bytes 196616 | tf_op jit(solution)/shard_map/ppermute | solution.py:737
  42.9 1.7 %collective-permute-start.20 = (bf16[1,256,128]{2,1,0:T(8,128)(2,1)S(1)}, bf16[1,256,128]{2,1,0:T(8,128)(2,1)S(1)}, u32[]{:S(2)}, u32[]{:S(2)}) collective-permute-start(bf16[1,256,128]{2,1,0:T(8,128)(2,1)S(1)} %collective-permute-done.14.refs_10_), channel_id=1, source_target_pairs={{0,1},{1,0},{2,3},{3,2},{4,5},{5,4},{6,7},{7,6},{8,9},{9,8},{10,11... | collective-permute-start | bytes 196616 | tf_op jit(solution)/shard_map/ppermute | solution.py:737
  42.9 1.7 %collective-permute-start.21 = (bf16[1,256,128]{2,1,0:T(8,128)(2,1)S(1)}, bf16[1,256,128]{2,1,0:T(8,128)(2,1)S(1)}, u32[]{:S(2)}, u32[]{:S(2)}) collective-permute-start(bf16[1,256,128]{2,1,0:T(8,128)(2,1)S(1)} %collective-permute-done.15.refs_11_), channel_id=1, source_target_pairs={{0,1},{1,0},{2,3},{3,2},{4,5},{5,4},{6,7},{7,6},{8,9},{9,8},{10,11... | collective-permute-start | bytes 196616 | tf_op jit(solution)/shard_map/ppermute | solution.py:737
  43.4 1.2 %collective-permute-start.22 = (bf16[1,128,128]{2,1,0:T(8,128)(2,1)S(1)}, bf16[1,128,128]{2,1,0:T(8,128)(2,1)S(1)}, u32[]{:S(2)}, u32[]{:S(2)}) collective-permute-start(bf16[1,128,128]{2,1,0:T(8,128)(2,1)S(1)} %collective-permute-done.16.refs_12_), channel_id=1, source_target_pairs={{0,1},{1,0},{2,3},{3,2},{4,5},{5,4},{6,7},{7,6},{8,9},{9,8},{10,11... | collective-permute-start | bytes 98312 | tf_op jit(solution)/shard_map/ppermute | solution.py:737

commit v4 on v2

--- a/solution.py
+++ b/solution.py
@@ -143,7 +143,7 @@
 
 
 def sort_kernel(
-    f_hbm, g_hbm, w1_hbm, wd_hbm, w2_hbm, up_hbm, pack_ref, rims_ref, sorted_ref, pack2_ref, f_ref, g_ref, m_ref, sems
+    f_hbm, g_hbm, w1_hbm, wd_hbm, w2_hbm, up_hbm, pack_ref, rims_ref, sorted_ref, pooled_ref, f_ref, g_ref, m_ref, sems
 ):
     count = f_ref.shape[0]
     started = fetch(
@@ -152,8 +152,8 @@
             (g_hbm, g_ref),
             (w1_hbm, pack_ref.at[32:41]),
             (wd_hbm, pack_ref.at[41:45]),
-            (w2_hbm, pack2_ref.at[8:17]),
-            (up_hbm, pack2_ref.at[17]),
+            (w2_hbm, pack_ref.at[45:54]),
+            (up_hbm, pack_ref.at[54]),
         ],
         sems,
     )
@@ -188,7 +188,7 @@
     for jb in range(8):
         for ph in range(4):
             sorted_ref[:, ph * CELLS + jb * 128 : ph * CELLS + (jb + 1) * 128] = pieces[jb][ph].astype(BF16)
-        pack2_ref[jb] = ((pieces[jb][0] + pieces[jb][1]) + (pieces[jb][2] + pieces[jb][3])).astype(BF16)
+        pooled_ref[jb] = ((pieces[jb][0] + pieces[jb][1]) + (pieces[jb][2] + pieces[jb][3])).astype(BF16)
     for copy in started[2:]:
         copy.wait()
 
@@ -200,7 +200,7 @@
             put(slot, ref, index)
 
 
-def pick_kernel(spots, codes_ref, where_ref, *refs):
+def pick_kernel(spots, codes_ref, where_ref, pooled_ref, *refs):
     *rims, out_ref, held = refs
     tile, base, core = where_ref[0], where_ref[2], where_ref[1] & 1
 
@@ -220,12 +220,14 @@
             moved = pltpu.roll(picked, shift, 1) if shift else picked
             corners = corners + jnp.where(lane == spot, moved, 0.0)
     out_ref[4] = corners.astype(BF16)
-    for other in range(out_ref.shape[0] - 5):
-        out_ref[5 + other] = held[other ^ base, 4]
-
-
-def stage_kernel(pack_ref, rims_ref, far_ref, near_ref, pair_ref):
+    out_ref[5:13] = pooled_ref[...]
+    for other in range(out_ref.shape[0] - 13):
+        out_ref[13 + other] = held[other ^ base, 4]
+
+
+def stage_kernel(pack_ref, pooled_ref, rims_ref, far_ref, near_ref, near_pooled_ref, pair_ref):
     near_ref[...] = pack_ref[...]
+    near_pooled_ref[...] = pooled_ref[...]
     pair_ref[0:1] = rims_ref[...]
     pair_ref[1:2] = far_ref[...]
 
@@ -534,14 +536,14 @@
     *rims, out_ref, grad_ref, w2s, w2t, ups, pooled_all, prims, rims_all, left, right, g3pad, sums, a3, coarse, field, back = refs
     tile, me, tile_base, base = where_ref[0], where_ref[1], where_ref[2], where_ref[3]
     own = packs[0].shape[1]
-    place_conv(packs, base, 8, w2s)
+    place_conv(packs, base, 45, w2s)
     for slot in range(nc):
         row = rows_of(slot, base, own)
-        ups[pl.ds(row, own), :] = packs[slot][17]
+        ups[pl.ds(row, own), :] = packs[slot][54]
         for jb in range(8):
-            pooled_all[pl.ds(row, own), jb * 128 : (jb + 1) * 128] = packs[slot][jb]
-        for other in range(mores[slot].shape[0] - 5):
-            prims[pl.ds(row, own), other * 128 : (other + 1) * 128] = mores[slot][5 + other]
+            pooled_all[pl.ds(row, own), jb * 128 : (jb + 1) * 128] = mores[slot][5 + jb]
+        for other in range(mores[slot].shape[0] - 13):
+            prims[pl.ds(row, own), other * 128 : (other + 1) * 128] = mores[slot][13 + other]
 
     def put(slot, ref, index):
         rims_all[slot] = ref[index]
@@ -791,13 +793,13 @@
     matrix = sort_matrix()
     half = nc // 2
 
-    pack, rims, sorted_g, pack2 = call(
+    pack, rims, sorted_g, pooled = call(
         sort_kernel,
         [
-            shape((45, own, 128)),
+            shape((55, own, 128)),
             shape((1, 5, own, 128)),
             shape((own, 4 * CELLS)),
-            shape((18, own, 128)),
+            shape((8, own, 128)),
         ],
         features,
         out_grad,
@@ -818,13 +820,16 @@
     if is_split():
         far, near = paired(rims, "tile", 4), paired(rims, "tile", 2)
         cross = paired(far, "tile", 2)
-        pack_near, pair = call(
-            stage_kernel, [shape(pack.shape), shape((2,) + rims.shape[1:])], pack, rims, far
+        pack_near, pooled, pair = call(
+            stage_kernel,
+            [shape(pack.shape), shape(pooled.shape), shape((2,) + rims.shape[1:])],
+            pack,
+            pooled,
+            rims,
+            far,
         )
         beside = paired(pair, "tile", 1)
-        cross, near, pack_near, pack2, adjacency = lax.optimization_barrier(
-            (cross, near, pack_near, pack2, adjacency)
-        )
+        cross, near, pack_near, adjacency = lax.optimization_barrier((cross, near, pack_near, adjacency))
         last = [paired(near, "tile", 1), paired(cross, "tile", 1)]
         all_rims = [pair, near, cross, beside] + last
         rim_spots = [[(slot, slot) for slot in group] for group in ((0, 4), (2,), (6,), (1, 5), (3,), (7,))]
@@ -835,9 +840,10 @@
     codes = jnp.where(adjacency[:, :, 0] < 0, -1, adjacency[:, :, 0] * 4 + turns)
     ring = call(
         partial(pick_kernel, rim_spots),
-        shape((5 + tiles, own, 128)),
+        shape((13 + tiles, own, 128)),
         codes,
         where,
+        pooled,
         *all_rims,
         scratch=[pltpu.VMEM((tiles + 1, 5, own, 128), BF16)],
     )
@@ -864,8 +870,7 @@
             pltpu.VMEM((128, 4 * CELLS), BF16),
         ],
     )
-    x3, ring_far, pack2 = lax.optimization_barrier((x3, ring_far, pack2))
-    pack2_far, pack2_side = paired(pack2, "chan", half), paired(pack2, "chan", 1)
+    x3, ring_far = lax.optimization_barrier((x3, ring_far))
     rings = whole(ring, ring_far)
     act, slope2, act2, rims2, half2, ring_sorted = call(
         partial(fine_ring_kernel, nc),
@@ -888,7 +893,6 @@
             pltpu.VMEM((CELLS, 128), F32),
         ],
     )
-    rims2, half2, pack2_side = lax.optimization_barrier((rims2, half2, pack2_side))
     act1, slope1, x3 = call(
         own_fine_kernel,
         [shape((own, 4 * CELLS)), shape((own, 4 * CELLS), F32), shape((4, PADDED, 384))],
@@ -897,8 +901,7 @@
         x3,
         alias={2: 2},
     )
-    all_rims2, (act1, slope1, x3, pack2_far) = copies(rims2, half2, (act1, slope1, x3, pack2_far))
-    packs2 = [pack2, pack2_side, pack2_far, paired(pack2_far, "chan", 1)]
+    all_rims2, (act1, slope1, x3) = copies(rims2, half2, (act1, slope1, x3))
     rows = -(-23 * own // (16 * tiles)) * 16
     output, late = call(
         partial(level_kernel, nc, spots_of()),
@@ -914,7 +917,7 @@
         sorted_g,
         x3,
         matrix,
-        *packs2,
+        *packs,
         *rings,
         *all_rims2,
         scratch=[

time: 75 us -> 77.7 us (1.036)
  waiting for transfers between devices: 3.87 us -> 8.06 us
  starting transfers between devices: 22.3 us -> 20 us
  local copies, waits for them, and re-layouts: 2.51 us -> 3.37 us
    ppermute x20 -> x17, waiting for transfers between devices: 3.35 us -> 7.5 us  [paired(): return lax.ppermute(values, axis, [(i, i ^ bit) for i in range(count)])]
    ppermute x20 -> x17, starting transfers between devices: 17.2 us -> 14.6 us  [paired(): return lax.ppermute(values, axis, [(i, i ^ bit) for i in range(count)])]
    unnamed x12, local copies, waits for them, and re-layouts: 1.79 us -> 2.65 us
  transfers between devices with their start and end apart: 23 -> 20, of which waited for: 7 -> 9; matrix products, arithmetic and copies ran while one was open for 2% -> 2% of each run, Pallas kernels for 13% -> 10%
where the time goes in v4:
time: 77.7 us; the launch traced here: 77.3 us
  blocking collectives  23.4 us (30%)
  Pallas kernels  21 us (27%)
  starting transfers between devices  20 us (26%)
  waiting for transfers between devices  8.06 us (10%)
  local copies, waits for them, and re-layouts  3.37 us (4%)
    all_to_all x2, blocking collectives, swap(): return lax.all_to_all(values, 'tile', split_axis=0, concat_axis=0)  23.4 us
    pallas_call x9, Pallas kernels, call(): pl.pallas_call(kernel, out_shape=outs, in_specs=specs, out_specs=[vmem] *...  21 us
    ppermute x17, starting transfers between devices, paired(): return lax.ppermute(values, axis, [(i, i ^ bit) for i in range(count)])  14.6 us
    ppermute x17, waiting for transfers between devices, paired(): return lax.ppermute(values, axis, [(i, i ^ bit) for i in range(count)])  7.5 us
    ppermute x3, starting transfers between devices, copies(): got.append(lax.ppermute(block, ('tile', 'chan'), perm))  5.4 us
    unnamed x12, local copies, waits for them, and re-layouts  2.65 us
  transfers between devices with their start and end apart: 20, of which 9 were waited for; matrix products, arithmetic and copies ran while one was open for 2% of the time, Pallas kernels for 10%

profile of v4, /device:TPU:0, one launch (start us, length us, event | category | flops | bytes accessed | tf_op | source)
XLA Modules:
  0.0 77.3 jit_solution(18399666212945611929)
XLA Ops:
  0.6 2.9 %shard_map.128 = (bf16[55,32,128]{2,1,0:T(8,128)(2,1)}, bf16[1,5,32,128]{3,2,1,0:T(8,128)(2,1)}, bf16[32,4096]{1,0:T(8,128)(2,1)}, bf16[8,32,128]{2,1,0:T(8,128)(2,1)}) custom-call(bf16[32,4096]{1,0:T(8,128)(2,1)} %f_hbm.1, bf16[32,4096]{1,0:T(8,128)(2,1)} %g_hbm.1, bf16[9,32,128]{2,1,0:T(8,128)(2,1)} %w1_ref.1, bf16[4,32,128]{2,1,0:T(8,128)(2,1)} %wd_hbm.1, ...), custom_call_target="tpu_custom_call" | custom-call | tf_op jit(solution)/shard_map/pallas_call | solution.py:712
  3.6 3.0 %collective-permute-start.4 = (bf16[55,32,128]{2,1,0:T(8,128)(2,1)}, bf16[55,32,128]{2,1,0:T(8,128)(2,1)S(1)}, u32[]{:S(2)}, u32[]{:S(2)}) collective-permute-start(bf16[55,32,128]{2,1,0:T(8,128)(2,1)} %get-tuple-element.47.pack_ref), channel_id=1, source_target_pairs={{0,2},{1,3},{2,0},{3,1},{4,6},{5,7},{6,4},{7,5},{8,10},{9,11},{10,... | collective-permute-start | bytes 1351688 | tf_op jit(solution)/shard_map/ppermute | solution.py:739
  6.6 2.6 %collective-permute-start = (bf16[1,5,32,128]{3,2,1,0:T(8,128)(2,1)}, bf16[1,5,32,128]{3,2,1,0:T(8,128)(2,1)S(1)}, u32[]{:S(2)}, u32[]{:S(2)}) collective-permute-start(bf16[1,5,32,128]{3,2,1,0:T(8,128)(2,1)} %get-tuple-element.46.rims_ref), channel_id=1, source_target_pairs={{0,16},{4,20},{8,24},{12,28},{16,0},{20,4},{24,8},{28,12},{1,17},{... | collective-permute-start | bytes 122888 | tf_op jit(solution)/shard_map/ppermute | solution.py:739
  9.2 1.6 %collective-permute-start.2 = (bf16[1,5,32,128]{3,2,1,0:T(8,128)(2,1)}, bf16[1,5,32,128]{3,2,1,0:T(8,128)(2,1)S(1)}, u32[]{:S(2)}, u32[]{:S(2)}) collective-permute-start(bf16[1,5,32,128]{3,2,1,0:T(8,128)(2,1)} %get-tuple-element.46.rims_ref), channel_id=1, source_target_pairs={{0,8},{4,12},{8,0},{12,4},{16,24},{20,28},{24,16},{28,20},{1,9},{5... | collective-permute-start | bytes 122888 | tf_op jit(solution)/shard_map/ppermute | solution.py:739
  10.8 1.1 %collective-permute-done.far_ref = bf16[1,5,32,128]{3,2,1,0:T(8,128)(2,1)S(1)} collective-permute-done((bf16[1,5,32,128]{3,2,1,0:T(8,128)(2,1)}, bf16[1,5,32,128]{3,2,1,0:T(8,128)(2,1)S(1)}, u32[]{:S(2)}, u32[]{:S(2)}) %collective-permute-start) | collective-permute-done | bytes 40992 | tf_op jit(solution)/shard_map/ppermute | solution.py:739
  11.8 1.4 %collective-permute-start.1 = (bf16[1,5,32,128]{3,2,1,0:T(8,128)(2,1)S(1)}, bf16[1,5,32,128]{3,2,1,0:T(8,128)(2,1)S(1)}, u32[]{:S(2)}, u32[]{:S(2)}) collective-permute-start(bf16[1,5,32,128]{3,2,1,0:T(8,128)(2,1)S(1)} %collective-permute-done.far_ref), channel_id=1, source_target_pairs={{0,8},{4,12},{8,0},{12,4},{16,24},{20,28},{24,16},{28,20},{1,9},{5... | collective-permute-start | bytes 122888 | tf_op jit(solution)/shard_map/ppermute | solution.py:739
  13.3 1.0 %copy-done.1 = bf16[55,32,128]{2,1,0:T(8,128)(2,1)S(1)} copy-done((bf16[55,32,128]{2,1,0:T(8,128)(2,1)S(1)}, bf16[55,32,128]{2,1,0:T(8,128)(2,1)}, u32[]{:S(2)}) %copy-start.1) | copy-done | bytes 450584
  14.4 0.8 %copy-done.4 = bf16[8,32,128]{2,1,0:T(8,128)(2,1)S(1)} copy-done((bf16[8,32,128]{2,1,0:T(8,128)(2,1)S(1)}, bf16[8,32,128]{2,1,0:T(8,128)(2,1)}, u32[]{:S(2)}) %copy-start.4) | copy-done | bytes 65560
  15.2 0.8 %copy-done.5 = bf16[1,5,32,128]{3,2,1,0:T(8,128)(2,1)S(1)} copy-done((bf16[1,5,32,128]{3,2,1,0:T(8,128)(2,1)S(1)}, bf16[1,5,32,128]{3,2,1,0:T(8,128)(2,1)}, u32[]{:S(2)}) %copy-start.5) | copy-done | bytes 40984
  16.0 1.6 %collective-permute-start.5 = (bf16[2,5,32,128]{3,2,1,0:T(8,128)(2,1)S(1)}, bf16[2,5,32,128]{3,2,1,0:T(8,128)(2,1)S(1)}, u32[]{:S(2)}, u32[]{:S(2)}) collective-permute-start(bf16[2,5,32,128]{3,2,1,0:T(8,128)(2,1)S(1)} %get-tuple-element.53.refs_0_), channel_id=1, source_target_pairs={{0,4},{4,0},{8,12},{12,8},{16,20},{20,16},{24,28},{28,24},{1,5},{5... | collective-permute-start | bytes 245768 | tf_op jit(solution)/shard_map/ppermute | solution.py:739
  18.1 1.5 %collective-permute-start.7 = (bf16[1,5,32,128]{3,2,1,0:T(8,128)(2,1)S(1)}, bf16[1,5,32,128]{3,2,1,0:T(8,128)(2,1)S(1)}, u32[]{:S(2)}, u32[]{:S(2)}) collective-permute-start(bf16[1,5,32,128]{3,2,1,0:T(8,128)(2,1)S(1)} %collective-permute-done.1.refs_2_), channel_id=1, source_target_pairs={{0,4},{4,0},{8,12},{12,8},{16,20},{20,16},{24,28},{28,24},{1,5},{5... | collective-permute-start | bytes 122888 | tf_op jit(solution)/shard_map/ppermute | solution.py:739
  19.6 0.7 copy.15
  20.3 0.7 fusion.3.codes_ref
  21.0 0.6 collective-permute-done.6.refs_4_
  22.1 0.7 shard_map.130.refs_0_.refs_4_
  22.9 0.6 collective-permute-start.10
  23.7 1.0 %collective-permute-done.8.refs_3_ = bf16[55,32,128]{2,1,0:T(8,128)(2,1)S(1)} collective-permute-done((bf16[55,32,128]{2,1,0:T(8,128)(2,1)S(1)}, bf16[55,32,128]{2,1,0:T(8,128)(2,1)S(1)}, u32[]{:S(2)}, u32[]{:S(2)}) %collective-permute-start.8) | collective-permute-done | bytes 450592 | tf_op jit(solution)/shard_map/ppermute | solution.py:739
  24.7 3.6 %shard_map.131 = (bf16[4,1152,384]{2,1,0:T(8,128)(2,1)S(1)}, f32[4,1024,128]{2,1,0:T(8,128)S(1)}, bf16[1152,128]{1,0:T(8,128)(2,1)S(1)}, bf16[512,128]{1,0:T(8,128)(2,1)S(1)}) custom-call(s32[4]{0:T(128)S(1)} %pad_add_fusion.where_ref, bf16[55,32,128]{2,1,0:T(8,128)(2,1)S(1)} %get-tuple-element.51.refs_0_, ...), custom_call_target="tpu_custom_call" | custom-call | tf_op jit(solution)/shard_map/pallas_call | solution.py:712
  28.3 1.4 %collective-permute-done.10.refs_2_.refs_6_ = bf16[21,32,128]{2,1,0:T(8,128)(2,1)S(1)} collective-permute-done((bf16[21,32,128]{2,1,0:T(8,128)(2,1)S(1)}, bf16[21,32,128]{2,1,0:T(8,128)(2,1)S(1)}, u32[]{:S(2)}, u32[]{:S(2)}) %collective-permute-start.10) | collective-permute-done | bytes 172064 | tf_op jit(solution)/shard_map/ppermute | solution.py:739
  29.7 1.4 %collective-permute-done.11.refs_3_.refs_7_ = bf16[21,32,128]{2,1,0:T(8,128)(2,1)S(1)} collective-permute-done((bf16[21,32,128]{2,1,0:T(8,128)(2,1)S(1)}, bf16[21,32,128]{2,1,0:T(8,128)(2,1)S(1)}, u32[]{:S(2)}, u32[]{:S(2)}) %collective-permute-start.11) | collective-permute-done | bytes 172064 | tf_op jit(solution)/shard_map/ppermute | solution.py:739
  31.1 2.6 %shard_map.132 = (bf16[4,1024,128]{2,1,0:T(8,128)(2,1)S(1)}, f32[1024,128]{1,0:T(8,128)S(1)}, bf16[1024,128]{1,0:T(8,128)(2,1)S(1)}, bf16[1,256,128]{2,1,0:T(8,1...) custom-call(s32[4]{0:T(128)S(1)} %pad_add_fusion.where_ref, ...), custom_call_target="tpu_custom_call" | custom-call | tf_op jit(solution)/shard_map/pallas_call | solution.py:712
  33.8 3.9 %collective-permute-start.12 = (bf16[1,256,128]{2,1,0:T(8,128)(2,1)S(1)}, bf16[1,256,128]{2,1,0:T(8,128)(2,1)S(1)}, u32[]{:S(2)}, u32[]{:S(2)}) collective-permute-start(bf16[1,256,128]{2,1,0:T(8,128)(2,1)S(1)} %get-tuple-element.66.refs_8_), channel_id=1, source_target_pairs={{0,28},{1,25},{2,30},{3,27},{4,24},{5,29},{6,26},{7,31},{8,20},{9,... | collective-permute-start | bytes 196616 | tf_op jit(solution)/shard_map/ppermute | solution.py:768
  37.7 1.5 %collective-permute-start.14 = (bf16[1,256,128]{2,1,0:T(8,128)(2,1)S(1)}, bf16[1,256,128]{2,1,0:T(8,128)(2,1)S(1)}, u32[]{:S(2)}, u32[]{:S(2)}) collective-permute-start(bf16[1,256,128]{2,1,0:T(8,128)(2,1)S(1)} %get-tuple-element.66.refs_8_), channel_id=1, source_target_pairs={{0,8},{1,13},{2,10},{3,15},{4,12},{5,9},{6,14},{7,11},{8,0},{9,5},... | collective-permute-start | bytes 196616 | tf_op jit(solution)/shard_map/ppermute | solution.py:768
  39.2 0.5 collective-permute-start.15
  39.7 3.0 %shard_map.133 = (bf16[32,4096]{1,0:T(8,128)(2,1)S(1)}, f32[32,4096]{1,0:T(8,128)S(1)}, bf16[4,1152,384]{2,1,0:T(8,128)(2,1)S(1)}) custom-call(bf16[9,32,128]{2,1,0:T(8,128)(2,1)S(1)} %copy-done.2, f32[5,128,128]{2,1,0:T(8,128)S(1)} %get-tuple-element.68.ring, bf16[4,1152,384]{2,1,0:T(8,128)(2,1)S(1)} %get-tuple-element.69.x3_in), custom_call_target="tpu_custom_call", output_to_operand_aliasing={{2}: (2, {})} | custom-call | tf_op jit(solution)/shard_map/pallas_call | solution.py:712
  42.7 0.6 collective-permute-done.15.refs_12_
  43.3 0.6 collective-permute-done.13.refs_10_
  44.9 0.9 %collective-permute-done.19.refs_16_ = bf16[1,128,128]{2,1,0:T(8,128)(2,1)S(1)} collective-permute-done((bf16[1,128,128]{2,1,0:T(8,128)(2,1)S(1)}, bf16[1,128,128]{2,1,0:T(8,128)(2,1)S(1)}, u32[]{:S(2)}, u32[]{:S(2)}) %collective-permute-start.19) | collective-permute-done | bytes 32800 | tf_op jit(solution)/shard_map/ppermute | solution.py:739
  45.8 7.3 %shard_map.134 = (bf16[32,4096]{1,0:T(8,128)(2,1)}, bf16[768,128]{1,0:T(8,128)(2,1)S(1)}) custom-call(s32[8,8]{1,0:T(8,128)S(1)} %fusion.3.codes_ref, s32[4]{0:T(128)S(1)} %pad_add_fusion.where_ref, bf16[1024,128]{1,0:T(8,128)(2,1)S(1)} %get-tuple-element.63.act2_ref, f32[1024,128]{1,0:T(8,128)S(1)} %get-tuple-element.64.slope2_ref, ...), custom_call_target="tpu_custom_call" | custom-call | tf_op jit(solution)/shard_map/pallas_call | solution.py:712
  53.1 12.7 %all_to_all.10.in_ref = bf16[8,96,128]{2,1,0:T(8,128)(2,1)S(1)} all-to-all(bf16[8,96,128]{2,1,0:T(8,128)(2,1)S(1)} %bitcast.19), channel_id=1, replica_groups=mesh['tile'=8,'chan'=4] {'tile'}, dimensions={0} | all-to-all | bytes 393216 | tf_op jit(solution)/shard_map/all_to_all | solution.py:775
  65.8 10.7 %all_to_all.11 = bf16[8,96,128]{2,1,0:T(8,128)(2,1)S(1)} all-to-all(bf16[8,96,128]{2,1,0:T(8,128)(2,1)S(1)} %broadcast_in_dim.12), channel_id=1, replica_groups=mesh['tile'=8,'chan'=4] {'tile'}, dimensions={0} | all-to-all | bytes 393216 | tf_op jit(solution)/shard_map/all_to_all | solution.py:775
  76.5 0.7 shard_map.136
  (35 shorter events, 2.5 us)
Async XLA Ops:
  0.6 39.0 %copy-start.2 = (bf16[9,32,128]{2,1,0:T(8,128)(2,1)S(1)}, bf16[9,32,128]{2,1,0:T(8,128)(2,1)}, u32[]{:S(2)}) copy-start(bf16[9,32,128]{2,1,0:T(8,128)(2,1)} %w1_ref.1) | copy-start | bytes 221188
  3.6 19.3 %collective-permute-start.4 = (bf16[55,32,128]{2,1,0:T(8,128)(2,1)}, bf16[55,32,128]{2,1,0:T(8,128)(2,1)S(1)}, u32[]{:S(2)}, u32[]{:S(2)}) collective-permute-start(bf16[55,32,128]{2,1,0:T(8,128)(2,1)} %get-tuple-element.47.pack_ref), channel_id=1, source_target_pairs={{0,2},{1,3},{2,0},{3,1},{4,6},{5,7},{6,4},{7,5},{8,10},{9,11},{10,... | collective-permute-start | bytes 1351688 | tf_op jit(solution)/shard_map/ppermute | solution.py:739
  6.6 5.3 %collective-permute-start = (bf16[1,5,32,128]{3,2,1,0:T(8,128)(2,1)}, bf16[1,5,32,128]{3,2,1,0:T(8,128)(2,1)S(1)}, u32[]{:S(2)}, u32[]{:S(2)}) collective-permute-start(bf16[1,5,32,128]{3,2,1,0:T(8,128)(2,1)} %get-tuple-element.46.rims_ref), channel_id=1, source_target_pairs={{0,16},{4,20},{8,24},{12,28},{16,0},{20,4},{24,8},{28,12},{1,17},{... | collective-permute-start | bytes 122888 | tf_op jit(solution)/shard_map/ppermute | solution.py:739
  9.2 8.4 %collective-permute-start.2 = (bf16[1,5,32,128]{3,2,1,0:T(8,128)(2,1)}, bf16[1,5,32,128]{3,2,1,0:T(8,128)(2,1)S(1)}, u32[]{:S(2)}, u32[]{:S(2)}) collective-permute-start(bf16[1,5,32,128]{3,2,1,0:T(8,128)(2,1)} %get-tuple-element.46.rims_ref), channel_id=1, source_target_pairs={{0,8},{4,12},{8,0},{12,4},{16,24},{20,28},{24,16},{28,20},{1,9},{5... | collective-permute-start | bytes 122888 | tf_op jit(solution)/shard_map/ppermute | solution.py:739
  10.8 12.9 %collective-permute-start.3 = (bf16[55,32,128]{2,1,0:T(8,128)(2,1)}, bf16[55,32,128]{2,1,0:T(8,128)(2,1)S(1)}, u32[]{:S(2)}, u32[]{:S(2)}) collective-permute-start(bf16[55,32,128]{2,1,0:T(8,128)(2,1)} %get-tuple-element.47.pack_ref), channel_id=1, source_target_pairs={{0,1},{1,0},{2,3},{3,2},{4,5},{5,4},{6,7},{7,6},{8,9},{9,8},{10,11... | collective-permute-start | bytes 1351688 | tf_op jit(solution)/shard_map/ppermute | solution.py:739
  11.8 5.8 %collective-permute-start.1 = (bf16[1,5,32,128]{3,2,1,0:T(8,128)(2,1)S(1)}, bf16[1,5,32,128]{3,2,1,0:T(8,128)(2,1)S(1)}, u32[]{:S(2)}, u32[]{:S(2)}) collective-permute-start(bf16[1,5,32,128]{3,2,1,0:T(8,128)(2,1)S(1)} %collective-permute-done.far_ref), channel_id=1, source_target_pairs={{0,8},{4,12},{8,0},{12,4},{16,24},{20,28},{24,16},{28,20},{1,9},{5... | collective-permute-start | bytes 122888 | tf_op jit(solution)/shard_map/ppermute | solution.py:739
  13.3 1.0 %copy-start.1 = (bf16[55,32,128]{2,1,0:T(8,128)(2,1)S(1)}, bf16[55,32,128]{2,1,0:T(8,128)(2,1)}, u32[]{:S(2)}) copy-start(bf16[55,32,128]{2,1,0:T(8,128)(2,1)} %get-tuple-element.47.pack_ref) | copy-start | bytes 1351684
  14.4 0.8 %copy-start.4 = (bf16[8,32,128]{2,1,0:T(8,128)(2,1)S(1)}, bf16[8,32,128]{2,1,0:T(8,128)(2,1)}, u32[]{:S(2)}) copy-start(bf16[8,32,128]{2,1,0:T(8,128)(2,1)} %get-tuple-element.48.pooled_ref) | copy-start | bytes 196612
  15.2 0.8 %copy-start.5 = (bf16[1,5,32,128]{3,2,1,0:T(8,128)(2,1)S(1)}, bf16[1,5,32,128]{3,2,1,0:T(8,128)(2,1)}, u32[]{:S(2)}) copy-start(bf16[1,5,32,128]{3,2,1,0:T(8,128)(2,1)} %get-tuple-element.46.rims_ref) | copy-start | bytes 122884
  16.0 6.1 %collective-permute-start.5 = (bf16[2,5,32,128]{3,2,1,0:T(8,128)(2,1)S(1)}, bf16[2,5,32,128]{3,2,1,0:T(8,128)(2,1)S(1)}, u32[]{:S(2)}, u32[]{:S(2)}) collective-permute-start(bf16[2,5,32,128]{3,2,1,0:T(8,128)(2,1)S(1)} %get-tuple-element.53.refs_0_), channel_id=1, source_target_pairs={{0,4},{4,0},{8,12},{12,8},{16,20},{20,16},{24,28},{28,24},{1,5},{5... | collective-permute-start | bytes 245768 | tf_op jit(solution)/shard_map/ppermute | solution.py:739
  17.6 4.0 %collective-permute-start.6 = (bf16[1,5,32,128]{3,2,1,0:T(8,128)(2,1)S(1)}, bf16[1,5,32,128]{3,2,1,0:T(8,128)(2,1)S(1)}, u32[]{:S(2)}, u32[]{:S(2)}) collective-permute-start(bf16[1,5,32,128]{3,2,1,0:T(8,128)(2,1)S(1)} %collective-permute-done.2.refs_1_), channel_id=1, source_target_pairs={{0,4},{4,0},{8,12},{12,8},{16,20},{20,16},{24,28},{28,24},{1,5},{5... | collective-permute-start | bytes 122888 | tf_op jit(solution)/shard_map/ppermute | solution.py:739
  18.1 4.0 %collective-permute-start.7 = (bf16[1,5,32,128]{3,2,1,0:T(8,128)(2,1)S(1)}, bf16[1,5,32,128]{3,2,1,0:T(8,128)(2,1)S(1)}, u32[]{:S(2)}, u32[]{:S(2)}) collective-permute-start(bf16[1,5,32,128]{3,2,1,0:T(8,128)(2,1)S(1)} %collective-permute-done.1.refs_2_), channel_id=1, source_target_pairs={{0,4},{4,0},{8,12},{12,8},{16,20},{20,16},{24,28},{28,24},{1,5},{5... | collective-permute-start | bytes 122888 | tf_op jit(solution)/shard_map/ppermute | solution.py:739
  22.8 1.9 %collective-permute-start.8 = (bf16[55,32,128]{2,1,0:T(8,128)(2,1)S(1)}, bf16[55,32,128]{2,1,0:T(8,128)(2,1)S(1)}, u32[]{:S(2)}, u32[]{:S(2)}) collective-permute-start(bf16[55,32,128]{2,1,0:T(8,128)(2,1)S(1)} %collective-permute-done.4.refs_2_), channel_id=1, source_target_pairs={{0,1},{1,0},{2,3},{3,2},{4,5},{5,4},{6,7},{7,6},{8,9},{9,8},{10,11... | collective-permute-start | bytes 1351688 | tf_op jit(solution)/shard_map/ppermute | solution.py:739
  22.9 6.8 %collective-permute-start.10 = (bf16[21,32,128]{2,1,0:T(8,128)(2,1)S(1)}, bf16[21,32,128]{2,1,0:T(8,128)(2,1)S(1)}, u32[]{:S(2)}, u32[]{:S(2)}) collective-permute-start(bf16[21,32,128]{2,1,0:T(8,128)(2,1)S(1)} %shard_map.130.refs_0_.refs_4_), channel_id=1, source_target_pairs={{0,2},{1,3},{2,0},{3,1},{4,6},{5,7},{6,4},{7,5},{8,10},{9,11},{10,... | collective-permute-start | bytes 516104 | tf_op jit(solution)/shard_map/ppermute | solution.py:739
  23.5 6.2 %collective-permute-start.9 = (bf16[21,32,128]{2,1,0:T(8,128)(2,1)S(1)}, bf16[21,32,128]{2,1,0:T(8,128)(2,1)S(1)}, u32[]{:S(2)}, u32[]{:S(2)}) collective-permute-start(bf16[21,32,128]{2,1,0:T(8,128)(2,1)S(1)} %shard_map.130.refs_0_.refs_4_), channel_id=1, source_target_pairs={{0,1},{1,0},{2,3},{3,2},{4,5},{5,4},{6,7},{7,6},{8,9},{9,8},{10,11... | collective-permute-start | bytes 516104 | tf_op jit(solution)/shard_map/ppermute | solution.py:739
  29.7 1.4 %collective-permute-start.11 = (bf16[21,32,128]{2,1,0:T(8,128)(2,1)S(1)}, bf16[21,32,128]{2,1,0:T(8,128)(2,1)S(1)}, u32[]{:S(2)}, u32[]{:S(2)}) collective-permute-start(bf16[21,32,128]{2,1,0:T(8,128)(2,1)S(1)} %collective-permute-done.10.refs_2_.refs_6_), channel_id=1, source_target_pairs={{0,1},{1,0},{2,3},{3,2},{4,5},{5,4},{6,7},{7,6},{8,9},{9,8},{10,11... | collective-permute-start | bytes 516104 | tf_op jit(solution)/shard_map/ppermute | solution.py:739
  31.1 14.6 %copy-start = (bf16[512,512]{1,0:T(8,128)(2,1)S(1)}, bf16[512,512]{1,0:T(8,128)(2,1)}, u32[]{:S(2)}) copy-start(bf16[512,512]{1,0:T(8,128)(2,1)} %constant.21.clone.m_ref) | copy-start | bytes 1572868
  31.1 14.6 %copy-start.3 = (bf16[32,4096]{1,0:T(8,128)(2,1)S(1)}, bf16[32,4096]{1,0:T(8,128)(2,1)}, u32[]{:S(2)}) copy-start(bf16[32,4096]{1,0:T(8,128)(2,1)} %get-tuple-element.75.og_ref) | copy-start | bytes 786436
  33.8 9.5 %collective-permute-start.12 = (bf16[1,256,128]{2,1,0:T(8,128)(2,1)S(1)}, bf16[1,256,128]{2,1,0:T(8,128)(2,1)S(1)}, u32[]{:S(2)}, u32[]{:S(2)}) collective-permute-start(bf16[1,256,128]{2,1,0:T(8,128)(2,1)S(1)} %get-tuple-element.66.refs_8_), channel_id=1, source_target_pairs={{0,28},{1,25},{2,30},{3,27},{4,24},{5,29},{6,26},{7,31},{8,20},{9,... | collective-permute-start | bytes 196616 | tf_op jit(solution)/shard_map/ppermute | solution.py:768
  37.7 6.2 %collective-permute-start.13 = (bf16[1,256,128]{2,1,0:T(8,128)(2,1)S(1)}, bf16[1,256,128]{2,1,0:T(8,128)(2,1)S(1)}, u32[]{:S(2)}, u32[]{:S(2)}) collective-permute-start(bf16[1,256,128]{2,1,0:T(8,128)(2,1)S(1)} %get-tuple-element.66.refs_8_), channel_id=1, source_target_pairs={{0,16},{1,21},{2,18},{3,23},{4,20},{5,17},{6,22},{7,19},{8,24},{9,... | collective-permute-start | bytes 196616 | tf_op jit(solution)/shard_map/ppermute | solution.py:768
  37.7 6.2 %collective-permute-start.14 = (bf16[1,256,128]{2,1,0:T(8,128)(2,1)S(1)}, bf16[1,256,128]{2,1,0:T(8,128)(2,1)S(1)}, u32[]{:S(2)}, u32[]{:S(2)}) collective-permute-start(bf16[1,256,128]{2,1,0:T(8,128)(2,1)S(1)} %get-tuple-element.66.refs_8_), channel_id=1, source_target_pairs={{0,8},{1,13},{2,10},{3,15},{4,12},{5,9},{6,14},{7,11},{8,0},{9,5},... | collective-permute-start | bytes 196616 | tf_op jit(solution)/shard_map/ppermute | solution.py:768
  39.2 4.1 %collective-permute-start.15 = (bf16[1,128,128]{2,1,0:T(8,128)(2,1)S(1)}, bf16[1,128,128]{2,1,0:T(8,128)(2,1)S(1)}, u32[]{:S(2)}, u32[]{:S(2)}) collective-permute-start(bf16[1,128,128]{2,1,0:T(8,128)(2,1)S(1)} %get-tuple-element.67), channel_id=1, source_target_pairs={{0,4},{4,0},{8,12},{12,8},{16,20},{20,16},{24,28},{28,24},{1,5},{5... | collective-permute-start | bytes 98312 | tf_op jit(solution)/shard_map/ppermute | solution.py:739
  43.8 1.9 %collective-permute-start.16 = (bf16[1,256,128]{2,1,0:T(8,128)(2,1)S(1)}, bf16[1,256,128]{2,1,0:T(8,128)(2,1)S(1)}, u32[]{:S(2)}, u32[]{:S(2)}) collective-permute-start(bf16[1,256,128]{2,1,0:T(8,128)(2,1)S(1)} %collective-permute-done.12.refs_9_), channel_id=1, source_target_pairs={{0,1},{1,0},{2,3},{3,2},{4,5},{5,4},{6,7},{7,6},{8,9},{9,8},{10,11... | collective-permute-start | bytes 196616 | tf_op jit(solution)/shard_map/ppermute | solution.py:739
  43.9 1.9 %collective-permute-start.17 = (bf16[1,256,128]{2,1,0:T(8,128)(2,1)S(1)}, bf16[1,256,128]{2,1,0:T(8,128)(2,1)S(1)}, u32[]{:S(2)}, u32[]{:S(2)}) collective-permute-start(bf16[1,256,128]{2,1,0:T(8,128)(2,1)S(1)} %collective-permute-done.13.refs_10_), channel_id=1, source_target_pairs={{0,1},{1,0},{2,3},{3,2},{4,5},{5,4},{6,7},{7,6},{8,9},{9,8},{10,11... | collective-permute-start | bytes 196616 | tf_op jit(solution)/shard_map/ppermute | solution.py:739
  44.4 1.4 %collective-permute-start.18 = (bf16[1,256,128]{2,1,0:T(8,128)(2,1)S(1)}, bf16[1,256,128]{2,1,0:T(8,128)(2,1)S(1)}, u32[]{:S(2)}, u32[]{:S(2)}) collective-permute-start(bf16[1,256,128]{2,1,0:T(8,128)(2,1)S(1)} %collective-permute-done.14.refs_11_), channel_id=1, source_target_pairs={{0,1},{1,0},{2,3},{3,2},{4,5},{5,4},{6,7},{7,6},{8,9},{9,8},{10,11... | collective-permute-start | bytes 196616 | tf_op jit(solution)/shard_map/ppermute | solution.py:739
  44.4 1.4 %collective-permute-start.19 = (bf16[1,128,128]{2,1,0:T(8,128)(2,1)S(1)}, bf16[1,128,128]{2,1,0:T(8,128)(2,1)S(1)}, u32[]{:S(2)}, u32[]{:S(2)}) collective-permute-start(bf16[1,128,128]{2,1,0:T(8,128)(2,1)S(1)} %collective-permute-done.15.refs_12_), channel_id=1, source_target_pairs={{0,1},{1,0},{2,3},{3,2},{4,5},{5,4},{6,7},{7,6},{8,9},{9,8},{10,11... | collective-permute-start | bytes 98312 | tf_op jit(solution)/shard_map/ppermute | solution.py:739

commit v5 on v2

--- a/solution.py
+++ b/solution.py
@@ -136,8 +136,8 @@
             ),
         ),
     )
-    place = jnp.concatenate([sort_place, rim_place], axis=1)
-    row = iota((16, 2 * BLOCK), 0)
+    place = jnp.concatenate([sort_place, rim_place], axis=1)[:, : m_ref.shape[1]]
+    row = iota(place.shape, 0)
     for group in range(BLOCK // 16):
         m_ref[group * 16 : (group + 1) * 16, :] = one_hot(row + group * 16 == place)
 
@@ -527,11 +527,10 @@
     slope1_ref,
     og_ref,
     x3_ref,
-    m_ref,
     *refs,
 ):
     packs, mores, refs = refs[:nc], refs[nc : 2 * nc], refs[2 * nc :]
-    *rims, out_ref, grad_ref, w2s, w2t, ups, pooled_all, prims, rims_all, left, right, g3pad, sums, a3, coarse, field, back = refs
+    *rims, out_ref, grad_ref, w2s, w2t, ups, pooled_all, prims, rims_all, left, right, g3pad, sums, a3, coarse, field, back, m_ref = refs
     tile, me, tile_base, base = where_ref[0], where_ref[1], where_ref[2], where_ref[3]
     own = packs[0].shape[1]
     place_conv(packs, base, 8, w2s)
@@ -665,6 +664,7 @@
     if grad_ref.shape[0] > 23 * own:
         grad_ref[23 * own :, :] = jnp.zeros((grad_ref.shape[0] - 23 * own, 128), BF16)
 
+    fill_table(m_ref)
     lifted = mm_nt(ups[own_spot, :], coarse[...])
     total = [
         own_ref[:, ph * CELLS : (ph + 1) * CELLS].astype(F32) + lifted for ph in range(4)
@@ -720,16 +720,6 @@
 
 def shape(dims, kind=BF16):
     return jax.ShapeDtypeStruct(dims, kind)
-
-
-def sort_matrix():
-    table = np.zeros((BLOCK, BLOCK), np.float32)
-    for a in range(2):
-        for b in range(2):
-            for q in range(4):
-                for k in range(HALF):
-                    table[q * 128 + a * 64 + 2 * k + b, (2 * a + b) * 128 + q * HALF + k] = 1
-    return jnp.asarray(table, BF16)
 
 
 def paired(values, axis, bit):
@@ -788,7 +778,6 @@
     scale = float((tiles * SIDE * SIDE) ** (-0.5))
     tile, chan = lax.axis_index("tile"), lax.axis_index("chan")
     where = jnp.stack([tile, chan, tile if is_split() else tile * 0, chan]).astype(jnp.int32)
-    matrix = sort_matrix()
     half = nc // 2
 
     pack, rims, sorted_g, pack2 = call(
@@ -913,7 +902,6 @@
         slope1,
         sorted_g,
         x3,
-        matrix,
         *packs2,
         *rings,
         *all_rims2,
@@ -932,6 +920,7 @@
             pltpu.VMEM((CELLS, 128), BF16),
             pltpu.VMEM((CELLS, 128), F32),
             pltpu.VMEM((128, 128), F32),
+            pltpu.VMEM((BLOCK, BLOCK), BF16),
         ],
     )
     pieces = swap(late.reshape(tiles, rows, 128))

time: 75 us -> 75 us (level)
    unnamed x12 -> x10, local copies, waits for them, and re-layouts: 1.79 us -> 1.78 us
where the time goes in v5:
time: 75 us; the launch traced here: 74.6 us
  blocking collectives  23.4 us (31%)
  starting transfers between devices  22.3 us (30%)
  Pallas kernels  21 us (28%)
  waiting for transfers between devices  3.89 us (5%)
  local copies, waits for them, and re-layouts  2.51 us (3%)
  between operations  0.78 us (1%)
    all_to_all x2, blocking collectives, swap(): return lax.all_to_all(values, 'tile', split_axis=0, concat_axis=0)  23.4 us
    pallas_call x9, Pallas kernels, call(): pl.pallas_call(kernel, out_shape=outs, in_specs=specs, out_specs=[vmem] *...  21 us
    ppermute x20, starting transfers between devices, paired(): return lax.ppermute(values, axis, [(i, i ^ bit) for i in range(count)])  17.2 us
    ppermute x3, starting transfers between devices, copies(): got.append(lax.ppermute(block, ('tile', 'chan'), perm))  5.1 us
    ppermute x20, waiting for transfers between devices, paired(): return lax.ppermute(values, axis, [(i, i ^ bit) for i in range(count)])  3.37 us
    unnamed x10, local copies, waits for them, and re-layouts  1.78 us
  transfers between devices with their start and end apart: 23, of which 7 were waited for; matrix products, arithmetic and copies ran while one was open for 2% of the time, Pallas kernels for 13%

profile of v5, /device:TPU:0, one launch (start us, length us, event | category | flops | bytes accessed | tf_op | source)
XLA Modules:
  0.0 74.6 jit_solution(10036986549767139309)
XLA Ops:
  0.6 2.9 %shard_map.119 = (bf16[45,32,128]{2,1,0:T(8,128)(2,1)}, bf16[1,5,32,128]{3,2,1,0:T(8,128)(2,1)}, bf16[32,4096]{1,0:T(8,128)(2,1)}, bf16[18,32,128]{2,1,0:T(8,128)(2,1)}) custom-call(bf16[32,4096]{1,0:T(8,128)(2,1)} %f_hbm.1, bf16[32,4096]{1,0:T(8,128)(2,1)} %g_hbm.1, bf16[9,32,128]{2,1,0:T(8,128)(2,1)} %w1_ref.1, bf16[4,32,128]{2,1,0:T(8,128)(2,1)} %wd_hbm.1, ...), custom_call_target="tpu_custom_call" | custom-call | tf_op jit(solution)/shard_map/pallas_call | solution.py:710
  3.6 4.1 %collective-permute-start = (bf16[1,5,32,128]{3,2,1,0:T(8,128)(2,1)}, bf16[1,5,32,128]{3,2,1,0:T(8,128)(2,1)S(1)}, u32[]{:S(2)}, u32[]{:S(2)}) collective-permute-start(bf16[1,5,32,128]{3,2,1,0:T(8,128)(2,1)} %get-tuple-element.51.rims_ref), channel_id=1, source_target_pairs={{0,16},{4,20},{8,24},{12,28},{16,0},{20,4},{24,8},{28,12},{1,17},{... | collective-permute-start | bytes 122888 | tf_op jit(solution)/shard_map/ppermute | solution.py:727
  7.7 1.5 %collective-permute-start.4 = (bf16[45,32,128]{2,1,0:T(8,128)(2,1)}, bf16[45,32,128]{2,1,0:T(8,128)(2,1)S(1)}, u32[]{:S(2)}, u32[]{:S(2)}) collective-permute-start(bf16[45,32,128]{2,1,0:T(8,128)(2,1)} %get-tuple-element.52.pack_ref), channel_id=1, source_target_pairs={{0,2},{1,3},{2,0},{3,1},{4,6},{5,7},{6,4},{7,5},{8,10},{9,11},{10,... | collective-permute-start | bytes 1105928 | tf_op jit(solution)/shard_map/ppermute | solution.py:727
  9.2 1.6 %collective-permute-start.2 = (bf16[1,5,32,128]{3,2,1,0:T(8,128)(2,1)}, bf16[1,5,32,128]{3,2,1,0:T(8,128)(2,1)S(1)}, u32[]{:S(2)}, u32[]{:S(2)}) collective-permute-start(bf16[1,5,32,128]{3,2,1,0:T(8,128)(2,1)} %get-tuple-element.51.rims_ref), channel_id=1, source_target_pairs={{0,8},{4,12},{8,0},{12,4},{16,24},{20,28},{24,16},{28,20},{1,9},{5... | collective-permute-start | bytes 122888 | tf_op jit(solution)/shard_map/ppermute | solution.py:727
  10.8 1.2 %collective-permute-start.1 = (bf16[1,5,32,128]{3,2,1,0:T(8,128)(2,1)S(1)}, bf16[1,5,32,128]{3,2,1,0:T(8,128)(2,1)S(1)}, u32[]{:S(2)}, u32[]{:S(2)}) collective-permute-start(bf16[1,5,32,128]{3,2,1,0:T(8,128)(2,1)S(1)} %collective-permute-done.far_ref), channel_id=1, source_target_pairs={{0,8},{4,12},{8,0},{12,4},{16,24},{20,28},{24,16},{28,20},{1,9},{5... | collective-permute-start | bytes 122888 | tf_op jit(solution)/shard_map/ppermute | solution.py:727
  12.0 1.0 %copy-done = bf16[45,32,128]{2,1,0:T(8,128)(2,1)S(1)} copy-done((bf16[45,32,128]{2,1,0:T(8,128)(2,1)S(1)}, bf16[45,32,128]{2,1,0:T(8,128)(2,1)}, u32[]{:S(2)}) %copy-start) | copy-done | bytes 368664
  13.0 0.8 %copy-done.4 = bf16[1,5,32,128]{3,2,1,0:T(8,128)(2,1)S(1)} copy-done((bf16[1,5,32,128]{3,2,1,0:T(8,128)(2,1)S(1)}, bf16[1,5,32,128]{3,2,1,0:T(8,128)(2,1)}, u32[]{:S(2)}) %copy-start.4) | copy-done | bytes 40984
  13.8 1.6 %collective-permute-start.5 = (bf16[2,5,32,128]{3,2,1,0:T(8,128)(2,1)S(1)}, bf16[2,5,32,128]{3,2,1,0:T(8,128)(2,1)S(1)}, u32[]{:S(2)}, u32[]{:S(2)}) collective-permute-start(bf16[2,5,32,128]{3,2,1,0:T(8,128)(2,1)S(1)} %get-tuple-element.57.refs_0_), channel_id=1, source_target_pairs={{0,4},{4,0},{8,12},{12,8},{16,20},{20,16},{24,28},{28,24},{1,5},{5... | collective-permute-start | bytes 245768 | tf_op jit(solution)/shard_map/ppermute | solution.py:727
  15.4 0.9 %collective-permute-start.6 = (bf16[1,5,32,128]{3,2,1,0:T(8,128)(2,1)S(1)}, bf16[1,5,32,128]{3,2,1,0:T(8,128)(2,1)S(1)}, u32[]{:S(2)}, u32[]{:S(2)}) collective-permute-start(bf16[1,5,32,128]{3,2,1,0:T(8,128)(2,1)S(1)} %collective-permute-done.2.refs_1_), channel_id=1, source_target_pairs={{0,4},{4,0},{8,12},{12,8},{16,20},{20,16},{24,28},{28,24},{1,5},{5... | collective-permute-start | bytes 122888 | tf_op jit(solution)/shard_map/ppermute | solution.py:727
  16.3 1.2 %collective-permute-start.7 = (bf16[1,5,32,128]{3,2,1,0:T(8,128)(2,1)S(1)}, bf16[1,5,32,128]{3,2,1,0:T(8,128)(2,1)S(1)}, u32[]{:S(2)}, u32[]{:S(2)}) collective-permute-start(bf16[1,5,32,128]{3,2,1,0:T(8,128)(2,1)S(1)} %collective-permute-done.1.refs_2_), channel_id=1, source_target_pairs={{0,4},{4,0},{8,12},{12,8},{16,20},{20,16},{24,28},{28,24},{1,5},{5... | collective-permute-start | bytes 122888 | tf_op jit(solution)/shard_map/ppermute | solution.py:727
  17.4 0.7 copy.14
  18.1 0.7 fusion.3.codes_ref
  18.8 0.6 collective-permute-done.6.refs_4_
  19.4 0.9 %collective-permute-done.7.refs_5_ = bf16[1,5,32,128]{3,2,1,0:T(8,128)(2,1)S(1)} collective-permute-done((bf16[1,5,32,128]{3,2,1,0:T(8,128)(2,1)S(1)}, bf16[1,5,32,128]{3,2,1,0:T(8,128)(2,1)S(1)}, u32[]{:S(2)}, u32[]{:S(2)}) %collective-permute-start.7) | collective-permute-done | bytes 40992 | tf_op jit(solution)/shard_map/ppermute | solution.py:727
  20.3 0.7 shard_map.121.refs_0_.refs_4_
  21.1 1.3 %collective-permute-start.10 = (bf16[13,32,128]{2,1,0:T(8,128)(2,1)S(1)}, bf16[13,32,128]{2,1,0:T(8,128)(2,1)S(1)}, u32[]{:S(2)}, u32[]{:S(2)}) collective-permute-start(bf16[13,32,128]{2,1,0:T(8,128)(2,1)S(1)} %shard_map.121.refs_0_.refs_4_), channel_id=1, source_target_pairs={{0,2},{1,3},{2,0},{3,1},{4,6},{5,7},{6,4},{7,5},{8,10},{9,11},{10,... | collective-permute-start | bytes 319496 | tf_op jit(solution)/shard_map/ppermute | solution.py:727
  22.8 3.6 %shard_map.122 = (bf16[4,1152,384]{2,1,0:T(8,128)(2,1)S(1)}, f32[4,1024,128]{2,1,0:T(8,128)S(1)}, bf16[1152,128]{1,0:T(8,128)(2,1)S(1)}, bf16[512,128]{1,0:T(8,128)(2,1)S(1)}) custom-call(s32[4]{0:T(128)S(1)} %pad_add_fusion.where_ref, bf16[45,32,128]{2,1,0:T(8,128)(2,1)S(1)} %get-tuple-element.56.refs_0_, ...), custom_call_target="tpu_custom_call" | custom-call | tf_op jit(solution)/shard_map/pallas_call | solution.py:710
  26.6 0.4 collective-permute-start.9
  27.1 1.3 %collective-permute-start.17 = (bf16[18,32,128]{2,1,0:T(8,128)(2,1)}, bf16[18,32,128]{2,1,0:T(8,128)(2,1)S(1)}, u32[]{:S(2)}, u32[]{:S(2)}) collective-permute-start(bf16[18,32,128]{2,1,0:T(8,128)(2,1)} %get-tuple-element.73.refs_0_), channel_id=1, source_target_pairs={{0,2},{1,3},{2,0},{3,1},{4,6},{5,7},{6,4},{7,5},{8,10},{9,11},{10,... | collective-permute-start | bytes 442376 | tf_op jit(solution)/shard_map/ppermute | solution.py:727
  28.4 2.6 %shard_map.123 = (bf16[4,1024,128]{2,1,0:T(8,128)(2,1)S(1)}, f32[1024,128]{1,0:T(8,128)S(1)}, bf16[1024,128]{1,0:T(8,128)(2,1)S(1)}, bf16[1,256,128]{2,1,0:T(8,1...) custom-call(s32[4]{0:T(128)S(1)} %pad_add_fusion.where_ref, ...), custom_call_target="tpu_custom_call" | custom-call | tf_op jit(solution)/shard_map/pallas_call | solution.py:710
  31.0 3.7 %collective-permute-start.13 = (bf16[1,256,128]{2,1,0:T(8,128)(2,1)S(1)}, bf16[1,256,128]{2,1,0:T(8,128)(2,1)S(1)}, u32[]{:S(2)}, u32[]{:S(2)}) collective-permute-start(bf16[1,256,128]{2,1,0:T(8,128)(2,1)S(1)} %get-tuple-element.74.refs_8_), channel_id=1, source_target_pairs={{0,28},{1,25},{2,30},{3,27},{4,24},{5,29},{6,26},{7,31},{8,20},{9,... | collective-permute-start | bytes 196616 | tf_op jit(solution)/shard_map/ppermute | solution.py:756
  34.7 1.4 %collective-permute-start.15 = (bf16[1,256,128]{2,1,0:T(8,128)(2,1)S(1)}, bf16[1,256,128]{2,1,0:T(8,128)(2,1)S(1)}, u32[]{:S(2)}, u32[]{:S(2)}) collective-permute-start(bf16[1,256,128]{2,1,0:T(8,128)(2,1)S(1)} %get-tuple-element.74.refs_8_), channel_id=1, source_target_pairs={{0,8},{1,13},{2,10},{3,15},{4,12},{5,9},{6,14},{7,11},{8,0},{9,5},... | collective-permute-start | bytes 196616 | tf_op jit(solution)/shard_map/ppermute | solution.py:756
  36.1 0.8 %collective-permute-start.16 = (bf16[1,128,128]{2,1,0:T(8,128)(2,1)S(1)}, bf16[1,128,128]{2,1,0:T(8,128)(2,1)S(1)}, u32[]{:S(2)}, u32[]{:S(2)}) collective-permute-start(bf16[1,128,128]{2,1,0:T(8,128)(2,1)S(1)} %get-tuple-element.75), channel_id=1, source_target_pairs={{0,4},{4,0},{8,12},{12,8},{16,20},{20,16},{24,28},{28,24},{1,5},{5... | collective-permute-start | bytes 98312 | tf_op jit(solution)/shard_map/ppermute | solution.py:727
  37.0 3.0 %shard_map.124 = (bf16[32,4096]{1,0:T(8,128)(2,1)S(1)}, f32[32,4096]{1,0:T(8,128)S(1)}, bf16[4,1152,384]{2,1,0:T(8,128)(2,1)S(1)}) custom-call(bf16[9,32,128]{2,1,0:T(8,128)(2,1)S(1)} %copy-done.1, f32[5,128,128]{2,1,0:T(8,128)S(1)} %get-tuple-element.76.ring, bf16[4,1152,384]{2,1,0:T(8,128)(2,1)S(1)} %get-tuple-element.77.x3_in), custom_call_target="tpu_custom_call", output_to_operand_aliasing={{2}: (2, {})} | custom-call | tf_op jit(solution)/shard_map/pallas_call | solution.py:710
  40.3 0.5 collective-permute-done.14.refs_10_
  40.9 0.4 collective-permute-start.19
  41.4 0.4 collective-permute-start.21
  41.9 1.1 %collective-permute-done.22.refs_16_ = bf16[1,128,128]{2,1,0:T(8,128)(2,1)S(1)} collective-permute-done((bf16[1,128,128]{2,1,0:T(8,128)(2,1)S(1)}, bf16[1,128,128]{2,1,0:T(8,128)(2,1)S(1)}, u32[]{:S(2)}, u32[]{:S(2)}) %collective-permute-start.22) | collective-permute-done | bytes 32800 | tf_op jit(solution)/shard_map/ppermute | solution.py:727
  43.1 7.3 %shard_map.125 = (bf16[32,4096]{1,0:T(8,128)(2,1)}, bf16[768,128]{1,0:T(8,128)(2,1)S(1)}) custom-call(s32[8,8]{1,0:T(8,128)S(1)} %fusion.3.codes_ref, s32[4]{0:T(128)S(1)} %pad_add_fusion.where_ref, bf16[1024,128]{1,0:T(8,128)(2,1)S(1)} %get-tuple-element.68.act2_ref, f32[1024,128]{1,0:T(8,128)S(1)} %get-tuple-element.69.slope2_ref, ...), custom_call_target="tpu_custom_call" | custom-call | tf_op jit(solution)/shard_map/pallas_call | solution.py:710
  50.4 12.7 %all_to_all.10.in_ref = bf16[8,96,128]{2,1,0:T(8,128)(2,1)S(1)} all-to-all(bf16[8,96,128]{2,1,0:T(8,128)(2,1)S(1)} %bitcast.19), channel_id=1, replica_groups=mesh['tile'=8,'chan'=4] {'tile'}, dimensions={0} | all-to-all | bytes 393216 | tf_op jit(solution)/shard_map/all_to_all | solution.py:763
  63.1 10.7 %all_to_all.11 = bf16[8,96,128]{2,1,0:T(8,128)(2,1)S(1)} all-to-all(bf16[8,96,128]{2,1,0:T(8,128)(2,1)S(1)} %broadcast_in_dim.12), channel_id=1, replica_groups=mesh['tile'=8,'chan'=4] {'tile'}, dimensions={0} | all-to-all | bytes 393216 | tf_op jit(solution)/shard_map/all_to_all | solution.py:763
  73.9 0.7 %shard_map.127 = (f32[9,32,128]{2,1,0:T(8,128)}, f32[4,32,128]{2,1,0:T(8,128)}, f32[9,32,128]{2,1,0:T(8,128)}, f32[32,128]{1,0:T(8,128)}) custom-call(bf16[768,128]{1,0:T(8,128)(2,1)S(1)} %bitcast.18), custom_call_target="tpu_custom_call" | custom-call | tf_op jit(solution)/shard_map/pallas_call | solution.py:710
  (39 shorter events, 1.4 us)
Async XLA Ops:
  0.6 36.3 %copy-start.1 = (bf16[9,32,128]{2,1,0:T(8,128)(2,1)S(1)}, bf16[9,32,128]{2,1,0:T(8,128)(2,1)}, u32[]{:S(2)}) copy-start(bf16[9,32,128]{2,1,0:T(8,128)(2,1)} %w1_ref.1) | copy-start | bytes 221188
  3.6 7.2 %collective-permute-start = (bf16[1,5,32,128]{3,2,1,0:T(8,128)(2,1)}, bf16[1,5,32,128]{3,2,1,0:T(8,128)(2,1)S(1)}, u32[]{:S(2)}, u32[]{:S(2)}) collective-permute-start(bf16[1,5,32,128]{3,2,1,0:T(8,128)(2,1)} %get-tuple-element.51.rims_ref), channel_id=1, source_target_pairs={{0,16},{4,20},{8,24},{12,28},{16,0},{20,4},{24,8},{28,12},{1,17},{... | collective-permute-start | bytes 122888 | tf_op jit(solution)/shard_map/ppermute | solution.py:727
  7.7 13.3 %collective-permute-start.4 = (bf16[45,32,128]{2,1,0:T(8,128)(2,1)}, bf16[45,32,128]{2,1,0:T(8,128)(2,1)S(1)}, u32[]{:S(2)}, u32[]{:S(2)}) collective-permute-start(bf16[45,32,128]{2,1,0:T(8,128)(2,1)} %get-tuple-element.52.pack_ref), channel_id=1, source_target_pairs={{0,2},{1,3},{2,0},{3,1},{4,6},{5,7},{6,4},{7,5},{8,10},{9,11},{10,... | collective-permute-start | bytes 1105928 | tf_op jit(solution)/shard_map/ppermute | solution.py:727
  9.2 6.2 %collective-permute-start.2 = (bf16[1,5,32,128]{3,2,1,0:T(8,128)(2,1)}, bf16[1,5,32,128]{3,2,1,0:T(8,128)(2,1)S(1)}, u32[]{:S(2)}, u32[]{:S(2)}) collective-permute-start(bf16[1,5,32,128]{3,2,1,0:T(8,128)(2,1)} %get-tuple-element.51.rims_ref), channel_id=1, source_target_pairs={{0,8},{4,12},{8,0},{12,4},{16,24},{20,28},{24,16},{28,20},{1,9},{5... | collective-permute-start | bytes 122888 | tf_op jit(solution)/shard_map/ppermute | solution.py:727
  10.8 11.7 %collective-permute-start.3 = (bf16[45,32,128]{2,1,0:T(8,128)(2,1)}, bf16[45,32,128]{2,1,0:T(8,128)(2,1)S(1)}, u32[]{:S(2)}, u32[]{:S(2)}) collective-permute-start(bf16[45,32,128]{2,1,0:T(8,128)(2,1)} %get-tuple-element.52.pack_ref), channel_id=1, source_target_pairs={{0,1},{1,0},{2,3},{3,2},{4,5},{5,4},{6,7},{7,6},{8,9},{9,8},{10,11... | collective-permute-start | bytes 1105928 | tf_op jit(solution)/shard_map/ppermute | solution.py:727
  10.8 4.7 %collective-permute-start.1 = (bf16[1,5,32,128]{3,2,1,0:T(8,128)(2,1)S(1)}, bf16[1,5,32,128]{3,2,1,0:T(8,128)(2,1)S(1)}, u32[]{:S(2)}, u32[]{:S(2)}) collective-permute-start(bf16[1,5,32,128]{3,2,1,0:T(8,128)(2,1)S(1)} %collective-permute-done.far_ref), channel_id=1, source_target_pairs={{0,8},{4,12},{8,0},{12,4},{16,24},{20,28},{24,16},{28,20},{1,9},{5... | collective-permute-start | bytes 122888 | tf_op jit(solution)/shard_map/ppermute | solution.py:727
  12.0 1.0 %copy-start = (bf16[45,32,128]{2,1,0:T(8,128)(2,1)S(1)}, bf16[45,32,128]{2,1,0:T(8,128)(2,1)}, u32[]{:S(2)}) copy-start(bf16[45,32,128]{2,1,0:T(8,128)(2,1)} %get-tuple-element.52.pack_ref) | copy-start | bytes 1105924
  13.0 0.8 %copy-start.4 = (bf16[1,5,32,128]{3,2,1,0:T(8,128)(2,1)S(1)}, bf16[1,5,32,128]{3,2,1,0:T(8,128)(2,1)}, u32[]{:S(2)}) copy-start(bf16[1,5,32,128]{3,2,1,0:T(8,128)(2,1)} %get-tuple-element.51.rims_ref) | copy-start | bytes 122884
  13.8 6.5 %collective-permute-start.5 = (bf16[2,5,32,128]{3,2,1,0:T(8,128)(2,1)S(1)}, bf16[2,5,32,128]{3,2,1,0:T(8,128)(2,1)S(1)}, u32[]{:S(2)}, u32[]{:S(2)}) collective-permute-start(bf16[2,5,32,128]{3,2,1,0:T(8,128)(2,1)S(1)} %get-tuple-element.57.refs_0_), channel_id=1, source_target_pairs={{0,4},{4,0},{8,12},{12,8},{16,20},{20,16},{24,28},{28,24},{1,5},{5... | collective-permute-start | bytes 245768 | tf_op jit(solution)/shard_map/ppermute | solution.py:727
  15.4 4.0 %collective-permute-start.6 = (bf16[1,5,32,128]{3,2,1,0:T(8,128)(2,1)S(1)}, bf16[1,5,32,128]{3,2,1,0:T(8,128)(2,1)S(1)}, u32[]{:S(2)}, u32[]{:S(2)}) collective-permute-start(bf16[1,5,32,128]{3,2,1,0:T(8,128)(2,1)S(1)} %collective-permute-done.2.refs_1_), channel_id=1, source_target_pairs={{0,4},{4,0},{8,12},{12,8},{16,20},{20,16},{24,28},{28,24},{1,5},{5... | collective-permute-start | bytes 122888 | tf_op jit(solution)/shard_map/ppermute | solution.py:727
  16.3 4.0 %collective-permute-start.7 = (bf16[1,5,32,128]{3,2,1,0:T(8,128)(2,1)S(1)}, bf16[1,5,32,128]{3,2,1,0:T(8,128)(2,1)S(1)}, u32[]{:S(2)}, u32[]{:S(2)}) collective-permute-start(bf16[1,5,32,128]{3,2,1,0:T(8,128)(2,1)S(1)} %collective-permute-done.1.refs_2_), channel_id=1, source_target_pairs={{0,4},{4,0},{8,12},{12,8},{16,20},{20,16},{24,28},{28,24},{1,5},{5... | collective-permute-start | bytes 122888 | tf_op jit(solution)/shard_map/ppermute | solution.py:727
  21.0 1.8 %collective-permute-start.8 = (bf16[45,32,128]{2,1,0:T(8,128)(2,1)S(1)}, bf16[45,32,128]{2,1,0:T(8,128)(2,1)S(1)}, u32[]{:S(2)}, u32[]{:S(2)}) collective-permute-start(bf16[45,32,128]{2,1,0:T(8,128)(2,1)S(1)} %collective-permute-done.4.refs_2_), channel_id=1, source_target_pairs={{0,1},{1,0},{2,3},{3,2},{4,5},{5,4},{6,7},{7,6},{8,9},{9,8},{10,11... | collective-permute-start | bytes 1105928 | tf_op jit(solution)/shard_map/ppermute | solution.py:727
  21.1 5.4 %collective-permute-start.10 = (bf16[13,32,128]{2,1,0:T(8,128)(2,1)S(1)}, bf16[13,32,128]{2,1,0:T(8,128)(2,1)S(1)}, u32[]{:S(2)}, u32[]{:S(2)}) collective-permute-start(bf16[13,32,128]{2,1,0:T(8,128)(2,1)S(1)} %shard_map.121.refs_0_.refs_4_), channel_id=1, source_target_pairs={{0,2},{1,3},{2,0},{3,1},{4,6},{5,7},{6,4},{7,5},{8,10},{9,11},{10,... | collective-permute-start | bytes 319496 | tf_op jit(solution)/shard_map/ppermute | solution.py:727
  26.4 16.7 %copy-start.2 = (bf16[32,4096]{1,0:T(8,128)(2,1)S(1)}, bf16[32,4096]{1,0:T(8,128)(2,1)}, u32[]{:S(2)}) copy-start(bf16[32,4096]{1,0:T(8,128)(2,1)} %get-tuple-element.83.og_ref) | copy-start | bytes 786436
  26.4 16.7 %copy-start.3 = (bf16[18,32,128]{2,1,0:T(8,128)(2,1)S(1)}, bf16[18,32,128]{2,1,0:T(8,128)(2,1)}, u32[]{:S(2)}) copy-start(bf16[18,32,128]{2,1,0:T(8,128)(2,1)} %get-tuple-element.73.refs_0_) | copy-start | bytes 442372
  26.5 4.6 %collective-permute-start.12 = (bf16[18,32,128]{2,1,0:T(8,128)(2,1)}, bf16[18,32,128]{2,1,0:T(8,128)(2,1)S(1)}, u32[]{:S(2)}, u32[]{:S(2)}) collective-permute-start(bf16[18,32,128]{2,1,0:T(8,128)(2,1)} %get-tuple-element.73.refs_0_), channel_id=1, source_target_pairs={{0,1},{1,0},{2,3},{3,2},{4,5},{5,4},{6,7},{7,6},{8,9},{9,8},{10,11... | collective-permute-start | bytes 442376 | tf_op jit(solution)/shard_map/ppermute | solution.py:727
  26.6 1.8 %collective-permute-start.9 = (bf16[13,32,128]{2,1,0:T(8,128)(2,1)S(1)}, bf16[13,32,128]{2,1,0:T(8,128)(2,1)S(1)}, u32[]{:S(2)}, u32[]{:S(2)}) collective-permute-start(bf16[13,32,128]{2,1,0:T(8,128)(2,1)S(1)} %shard_map.121.refs_0_.refs_4_), channel_id=1, source_target_pairs={{0,1},{1,0},{2,3},{3,2},{4,5},{5,4},{6,7},{7,6},{8,9},{9,8},{10,11... | collective-permute-start | bytes 319496 | tf_op jit(solution)/shard_map/ppermute | solution.py:727
  27.0 1.4 %collective-permute-start.11 = (bf16[13,32,128]{2,1,0:T(8,128)(2,1)S(1)}, bf16[13,32,128]{2,1,0:T(8,128)(2,1)S(1)}, u32[]{:S(2)}, u32[]{:S(2)}) collective-permute-start(bf16[13,32,128]{2,1,0:T(8,128)(2,1)S(1)} %collective-permute-done.10.refs_2_.refs_6_), channel_id=1, source_target_pairs={{0,1},{1,0},{2,3},{3,2},{4,5},{5,4},{6,7},{7,6},{8,9},{9,8},{10,11... | collective-permute-start | bytes 319496 | tf_op jit(solution)/shard_map/ppermute | solution.py:727
  27.1 12.9 %collective-permute-start.17 = (bf16[18,32,128]{2,1,0:T(8,128)(2,1)}, bf16[18,32,128]{2,1,0:T(8,128)(2,1)S(1)}, u32[]{:S(2)}, u32[]{:S(2)}) collective-permute-start(bf16[18,32,128]{2,1,0:T(8,128)(2,1)} %get-tuple-element.73.refs_0_), channel_id=1, source_target_pairs={{0,2},{1,3},{2,0},{3,1},{4,6},{5,7},{6,4},{7,5},{8,10},{9,11},{10,... | collective-permute-start | bytes 442376 | tf_op jit(solution)/shard_map/ppermute | solution.py:727
  31.0 9.3 %collective-permute-start.13 = (bf16[1,256,128]{2,1,0:T(8,128)(2,1)S(1)}, bf16[1,256,128]{2,1,0:T(8,128)(2,1)S(1)}, u32[]{:S(2)}, u32[]{:S(2)}) collective-permute-start(bf16[1,256,128]{2,1,0:T(8,128)(2,1)S(1)} %get-tuple-element.74.refs_8_), channel_id=1, source_target_pairs={{0,28},{1,25},{2,30},{3,27},{4,24},{5,29},{6,26},{7,31},{8,20},{9,... | collective-permute-start | bytes 196616 | tf_op jit(solution)/shard_map/ppermute | solution.py:756
  34.7 6.1 %collective-permute-start.14 = (bf16[1,256,128]{2,1,0:T(8,128)(2,1)S(1)}, bf16[1,256,128]{2,1,0:T(8,128)(2,1)S(1)}, u32[]{:S(2)}, u32[]{:S(2)}) collective-permute-start(bf16[1,256,128]{2,1,0:T(8,128)(2,1)S(1)} %get-tuple-element.74.refs_8_), channel_id=1, source_target_pairs={{0,16},{1,21},{2,18},{3,23},{4,20},{5,17},{6,22},{7,19},{8,24},{9,... | collective-permute-start | bytes 196616 | tf_op jit(solution)/shard_map/ppermute | solution.py:756
  34.7 6.1 %collective-permute-start.15 = (bf16[1,256,128]{2,1,0:T(8,128)(2,1)S(1)}, bf16[1,256,128]{2,1,0:T(8,128)(2,1)S(1)}, u32[]{:S(2)}, u32[]{:S(2)}) collective-permute-start(bf16[1,256,128]{2,1,0:T(8,128)(2,1)S(1)} %get-tuple-element.74.refs_8_), channel_id=1, source_target_pairs={{0,8},{1,13},{2,10},{3,15},{4,12},{5,9},{6,14},{7,11},{8,0},{9,5},... | collective-permute-start | bytes 196616 | tf_op jit(solution)/shard_map/ppermute | solution.py:756
  36.1 4.2 %collective-permute-start.16 = (bf16[1,128,128]{2,1,0:T(8,128)(2,1)S(1)}, bf16[1,128,128]{2,1,0:T(8,128)(2,1)S(1)}, u32[]{:S(2)}, u32[]{:S(2)}) collective-permute-start(bf16[1,128,128]{2,1,0:T(8,128)(2,1)S(1)} %get-tuple-element.75), channel_id=1, source_target_pairs={{0,4},{4,0},{8,12},{12,8},{16,20},{20,16},{24,28},{28,24},{1,5},{5... | collective-permute-start | bytes 98312 | tf_op jit(solution)/shard_map/ppermute | solution.py:727
  40.8 2.2 %collective-permute-start.18 = (bf16[18,32,128]{2,1,0:T(8,128)(2,1)S(1)}, bf16[18,32,128]{2,1,0:T(8,128)(2,1)S(1)}, u32[]{:S(2)}, u32[]{:S(2)}) collective-permute-start(bf16[18,32,128]{2,1,0:T(8,128)(2,1)S(1)} %collective-permute-done.17.refs_2_), channel_id=1, source_target_pairs={{0,1},{1,0},{2,3},{3,2},{4,5},{5,4},{6,7},{7,6},{8,9},{9,8},{10,11... | collective-permute-start | bytes 442376 | tf_op jit(solution)/shard_map/ppermute | solution.py:727
  40.9 2.2 %collective-permute-start.19 = (bf16[1,256,128]{2,1,0:T(8,128)(2,1)S(1)}, bf16[1,256,128]{2,1,0:T(8,128)(2,1)S(1)}, u32[]{:S(2)}, u32[]{:S(2)}) collective-permute-start(bf16[1,256,128]{2,1,0:T(8,128)(2,1)S(1)} %collective-permute-done.13.refs_9_), channel_id=1, source_target_pairs={{0,1},{1,0},{2,3},{3,2},{4,5},{5,4},{6,7},{7,6},{8,9},{9,8},{10,11... | collective-permute-start | bytes 196616 | tf_op jit(solution)/shard_map/ppermute | solution.py:727
  41.3 1.7 %collective-permute-start.20 = (bf16[1,256,128]{2,1,0:T(8,128)(2,1)S(1)}, bf16[1,256,128]{2,1,0:T(8,128)(2,1)S(1)}, u32[]{:S(2)}, u32[]{:S(2)}) collective-permute-start(bf16[1,256,128]{2,1,0:T(8,128)(2,1)S(1)} %collective-permute-done.14.refs_10_), channel_id=1, source_target_pairs={{0,1},{1,0},{2,3},{3,2},{4,5},{5,4},{6,7},{7,6},{8,9},{9,8},{10,11... | collective-permute-start | bytes 196616 | tf_op jit(solution)/shard_map/ppermute | solution.py:727
  41.4 1.7 %collective-permute-start.21 = (bf16[1,256,128]{2,1,0:T(8,128)(2,1)S(1)}, bf16[1,256,128]{2,1,0:T(8,128)(2,1)S(1)}, u32[]{:S(2)}, u32[]{:S(2)}) collective-permute-start(bf16[1,256,128]{2,1,0:T(8,128)(2,1)S(1)} %collective-permute-done.15.refs_11_), channel_id=1, source_target_pairs={{0,1},{1,0},{2,3},{3,2},{4,5},{5,4},{6,7},{7,6},{8,9},{9,8},{10,11... | collective-permute-start | bytes 196616 | tf_op jit(solution)/shard_map/ppermute | solution.py:727
  41.9 1.2 %collective-permute-start.22 = (bf16[1,128,128]{2,1,0:T(8,128)(2,1)S(1)}, bf16[1,128,128]{2,1,0:T(8,128)(2,1)S(1)}, u32[]{:S(2)}, u32[]{:S(2)}) collective-permute-start(bf16[1,128,128]{2,1,0:T(8,128)(2,1)S(1)} %collective-permute-done.16.refs_12_), channel_id=1, source_target_pairs={{0,1},{1,0},{2,3},{3,2},{4,5},{5,4},{6,7},{7,6},{8,9},{9,8},{10,11... | collective-permute-start | bytes 98312 | tf_op jit(solution)/shard_map/ppermute | solution.py:727
